TPU v7x, 32 devices: a whole 2x2x4 slice. The times are simulated.
32 devices in a mesh: groups: 2 (over x), req: 4 (over y, core), head: 4 (over z).
Axes of the slice: x: 2, y: 2, z: 4, core: 2. Of those that a mesh axis runs over, the one named last changes fastest.
Arguments:
- stretch_query: bfloat16 [2048, 12288], P(('groups', 'req'), 'head'), parts along dimension 0, may hold values from -48 to 48
- stretch_latent: bfloat16 [2048, 576], P(('groups', 'req')), parts along dimension 0, may hold values from -6 to 6
- cache_pool: bfloat16 [512, 36864], P(('groups', 'req'), 'head'), parts along dimension 0, may hold values from -6 to 6
- hit_slot: int32 [8, 16], P('groups'), parts along dimension 0, may hold values from 0 to 63
- hit_owner: int32 [8, 16], P('groups'), parts along dimension 0, may hold values from 0 to 3, as said below
- prefix_len: int32 [8], P('groups'), parts along dimension 0, may hold values from 768 to 1024, as said below
- head_mask: int32 [64], P('head'), may hold values 0 or 1
- up_key: bfloat16 [512, 8192], P(None, 'head'), may hold values from -0.25 to 0.25
- up_value: bfloat16 [512, 8192], P(None, 'head'), may hold values from -0.25 to 0.25
- out_weight: bfloat16 [5120, 8192], P('req', 'head'), may hold values from -0.5 to 0.5
Outputs:
- projected: bfloat16 [2048, 5120], P(('groups', 'req'), 'head'), parts along dimension 0
There are 2 independent parts, one for each index of `groups`. A program takes and returns all parts, laid end to end along the dimension named above; an argument that names none is the same for every part. Nothing has to cross between parts.
Inputs may be any that keep to these rules, and one draw needn't show every extreme that they name: `hit_owner`: within one request's list no owner appears more than 6 times; in every request's list some owner appears exactly 6 times. `prefix_len`: multiples of 64; in every draw one request has 1024 and another the least.
All inputs are finite; a program needn't handle non-finite values. No bound on the sum of `head_mask` on one device may be relied on, other than what follows from the above.
Results may differ from a plain program's by a relative error of at most 0.0072.
Values may be sent and summed in bfloat16 or wider, within the bound.
No kernel may reach another device: no remote copies, remote signals or barrier semaphores. Data moves between devices by JAX's collectives and lax.ppermute only.
A program may use at most 128 MiB of HBM per device.

v0:
```python
import math

import jax
import jax.numpy as jnp
from jax import lax
from jax.sharding import PartitionSpec as P

KVR = 512
NOPE = 128
VD = 128
BT = 64
STRETCH = 256
KEYBLK = 4
BLK = 16
LAT = 576
QKD = 192


def attend_block(carry_state, latent_block, allowed, query_nope, query_rope, up_key, up_value):
    running_max, row_total, weighted = carry_state
    local_heads = query_nope.shape[1]
    score_scale = 1.0 / math.sqrt(QKD)
    compressed = latent_block[:, :KVR]
    key_rope = latent_block[:, KVR:]
    key_nope = jnp.dot(compressed, up_key, preferred_element_type=jnp.float32).astype(jnp.bfloat16)
    key_nope = key_nope.reshape(-1, local_heads, NOPE)
    values = jnp.dot(compressed, up_value, preferred_element_type=jnp.float32).astype(jnp.bfloat16)
    values = values.reshape(-1, local_heads, VD)
    scores = jnp.einsum("qhn,khn->hqk", query_nope, key_nope, preferred_element_type=jnp.float32)
    scores = scores + jnp.einsum(
        "qhr,kr->hqk", query_rope, key_rope, preferred_element_type=jnp.float32
    )
    scores = jnp.where(allowed[None], scores * score_scale, -1e30)
    new_max = jnp.maximum(running_max, jnp.max(scores, axis=2))
    factor = jnp.exp(running_max - new_max)
    weights = jnp.exp(scores - new_max[:, :, None])
    row_total = row_total * factor + jnp.sum(weights, axis=2)
    update = jnp.einsum(
        "hqk,khv->qhv", weights.astype(jnp.bfloat16), values, preferred_element_type=jnp.float32
    )
    weighted = weighted * jnp.transpose(factor)[:, :, None] + update
    return (new_max, row_total, weighted)


def local(
    stretch_query,
    stretch_latent,
    cache_pool,
    hit_slot,
    hit_owner,
    prefix_len,
    head_mask,
    up_key,
    up_value,
    out_weight,
):
    req_count = lax.axis_size("req")
    head_count = lax.axis_size("head")
    capacity = max(2, (BLK + req_count - 1) // req_count * 3 // 2)
    own_req = lax.axis_index("req")
    slice_width = cache_pool.shape[1]
    block_index = jnp.arange(BLK)
    in_prefix = block_index[None, :] < (prefix_len // BT)[:, None]
    own_hits = in_prefix & (hit_owner == own_req)
    hit_rank = jnp.cumsum(own_hits.astype(jnp.int32), axis=1) - 1
    chosen_hit = own_hits[:, None, :] & (
        hit_rank[:, None, :] == jnp.arange(capacity)[None, :, None]
    )
    slot_pick = jnp.sum(jnp.where(chosen_hit, hit_slot[:, None, :], 0), axis=2)
    present = jnp.any(chosen_hit, axis=2)
    pool_rows = jnp.take(cache_pool, slot_pick.reshape(-1), axis=0).reshape(
        req_count, capacity, slice_width
    )
    pool_rows = jnp.where(present[:, :, None], pool_rows, jnp.zeros((), jnp.bfloat16))
    length = lax.dynamic_index_in_dim(prefix_len, own_req, 0, False)
    owners_row = lax.dynamic_index_in_dim(hit_owner, own_req, 0, False)
    in_row = block_index < length // BT
    owner_hot = (owners_row[:, None] == jnp.arange(req_count)[None, :]) & in_row[:, None]
    rank_table = jnp.cumsum(owner_hot.astype(jnp.int32), axis=0) - 1
    slot_rank = jnp.sum(jnp.where(owner_hot, rank_table, 0), axis=1)
    outgoing = jnp.broadcast_to(pool_rows[:, None], (req_count, head_count, capacity, slice_width))
    outgoing = outgoing.reshape(req_count * head_count * capacity, slice_width)
    incoming = lax.all_to_all(outgoing, ("req", "head"), split_axis=0, concat_axis=0, tiled=True)
    incoming = incoming.reshape(req_count, head_count, capacity, slice_width)
    fetched = incoming[owners_row, :, slot_rank]
    prefix = fetched.reshape(BLK * BT, LAT)
    local_heads = up_key.shape[1] // NOPE
    queries = stretch_query.reshape(STRETCH, local_heads, QKD)
    query_nope = queries[:, :, :NOPE]
    query_rope = queries[:, :, NOPE:]
    initial = (
        jnp.full((local_heads, STRETCH), -1e30, jnp.float32),
        jnp.zeros((local_heads, STRETCH), jnp.float32),
        jnp.zeros((STRETCH, local_heads, VD), jnp.float32),
    )
    span = KEYBLK * BT
    block_steps = (length + span - 1) // span

    def prefix_step(step_index, carry_state):
        start_row = step_index * span
        latent_block = lax.dynamic_slice_in_dim(prefix, start_row, span, 0)
        key_index = start_row + jnp.arange(span)
        allowed = jnp.broadcast_to((key_index < length)[None, :], (STRETCH, span))
        return attend_block(
            carry_state, latent_block, allowed, query_nope, query_rope, up_key, up_value
        )

    carry_state = lax.fori_loop(0, block_steps, prefix_step, initial)
    causal = jnp.arange(STRETCH)[None, :] <= jnp.arange(STRETCH)[:, None]
    running_max, row_total, weighted = attend_block(
        carry_state, stretch_latent, causal, query_nope, query_rope, up_key, up_value
    )
    attended = (weighted / jnp.transpose(row_total)[:, :, None]).astype(jnp.bfloat16)
    attended = (attended * head_mask.astype(jnp.bfloat16)[None, :, None]).reshape(
        STRETCH, local_heads * VD
    )
    partial_out = lax.dot_general(
        attended,
        lax.all_gather(out_weight, "req", axis=0, tiled=True),
        (((1,), (1,)), ((), ())),
        preferred_element_type=jnp.float32,
    )
    return lax.psum_scatter(partial_out, "head", scatter_dimension=1, tiled=True).astype(
        jnp.bfloat16
    )


def solution(mesh):
    placed = (
        P(("groups", "req"), "head"),
        P(("groups", "req"), None),
        P(("groups", "req"), "head"),
        P("groups", None),
        P("groups", None),
        P("groups"),
        P("head"),
        P(None, "head"),
        P(None, "head"),
        P("req", "head"),
    )
    return jax.shard_map(
        local, mesh=mesh, in_specs=placed, out_specs=P(("groups", "req"), "head"), check_vma=False
    )
```

profile of v0, /device:TPU:0, one launch (start us, length us, event | category | flops | bytes accessed | tf_op | source)
XLA Modules:
  0.0 290.6 jit_solution(4744160267127254096)
XLA Ops:
  11.2 7.4 %all-to-all-start = ((bf16[16,6,9216]{2,1,0:T(8,128)(2,1)}), bf16[16,6,9216]{2,1,0:T(8,128)(2,1)}, u32[]{:S(2)}, u32[]{:S(2)}) async-start(bf16[16,6,9216]{2,1,0:T(8,128)(2,1)} %bitcast.8), calls=%async_computation | async-start | bytes 4718592 | tf_op jit(solution)/shard_map/all_to_all | solution.py:83
  32.5 2.8 fusion.27
  36.0 3.7 %fusion.59 = (f32[16,256]{1,0:T(8,128)S(1)}, f32[16,256,256]{1,2,0:T(8,128)}) fusion(bf16[256,16,192]{0,2,1:T(8,128)(2,1)S(1)} %bitcast.109, bf16[256,576]{0,1:T(8,128)(2,1)} %param.13, f32[16,256,256]{2,1,0:T(8,128)S(1)} %fusion.33, pred[256,256]{0,1:T(8,128)(4,1)S(1)} %iota_compare_fusion), kind=kOutput, calls=%fused_computation.88 | convolution fusion | flops 138407936 | bytes 9027584 | tf_op jit(solution)/shard_map/qhr,kr->hqk/dot_general | solution.py:30
  39.7 34.2 %all-to-all-done = bf16[16,6,9216]{2,1,0:T(8,128)(2,1)} async-done(((bf16[16,6,9216]{2,1,0:T(8,128)(2,1)}), bf16[16,6,9216]{2,1,0:T(8,128)(2,1)}, u32[]{:S(2)}, u32[]{:S(2)}) %all-to-all-start) | async-done | bytes 1769504 | tf_op jit(solution)/shard_map/all_to_all | solution.py:83
  73.9 4.2 %copy.57 = bf16[4,4,6,9216]{3,1,2,0:T(4,128)(2,1)} copy(bf16[4,4,6,9216]{3,2,1,0:T(8,128)(2,1)} %bitcast.9) | data formatting | bytes 3538944 | tf_op jit(solution)/shard_map/reshape | solution.py:84
  78.1 3.0 %gather_fusion.1 = bf16[16,4,9216]{2,1,0:T(4,128)(2,1)S(1)} fusion(bf16[4,4,6,9216]{3,1,2,0:T(4,128)(2,1)} %copy.57, s32[16]{0:T(128)S(1)} %fusion.52), kind=kCustom, calls=%fused_computation.1 | custom fusion | bytes 2359424 | tf_op jit(solution)/shard_map/gather | solution.py:85
  87.2 83.0 %while.14 = (s32[]{:T(128)}, f32[16,256]{1,0:T(8,128)S(1)}, f32[16,256]{1,0:T(8,128)S(1)}, f32[256,16,128]{0,2,1:T(8,128)}, s32[]{:T(128)}, /*index=5*/s32[]{:T(...) while((s32[]{:T(128)}, f32[16,256]{1,0:T(8,128)S(1)}, ...), condition=%wide.region_8.9_spmd, body=%wide.region_5.8_spmd.sunk | while | flops 1755329024 | bytes 69501792 | solution.py:108
  89.8 2.7 fusion.95
  93.0 5.1 %fusion.96 = (f32[16,256]{1,0:T(8,128)S(1)}, f32[16,256,256]{1,2,0:T(8,128)}) fusion(bf16[256,16,64]{0,2,1:T(8,128)(2,1)S(1)} %copy-done.7, bf16[1024,576]{0,1:T(8,128)(2,1)} %get-tuple-element.269, s32[]{:T(128)S(6)} %select_n.137, s32[]{:T(128)S(6)} %add.155, f32[16,256,256]{2,1,0:T(8,128)} %fusion.95, pred[256]{0:T(512)(128)(4,1)S(1)} %add_compare_fusion.2), kind=kOutput, calls=%fused_computation.87.clone.1 | convolution fusion | flops 138407936 | bytes 8962312 | tf_op jit(solution)/shard_map/while/body/qhr,kr->hqk/dot_general | solution.py:30
  101.1 5.3 %bitcast_add_fusion.5 = f32[256,16,128]{0,2,1:T(8,128)} fusion(f32[256,16,128]{0,2,1:T(8,128)} %get-tuple-element.250, bf16[256,16,128]{0,2,1:T(8,128)(2,1)S(1)} %bitcast.105, f32[16,256,256]{1,2,0:T(8,128)} %get-tuple-element.229, f32[16,256]{1,0:T(8,128)S(1)} %get-tuple-element.264, f32[256,16]{0,1:T(8,128)S(1)} %get-tuple-element.230), kind=kOutput, calls=%fused_computation.11.clone.1 | convolution fusion | flops 271581184 | bytes 9469952 | tf_op jit(solution)/shard_map/while/body/hqk,khv->qhv/dot_general | solution.py:38
  110.5 2.7 fusion.95
  113.8 5.1 %fusion.96 = (f32[16,256]{1,0:T(8,128)S(1)}, f32[16,256,256]{1,2,0:T(8,128)}) fusion(bf16[256,16,64]{0,2,1:T(8,128)(2,1)S(1)} %copy-done.7, bf16[1024,576]{0,1:T(8,128)(2,1)} %get-tuple-element.269, s32[]{:T(128)S(6)} %select_n.137, s32[]{:T(128)S(6)} %add.155, f32[16,256,256]{2,1,0:T(8,128)} %fusion.95, pred[256]{0:T(512)(128)(4,1)S(1)} %add_compare_fusion.2), kind=kOutput, calls=%fused_computation.87.clone.1 | convolution fusion | flops 138407936 | bytes 8962312 | tf_op jit(solution)/shard_map/while/body/qhr,kr->hqk/dot_general | solution.py:30
  121.8 5.3 %bitcast_add_fusion.5 = f32[256,16,128]{0,2,1:T(8,128)} fusion(f32[256,16,128]{0,2,1:T(8,128)} %get-tuple-element.250, bf16[256,16,128]{0,2,1:T(8,128)(2,1)S(1)} %bitcast.105, f32[16,256,256]{1,2,0:T(8,128)} %get-tuple-element.229, f32[16,256]{1,0:T(8,128)S(1)} %get-tuple-element.264, f32[256,16]{0,1:T(8,128)S(1)} %get-tuple-element.230), kind=kOutput, calls=%fused_computation.11.clone.1 | convolution fusion | flops 271581184 | bytes 9469952 | tf_op jit(solution)/shard_map/while/body/hqk,khv->qhv/dot_general | solution.py:38
  131.2 2.7 fusion.95
  134.5 5.1 %fusion.96 = (f32[16,256]{1,0:T(8,128)S(1)}, f32[16,256,256]{1,2,0:T(8,128)}) fusion(bf16[256,16,64]{0,2,1:T(8,128)(2,1)S(1)} %copy-done.7, bf16[1024,576]{0,1:T(8,128)(2,1)} %get-tuple-element.269, s32[]{:T(128)S(6)} %select_n.137, s32[]{:T(128)S(6)} %add.155, f32[16,256,256]{2,1,0:T(8,128)} %fusion.95, pred[256]{0:T(512)(128)(4,1)S(1)} %add_compare_fusion.2), kind=kOutput, calls=%fused_computation.87.clone.1 | convolution fusion | flops 138407936 | bytes 8962312 | tf_op jit(solution)/shard_map/while/body/qhr,kr->hqk/dot_general | solution.py:30
  142.5 5.3 %bitcast_add_fusion.5 = f32[256,16,128]{0,2,1:T(8,128)} fusion(f32[256,16,128]{0,2,1:T(8,128)} %get-tuple-element.250, bf16[256,16,128]{0,2,1:T(8,128)(2,1)S(1)} %bitcast.105, f32[16,256,256]{1,2,0:T(8,128)} %get-tuple-element.229, f32[16,256]{1,0:T(8,128)S(1)} %get-tuple-element.264, f32[256,16]{0,1:T(8,128)S(1)} %get-tuple-element.230), kind=kOutput, calls=%fused_computation.11.clone.1 | convolution fusion | flops 271581184 | bytes 9469952 | tf_op jit(solution)/shard_map/while/body/hqk,khv->qhv/dot_general | solution.py:38
  151.9 2.7 fusion.95
  155.2 5.1 %fusion.96 = (f32[16,256]{1,0:T(8,128)S(1)}, f32[16,256,256]{1,2,0:T(8,128)}) fusion(bf16[256,16,64]{0,2,1:T(8,128)(2,1)S(1)} %copy-done.7, bf16[1024,576]{0,1:T(8,128)(2,1)} %get-tuple-element.269, s32[]{:T(128)S(6)} %select_n.137, s32[]{:T(128)S(6)} %add.155, f32[16,256,256]{2,1,0:T(8,128)} %fusion.95, pred[256]{0:T(512)(128)(4,1)S(1)} %add_compare_fusion.2), kind=kOutput, calls=%fused_computation.87.clone.1 | convolution fusion | flops 138407936 | bytes 8962312 | tf_op jit(solution)/shard_map/while/body/qhr,kr->hqk/dot_general | solution.py:30
  160.3 2.5 convolution_convert_fusion.5
  163.4 5.3 %bitcast_add_fusion.5 = f32[256,16,128]{0,2,1:T(8,128)} fusion(f32[256,16,128]{0,2,1:T(8,128)} %get-tuple-element.250, bf16[256,16,128]{0,2,1:T(8,128)(2,1)S(1)} %bitcast.105, f32[16,256,256]{1,2,0:T(8,128)} %get-tuple-element.229, f32[16,256]{1,0:T(8,128)S(1)} %get-tuple-element.264, f32[256,16]{0,1:T(8,128)S(1)} %get-tuple-element.230), kind=kOutput, calls=%fused_computation.11.clone.1 | convolution fusion | flops 271581184 | bytes 9469952 | tf_op jit(solution)/shard_map/while/body/hqk,khv->qhv/dot_general | solution.py:38
  170.3 2.9 %fusion.20 = f32[16,256]{1,0:T(8,128)S(1)} fusion(f32[16,256,256]{1,2,0:T(8,128)} %get-tuple-element.154, f32[16,256]{1,0:T(8,128)S(1)} %get-tuple-element.148), kind=kLoop, calls=%fused_computation.30 | loop fusion | flops 2093056 | bytes 4227072 | tf_op jit(solution)/shard_map/reduce_sum | solution.py:37
  173.4 3.2 %fusion.30 = bf16[256,16,128]{0,2,1:T(8,128)(2,1)S(1)} fusion(bf16[256,16,128]{0,2,1:T(8,128)(2,1)S(1)} %bitcast.110, f32[16,256,256]{1,2,0:T(8,128)} %get-tuple-element.154, f32[16,256]{1,0:T(8,128)S(1)} %get-tuple-element.148, f32[256,16,128]{0,2,1:T(8,128)S(1)} %copy-done.5, f32[256,16]{0,1:T(8,128)S(1)} %add_bitcast_fusion, ...), kind=kOutput, calls=%fused_computation.40 | convolution fusion | flops 273154048 | bytes 8437792 | tf_op jit(solution)/shard_map/hqk,khv->qhv/dot_general | solution.py:38
  176.6 12.2 %fusion.60 = f32[256,5120]{1,0:T(8,128)} fusion(bf16[256,2048]{0,1:T(8,128)(2,1)S(1)} %bitcast.111, bf16[5120,2048]{1,0:T(8,128)(2,1)} %all-gather.2.cloned.1.call-done), kind=kOutput, calls=%fused_computation.89 | convolution fusion | flops 5368709120 | bytes 27262976 | tf_op jit(solution)/shard_map/dot_general | solution.py:117
  188.9 92.6 %reduce-scatter.2.cloned.1.call-done = f32[256,1280]{1,0:T(8,128)} async-done(((f32[256,5120]{1,0:T(8,128)}), f32[256,1280]{1,0:T(8,128)}) %reduce-scatter.2.cloned.1.call-update) | async-done | bytes 1310736 | tf_op jit(solution)/shard_map/reduce_scatter | solution.py:123
  (131 shorter events, 52.6 us)
Async XLA Ops:
  6.5 170.0 %all-gather.2.cloned.1.call-start = ((), (), s32[]{:S(2)}) async-start(), calls=%async_computation.2 | async-start | bytes 26214400 | tf_op jit(solution)/shard_map/all_gather | solution.py:119
  11.2 62.6 %all-to-all-start = ((bf16[16,6,9216]{2,1,0:T(8,128)(2,1)}), bf16[16,6,9216]{2,1,0:T(8,128)(2,1)}, u32[]{:S(2)}, u32[]{:S(2)}) async-start(bf16[16,6,9216]{2,1,0:T(8,128)(2,1)} %bitcast.8), calls=%async_computation | async-start | bytes 4718592 | tf_op jit(solution)/shard_map/all_to_all | solution.py:83
  18.7 262.8 %reduce-scatter.2.cloned.1.call-start = ((), (), s32[]{:S(2)}) async-start(), calls=%async_computation.3 | async-start | bytes 6553600 | tf_op jit(solution)/shard_map/reduce_scatter | solution.py:123
  25.0 4.2 %copy-start.3 = (bf16[512,2048]{1,0:T(8,128)(2,1)S(1)}, bf16[512,2048]{1,0:T(8,128)(2,1)}, u32[]{:S(2)}) copy-start(bf16[512,2048]{1,0:T(8,128)(2,1)} %param.20) | copy-start | bytes 6291460
  29.2 3.0 %copy-start.14 = (s32[16]{0:T(128)S(1)}, s32[16]{0:T(128)}, u32[]{:S(2)}) copy-start(s32[16]{0:T(128)} %param.18) | copy-start | bytes 196
  32.2 3.0 %copy-start.9 = (bf16[256,3072]{0,1:T(8,128)(2,1)S(1)}, bf16[256,3072]{0,1:T(8,128)(2,1)}, u32[]{:S(2)}) copy-start(bf16[256,3072]{0,1:T(8,128)(2,1)} %copy-done.8) | copy-start | bytes 4718596
  87.2 2.5 copy-start.6
  89.7 3.3 %copy-start.7 = (bf16[256,16,64]{0,2,1:T(8,128)(2,1)S(1)}, bf16[256,16,64]{0,2,1:T(8,128)(2,1)}, u32[]{:S(2)}) copy-start(bf16[256,16,64]{0,2,1:T(8,128)(2,1)} %get-tuple-element.272) | copy-start | bytes 1572868 | tf_op jit(solution)/shard_map/while
  101.1 5.3 %copy-start.2 = (f32[16,256,256]{1,2,0:T(8,128)S(1)}, f32[16,256,256]{1,2,0:T(8,128)}, u32[]{:S(2)}) copy-start(f32[16,256,256]{1,2,0:T(8,128)} %get-tuple-element.229) | copy-start | bytes 12582916 | tf_op jit(solution)/shard_map/while
  106.4 1.6 copy-start.4
  108.0 2.5 copy-start.6
  110.5 3.3 %copy-start.7 = (bf16[256,16,64]{0,2,1:T(8,128)(2,1)S(1)}, bf16[256,16,64]{0,2,1:T(8,128)(2,1)}, u32[]{:S(2)}) copy-start(bf16[256,16,64]{0,2,1:T(8,128)(2,1)} %get-tuple-element.272) | copy-start | bytes 1572868 | tf_op jit(solution)/shard_map/while
  121.8 5.3 %copy-start.2 = (f32[16,256,256]{1,2,0:T(8,128)S(1)}, f32[16,256,256]{1,2,0:T(8,128)}, u32[]{:S(2)}) copy-start(f32[16,256,256]{1,2,0:T(8,128)} %get-tuple-element.229) | copy-start | bytes 12582916 | tf_op jit(solution)/shard_map/while
  127.1 1.6 copy-start.4
  128.7 2.5 copy-start.6
  131.2 3.3 %copy-start.7 = (bf16[256,16,64]{0,2,1:T(8,128)(2,1)S(1)}, bf16[256,16,64]{0,2,1:T(8,128)(2,1)}, u32[]{:S(2)}) copy-start(bf16[256,16,64]{0,2,1:T(8,128)(2,1)} %get-tuple-element.272) | copy-start | bytes 1572868 | tf_op jit(solution)/shard_map/while
  142.5 5.3 %copy-start.2 = (f32[16,256,256]{1,2,0:T(8,128)S(1)}, f32[16,256,256]{1,2,0:T(8,128)}, u32[]{:S(2)}) copy-start(f32[16,256,256]{1,2,0:T(8,128)} %get-tuple-element.229) | copy-start | bytes 12582916 | tf_op jit(solution)/shard_map/while
  147.8 1.6 copy-start.4
  149.4 2.5 copy-start.6
  151.9 3.3 %copy-start.7 = (bf16[256,16,64]{0,2,1:T(8,128)(2,1)S(1)}, bf16[256,16,64]{0,2,1:T(8,128)(2,1)}, u32[]{:S(2)}) copy-start(bf16[256,16,64]{0,2,1:T(8,128)(2,1)} %get-tuple-element.272) | copy-start | bytes 1572868 | tf_op jit(solution)/shard_map/while
  163.3 5.3 %copy-start.2 = (f32[16,256,256]{1,2,0:T(8,128)S(1)}, f32[16,256,256]{1,2,0:T(8,128)}, u32[]{:S(2)}) copy-start(f32[16,256,256]{1,2,0:T(8,128)} %get-tuple-element.229) | copy-start | bytes 12582916 | tf_op jit(solution)/shard_map/while
  170.2 3.0 %copy-start.5 = (f32[256,16,128]{0,2,1:T(8,128)S(1)}, f32[256,16,128]{0,2,1:T(8,128)}, u32[]{:S(2)}) copy-start(f32[256,16,128]{0,2,1:T(8,128)} %get-tuple-element.284) | copy-start | bytes 6291460
  170.2 3.1 %copy-start.10 = (bf16[256,2048]{0,1:T(8,128)(2,1)S(1)}, bf16[256,2048]{0,1:T(8,128)(2,1)}, u32[]{:S(2)}) copy-start(bf16[256,2048]{0,1:T(8,128)(2,1)} %copy.69) | copy-start | bytes 3145732
  188.9 94.9 %copy-start.1 = (bf16[64,9216]{1,0:T(8,128)(2,1)S(1)}, bf16[64,9216]{1,0:T(8,128)(2,1)}, u32[]{:S(2)}) copy-start(bf16[64,9216]{1,0:T(8,128)(2,1)} %param.14) | copy-start | bytes 3538948
  (6 other events, 6.8 us)
Sparse Core Ops, SparseCore 0:
  8.9 152.7 all-gather.1
  189.0 92.4 reduce-scatter.1
where the time goes:
time: 291 us
  waiting for transfers between devices  128 us (44%)
  matrix products  96.2 us (33%)
  local copies, waits for them, and re-layouts  31.3 us (11%)
  between operations  16.6 us (6%)
  other arithmetic  11 us (4%)
  starting transfers between devices  7.5 us (3%)
    reduce_scatter x1, waiting for transfers between devices, local(): lax.psum_scatter(partial_out, 'head', scatter_dimension=1, tiled=True)  92.6 us
    all_to_all x1, waiting for transfers between devices, local(): lax.all_to_all(outgoing, ('req', 'head'), split_axis=0, concat_axis=0, ti...  34.2 us
    dot_general x5, matrix products, attend_block(): jnp.einsum('hqk,khv->qhv', weights.astype(jnp.bfloat16), values, preferre...  24.3 us
    dot_general x5, matrix products, attend_block(): jnp.einsum('qhr,kr->hqk', query_rope, key_rope, preferred_element_type=jn...  24 us
    dot_general x5, matrix products, attend_block(): jnp.dot(compressed, up_key, preferred_element_type=jnp.float32)  12.7 us
    dot_general x1, matrix products, local(): lax.dot_general(attended, lax.all_gather(out_weight, 'req', axis=0, tiled...  12.2 us
    dot_general x5, matrix products, attend_block(): jnp.dot(compressed, up_value, preferred_element_type=jnp.float32)  11.5 us
    dot_general x5, matrix products, attend_block(): jnp.einsum('qhn,khn->hqk', query_nope, key_nope, preferred_element_type=j...  11.4 us
  transfers between devices with their start and end apart: 3, of which 2 were waited for; matrix products, arithmetic and copies ran while one was open for 41% of the time, Pallas kernels for 0%

commit v1 on v0

v1 whole, which is shorter than its diff:
```python
import math

import jax
import jax.numpy as jnp
from jax import lax
from jax.experimental import pallas as pl
from jax.experimental.pallas import tpu as pltpu
from jax.sharding import PartitionSpec as P

KVR = 512
NOPE = 128
VD = 128
BT = 64
STRETCH = 256
BLK = 16
LAT = 576
QKD = 192
ROPE = LAT - KVR
MASKED = -1e30
BF16 = jnp.bfloat16
F32 = jnp.float32


def attention_kernel(
    blocks_ref, mask_ref, query_ref, stretch_ref, *refs, piece_count
):
    pieces = refs[:piece_count]
    key_ref, value_ref, out_ref, latent, rope = refs[piece_count:]
    step = pl.program_id(0)
    piece_tokens = pieces[0].shape[1] // LAT
    prefix = piece_count * piece_tokens * BLK
    total = prefix + STRETCH

    @pl.when(step == 0)
    def _():
        lane = lax.broadcasted_iota(jnp.int32, (BLK, ROPE), 1)
        row = lax.broadcasted_iota(jnp.int32, (BLK, ROPE), 0)
        hidden = (lane == 0) & (row >= blocks_ref[0])
        extra = jnp.where(hidden, MASKED, 0.0).astype(BF16)
        for index, piece in enumerate(pieces):
            for token in range(piece_tokens):
                start = (index * piece_tokens + token) * BLK
                base = LAT * token
                latent[start : start + BLK, :] = piece[:, base : base + KVR]
                rope[start : start + BLK, :] = jnp.concatenate(
                    [piece[:, base + KVR : base + LAT], extra], axis=1
                )
        latent[prefix:total, :] = stretch_ref[:, :KVR]
        rope[prefix:total, :] = jnp.concatenate(
            [stretch_ref[:, KVR:], jnp.zeros((STRETCH, ROPE), BF16)], axis=1
        )

    compressed = latent[...]
    keys = jnp.dot(compressed, key_ref[...], preferred_element_type=F32).astype(BF16)
    values = jnp.dot(compressed, value_ref[...], preferred_element_type=F32).astype(BF16)
    key_rope = rope[...]
    ones = jnp.ones((total, VD), BF16)
    lane = lax.broadcasted_iota(jnp.int32, (STRETCH, ROPE), 1)
    query_extra = jnp.where(lane == 0, 1.0, 0.0).astype(BF16)
    scale = 1.0 / (math.sqrt(QKD) * math.log(2.0))
    causal = lax.broadcasted_iota(jnp.int32, (STRETCH, STRETCH), 1) <= lax.broadcasted_iota(
        jnp.int32, (STRETCH, STRETCH), 0
    )
    for part in range(2):
        query = jnp.concatenate(
            [query_ref[:, part * QKD : (part + 1) * QKD], query_extra], axis=1
        )
        key = jnp.concatenate([keys[:, part * NOPE : (part + 1) * NOPE], key_rope], axis=1)
        scores = lax.dot_general(
            query, key, (((1,), (1,)), ((), ())), preferred_element_type=F32
        )
        before = scores[:, :prefix]
        own = jnp.where(causal, scores[:, prefix:], MASKED)
        largest = jnp.maximum(
            jnp.max(before, axis=1, keepdims=True), jnp.max(own, axis=1, keepdims=True)
        )
        weights = jnp.concatenate(
            [
                jnp.exp2((before - largest) * scale).astype(BF16),
                jnp.exp2((own - largest) * scale).astype(BF16),
            ],
            axis=1,
        )
        value = jnp.concatenate([values[:, part * VD : (part + 1) * VD], ones], axis=1)
        summed = jnp.dot(weights, value, preferred_element_type=F32)
        attended = (summed[:, :VD] / summed[:, VD:]).astype(BF16)
        kept = mask_ref[2 * step + part].astype(F32).astype(BF16)
        out_ref[:, part * VD : (part + 1) * VD] = attended * kept


def attention(blocks, head_mask, stretch_query, stretch_latent, pieces, up_key, up_value):
    heads = up_key.shape[1] // NOPE
    piece_tokens = pieces[0].shape[1] // LAT
    total = len(pieces) * piece_tokens * BLK + STRETCH

    def whole(array):
        return pl.BlockSpec(array.shape, lambda step: (0, 0))

    def columns(rows, width):
        return pl.BlockSpec((rows, width), lambda step: (0, step))

    smem = pl.BlockSpec(memory_space=pltpu.SMEM)
    return pl.pallas_call(
        lambda *refs: attention_kernel(*refs, piece_count=len(pieces)),
        grid=(heads // 2,),
        in_specs=[smem, smem, columns(STRETCH, 2 * QKD), whole(stretch_latent)]
        + [whole(piece) for piece in pieces]
        + [columns(KVR, 2 * NOPE), columns(KVR, 2 * VD)],
        out_specs=columns(STRETCH, 2 * VD),
        out_shape=jax.ShapeDtypeStruct((STRETCH, heads * VD), BF16),
        scratch_shapes=[
            pltpu.VMEM((total, KVR), BF16),
            pltpu.VMEM((total, 2 * ROPE), BF16),
        ],
        compiler_params=pltpu.CompilerParams(vmem_limit_bytes=48 * 1024 * 1024),
        cost_estimate=pl.CostEstimate(
            flops=2 * heads * total * VD * (2 * KVR + 4 * STRETCH),
            bytes_accessed=8 * 1024 * 1024,
            transcendentals=heads * total * STRETCH,
        ),
        name="attention",
    )(blocks, head_mask, stretch_query, stretch_latent, *pieces, up_key, up_value)


def hit_tables(hit_slot, hit_owner, prefix_len, own_req, capacity, sources, targets):
    block_index = jnp.arange(BLK)
    in_prefix = block_index[None, :] < (prefix_len // BT)[:, None]
    own_hits = in_prefix & (hit_owner == own_req)
    rank = jnp.cumsum(own_hits.astype(jnp.int32), axis=1) - 1
    chosen = own_hits[:, None, :] & (rank[:, None, :] == jnp.arange(capacity)[None, :, None])
    slots = jnp.sum(jnp.where(chosen, hit_slot[:, None, :], 0), axis=2)
    slots = jnp.take(slots, targets, axis=0)
    length = lax.dynamic_index_in_dim(prefix_len, own_req, 0, False)
    owners = lax.dynamic_index_in_dim(hit_owner, own_req, 0, False)
    from_source = (owners[:, None] == sources[None, :]) & (block_index < length // BT)[:, None]
    ranks = jnp.cumsum(from_source.astype(jnp.int32), axis=0) - 1
    picks = from_source[:, :, None] & (ranks[:, :, None] == jnp.arange(capacity)[None, None, :])
    return slots, picks.reshape(BLK, -1).astype(BF16), (length // BT).reshape(1)


def project_kernel(route_ref, attended_ref, *refs):
    weights, (mine_ref, other_ref, send_ref) = refs[:-3], refs[-3:]
    attended = attended_ref[...]
    own_half = route_ref[1]
    for unit in range(4):
        slot = unit ^ route_ref[0]
        if unit < 2:
            total = lax.dot_general(
                attended, weights[unit][...], (((1,), (1,)), ((), ())), preferred_element_type=F32
            )
        else:
            near, far = weights[2 * unit - 2], weights[2 * unit - 1]
            first, second = (
                lax.dot_general(
                    attended, piece[...], (((1,), (1,)), ((), ())), preferred_element_type=F32
                )
                for piece in (near, far)
            )
            swapped = own_half == 1
            total = jnp.concatenate(
                [jnp.where(swapped, second, first), jnp.where(swapped, first, second)], axis=1
            )

        @pl.when(slot == 0)
        def _():
            mine_ref[...] = total

        @pl.when(slot == 2)
        def _():
            other_ref[...] = total

        @pl.when(slot == 1)
        def _():
            send_ref[0] = total.astype(BF16)

        @pl.when(slot == 3)
        def _():
            send_ref[1] = total.astype(BF16)


def project(route, attended, own, beside, pieces, chunk, rows):
    width = attended.shape[1]
    half = rows // 2
    part = pl.BlockSpec((rows, width), lambda step: (chunk, 0))
    piece = pl.BlockSpec((half, width), lambda step: (0, 0))
    tokens = attended.shape[0]
    return pl.pallas_call(
        project_kernel,
        grid=(1,),
        in_specs=[
            pl.BlockSpec(memory_space=pltpu.SMEM),
            pl.BlockSpec(attended.shape, lambda step: (0, 0)),
            part,
            part,
            piece,
            piece,
            piece,
            piece,
        ],
        out_specs=[
            pl.BlockSpec((tokens, rows), lambda step: (0, 0)),
            pl.BlockSpec((tokens, rows), lambda step: (0, 0)),
            pl.BlockSpec((2, tokens, rows), lambda step: (0, 0, 0)),
        ],
        out_shape=[
            jax.ShapeDtypeStruct((tokens, rows), F32),
            jax.ShapeDtypeStruct((tokens, rows), F32),
            jax.ShapeDtypeStruct((2, tokens, rows), BF16),
        ],
        compiler_params=pltpu.CompilerParams(vmem_limit_bytes=48 * 1024 * 1024),
        cost_estimate=pl.CostEstimate(
            flops=8 * tokens * rows * width, bytes_accessed=8 * rows * width, transcendentals=0
        ),
        name="project",
    )(route, attended, own, beside, *pieces)


def flip(size, bit):
    return [(index, index ^ bit) for index in range(size)]


def local(
    stretch_query,
    stretch_latent,
    cache_pool,
    hit_slot,
    hit_owner,
    prefix_len,
    head_mask,
    up_key,
    up_value,
    out_weight,
):
    groups = lax.axis_size("groups")
    req_count = lax.axis_size("req")
    head_count = lax.axis_size("head")
    capacity = max(2, (BLK + req_count - 1) // req_count * 3 // 2)
    own_req = lax.axis_index("req")
    own_head = lax.axis_index("head")
    paired = groups == 2 and req_count == 4 and head_count == 4
    order = jnp.arange(req_count)
    partners = order ^ own_req if paired else order
    slots, picks, blocks = hit_tables(
        hit_slot, hit_owner, prefix_len, own_req, capacity, partners, partners
    )
    if not paired:
        outgoing = jnp.take(cache_pool, slots.reshape(-1), axis=0)
        incoming = lax.all_to_all(outgoing, "req", split_axis=0, concat_axis=0, tiled=True)
        prefix = jnp.dot(picks, incoming, preferred_element_type=F32).astype(BF16)
        gathered = lax.all_gather(prefix, "head", axis=0)
        pieces = [gathered[index] for index in range(head_count)]
        attended = attention(
            blocks, head_mask, stretch_query, stretch_latent, pieces, up_key, up_value
        )
        partial_out = lax.dot_general(
            attended,
            lax.all_gather(out_weight, "req", axis=0, tiled=True),
            (((1,), (1,)), ((), ())),
            preferred_element_type=F32,
        )
        return lax.psum_scatter(partial_out, "head", scatter_dimension=1, tiled=True).astype(BF16)

    own_group = lax.axis_index("groups")
    outgoing = [jnp.take(cache_pool, slots[index], axis=0) for index in range(req_count)]
    incoming = [outgoing[0]] + [
        lax.ppermute(outgoing[bit], "req", flip(req_count, bit)) for bit in (1, 2, 3)
    ]
    prefix = jnp.dot(
        picks, jnp.concatenate(incoming, axis=0), preferred_element_type=F32
    ).astype(BF16)
    far = lax.ppermute(prefix, "head", flip(head_count, 2))
    near = lax.ppermute(prefix, "head", flip(head_count, 1))
    farther = lax.ppermute(far, "head", flip(head_count, 1))

    rows = 256
    chunks = out_weight.shape[0] // rows
    half = rows // 2
    beside = lax.ppermute(out_weight, "req", flip(req_count, 1))
    across = []
    for chunk in range(chunks):
        piece = lax.dynamic_slice_in_dim(
            out_weight, chunk * rows + own_group * half, half, 0
        )
        first = lax.ppermute(piece, "req", flip(req_count, 2))
        second = lax.ppermute(first, "groups", flip(groups, 1))
        across.append(
            (
                first,
                second,
                lax.ppermute(first, "req", flip(req_count, 1)),
                lax.ppermute(second, "req", flip(req_count, 1)),
            )
        )

    attended = attention(
        blocks,
        head_mask,
        stretch_query,
        stretch_latent,
        [prefix, near, far, farther],
        up_key,
        up_value,
    )
    route = jnp.stack([own_req ^ own_head, own_group]).astype(jnp.int32)
    outs = []
    for chunk in range(chunks):
        mine, other, send = project(
            route, attended, out_weight, beside, across[chunk], chunk, rows
        )
        received = lax.ppermute(send, "head", flip(head_count, 1))
        passed = lax.ppermute(
            (other + received[1].astype(F32)).astype(BF16), "head", flip(head_count, 2)
        )
        outs.append((mine + received[0].astype(F32) + passed.astype(F32)).astype(BF16))
    return jnp.concatenate(outs, axis=1)


def solution(mesh):
    placed = (
        P(("groups", "req"), "head"),
        P(("groups", "req"), None),
        P(("groups", "req"), "head"),
        P("groups", None),
        P("groups", None),
        P("groups"),
        P("head"),
        P(None, "head"),
        P(None, "head"),
        P("req", "head"),
    )
    return jax.shard_map(
        local, mesh=mesh, in_specs=placed, out_specs=P(("groups", "req"), "head"), check_vma=False
    )
```

time: 291 us -> 213 us (0.73)
  matrix products: 96.2 us -> 0.44 us
  Pallas kernels: 0 us -> 41.7 us
  starting transfers between devices: 7.5 us -> 31.4 us
  waiting for transfers between devices: 128 us -> 110 us
  between operations: 16.6 us -> 3.01 us
  local copies, waits for them, and re-layouts: 31.3 us -> 20.9 us
  other arithmetic: 11 us -> 4.26 us
    ppermute x0 -> x37, waiting for transfers between devices: none -> 110 us  [the longest x5 40.3 us: local(): first = lax.ppermute(piece, 'req', flip(req_count, 2))]
    dot_general x26 -> x1, matrix products: 96.2 us -> 0.44 us  [local(): jnp.dot(picks, jnp.concatenate(incoming, axis=0), preferred_element_type=...]
    reduce_scatter x1 -> x0, waiting for transfers between devices: 92.6 us -> none  [local(): lax.psum_scatter(partial_out, 'head', scatter_dimension=1, tiled=True)]
    pallas_call x0 -> x6, Pallas kernels: none -> 41.7 us  [the longest x5 23.5 us: project(): pl.pallas_call(project_kernel, grid=(1,), in_specs=[pl.BlockSpec(memory_s...]
    all_to_all x1 -> x0, waiting for transfers between devices: 34.2 us -> none  [local(): lax.all_to_all(outgoing, ('req', 'head'), split_axis=0, concat_axis=0, ti...]
    ppermute x0 -> x37, starting transfers between devices: none -> 31.4 us  [the longest x5 6.93 us: local(): first = lax.ppermute(piece, 'req', flip(req_count, 2))]
    reshape x8 -> x0, local copies, waits for them, and re-layouts: 9.77 us -> none  [the longest x1 4.23 us: local(): incoming = incoming.reshape(req_count, head_count, capacity, slice_width)]
    unnamed x25 -> x49, local copies, waits for them, and re-layouts: 4.89 us -> 14.3 us
  transfers between devices with their start and end apart: 3 -> 37, of which waited for: 2 -> 15; matrix products, arithmetic and copies ran while one was open for 41% -> 4% of each run, Pallas kernels for 0% -> 20%
where the time goes in v1:
time: 213 us; the launch traced here: 212 us
  waiting for transfers between devices  110 us (52%)
  Pallas kernels  41.7 us (20%)
  starting transfers between devices  31.4 us (15%)
  local copies, waits for them, and re-layouts  20.9 us (10%)
  other arithmetic  4.26 us (2%)
  between operations  3.01 us (1%)
    ppermute x5, waiting for transfers between devices, local(): first = lax.ppermute(piece, 'req', flip(req_count, 2))  40.3 us
    ppermute x5, waiting for transfers between devices, local(): second = lax.ppermute(first, 'groups', flip(groups, 1))  35.9 us
    pallas_call x5, Pallas kernels, project(): pl.pallas_call(project_kernel, grid=(1,), in_specs=[pl.BlockSpec(memory_s...  23.5 us
    pallas_call x1, Pallas kernels, attention(): pl.pallas_call(lambda *refs: attention_kernel(*refs, piece_count=len(piec...  18.2 us
    ppermute x5, waiting for transfers between devices, local(): received = lax.ppermute(send, 'head', flip(head_count, 1))  16.7 us
    unnamed x49, local copies, waits for them, and re-layouts  14.3 us
    ppermute x5, waiting for transfers between devices, local(): lax.ppermute((other + received[1].astype(F32)).astype(BF16), 'head', flip...  10.6 us
    ppermute x5, starting transfers between devices, local(): first = lax.ppermute(piece, 'req', flip(req_count, 2))  6.93 us
  transfers between devices with their start and end apart: 37, of which 15 were waited for; matrix products, arithmetic and copies ran while one was open for 4% of the time, Pallas kernels for 20%

profile of v1, /device:TPU:0, one launch (start us, length us, event | category | flops | bytes accessed | tf_op | source)
XLA Modules:
  0.0 212.2 jit_solution(8068904620088568963)
XLA Ops:
  4.1 2.5 %collective-permute-start.2 = (bf16[6,9216]{1,0:T(8,128)(2,1)S(1)}, bf16[6,9216]{1,0:T(8,128)(2,1)S(1)}, u32[]{:S(2)}, u32[]{:S(2)}) collective-permute-start(bf16[6,9216]{1,0:T(8,128)(2,1)S(1)} %broadcast_select_fusion), channel_id=1, source_target_pairs={{0,12},{4,8},{8,4},{12,0},{1,13},{5,9},{9,5},{13,1},{2,14},{6,10},... | collective-permute-start | bytes 331784 | tf_op jit(solution)/shard_map/ppermute | solution.py:266
  14.8 2.2 %collective-permute-start.3 = (bf16[16,9216]{1,0:T(8,128)(2,1)S(1)}, bf16[16,9216]{1,0:T(8,128)(2,1)S(1)}, u32[]{:S(2)}, u32[]{:S(2)}) collective-permute-start(bf16[16,9216]{1,0:T(8,128)(2,1)S(1)} %convolution_convert_fusion.refs_4_), channel_id=1, source_target_pairs={{0,1},{1,0},{2,3},{3,2},{4,5},{5,4},{6,7},{7,6},{8,9},{9,8},{10,11... | collective-permute-start | bytes 884744 | tf_op jit(solution)/shard_map/ppermute | solution.py:272
  17.0 2.6 %collective-permute-start.4 = (bf16[16,9216]{1,0:T(8,128)(2,1)S(1)}, bf16[16,9216]{1,0:T(8,128)(2,1)S(1)}, u32[]{:S(2)}, u32[]{:S(2)}) collective-permute-start(bf16[16,9216]{1,0:T(8,128)(2,1)S(1)} %convolution_convert_fusion.refs_4_), channel_id=1, source_target_pairs={{0,2},{1,3},{2,0},{3,1},{4,6},{5,7},{6,4},{7,5},{8,10},{9,11},{10,... | collective-permute-start | bytes 884744 | tf_op jit(solution)/shard_map/ppermute | solution.py:271
  23.6 6.9 %collective-permute-done.3.refs_5_ = bf16[16,9216]{1,0:T(8,128)(2,1)S(1)} collective-permute-done((bf16[16,9216]{1,0:T(8,128)(2,1)S(1)}, bf16[16,9216]{1,0:T(8,128)(2,1)S(1)}, u32[]{:S(2)}, u32[]{:S(2)}) %collective-permute-start.3) | collective-permute-done | bytes 294944 | tf_op jit(solution)/shard_map/ppermute | solution.py:272
  34.5 1.9 collective-permute-done.7.refs_2_
  37.9 9.7 %collective-permute-done.13.refs_2_ = bf16[128,2048]{1,0:T(8,128)(2,1)S(1)} collective-permute-done((bf16[128,2048]{1,0:T(8,128)(2,1)S(1)}, bf16[128,2048]{1,0:T(8,128)(2,1)S(1)}, u32[]{:S(2)}, u32[]{:S(2)}) %collective-permute-start.13) | collective-permute-done | bytes 524320 | tf_op jit(solution)/shard_map/ppermute | solution.py:284
  49.1 9.7 %collective-permute-done.19.refs_2_ = bf16[128,2048]{1,0:T(8,128)(2,1)S(1)} collective-permute-done((bf16[128,2048]{1,0:T(8,128)(2,1)S(1)}, bf16[128,2048]{1,0:T(8,128)(2,1)S(1)}, u32[]{:S(2)}, u32[]{:S(2)}) %collective-permute-start.19) | collective-permute-done | bytes 524320 | tf_op jit(solution)/shard_map/ppermute | solution.py:284
  59.7 10.4 %collective-permute-done.25.refs_2_ = bf16[128,2048]{1,0:T(8,128)(2,1)S(1)} collective-permute-done((bf16[128,2048]{1,0:T(8,128)(2,1)S(1)}, bf16[128,2048]{1,0:T(8,128)(2,1)S(1)}, u32[]{:S(2)}, u32[]{:S(2)}) %collective-permute-start.25) | collective-permute-done | bytes 524320 | tf_op jit(solution)/shard_map/ppermute | solution.py:284
  71.3 8.5 %collective-permute-done.31.refs_2_ = bf16[128,2048]{1,0:T(8,128)(2,1)S(1)} collective-permute-done((bf16[128,2048]{1,0:T(8,128)(2,1)S(1)}, bf16[128,2048]{1,0:T(8,128)(2,1)S(1)}, u32[]{:S(2)}, u32[]{:S(2)}) %collective-permute-start.31) | collective-permute-done | bytes 524320 | tf_op jit(solution)/shard_map/ppermute | solution.py:284
  83.6 11.2 %collective-permute-done.14.refs_3_ = bf16[128,2048]{1,0:T(8,128)(2,1)} collective-permute-done((bf16[128,2048]{1,0:T(8,128)(2,1)S(1)}, bf16[128,2048]{1,0:T(8,128)(2,1)}, u32[]{:S(2)}, u32[]{:S(2)}) %collective-permute-start.14) | collective-permute-done | bytes 524320 | tf_op jit(solution)/shard_map/ppermute | solution.py:285
  97.6 8.2 %collective-permute-done.20.refs_3_ = bf16[128,2048]{1,0:T(8,128)(2,1)S(1)} collective-permute-done((bf16[128,2048]{1,0:T(8,128)(2,1)S(1)}, bf16[128,2048]{1,0:T(8,128)(2,1)S(1)}, u32[]{:S(2)}, u32[]{:S(2)}) %collective-permute-start.20) | collective-permute-done | bytes 524320 | tf_op jit(solution)/shard_map/ppermute | solution.py:285
  109.5 7.8 %collective-permute-done.26.refs_3_ = bf16[128,2048]{1,0:T(8,128)(2,1)} collective-permute-done((bf16[128,2048]{1,0:T(8,128)(2,1)S(1)}, bf16[128,2048]{1,0:T(8,128)(2,1)}, u32[]{:S(2)}, u32[]{:S(2)}) %collective-permute-start.26) | collective-permute-done | bytes 524320 | tf_op jit(solution)/shard_map/ppermute | solution.py:285
  117.2 8.8 %collective-permute-done.32.refs_3_ = bf16[128,2048]{1,0:T(8,128)(2,1)} collective-permute-done((bf16[128,2048]{1,0:T(8,128)(2,1)S(1)}, bf16[128,2048]{1,0:T(8,128)(2,1)}, u32[]{:S(2)}, u32[]{:S(2)}) %collective-permute-start.32) | collective-permute-done | bytes 524320 | tf_op jit(solution)/shard_map/ppermute | solution.py:285
  133.2 18.2 %attention.1.attended_ref = bf16[256,2048]{1,0:T(8,128)(2,1)S(1)} custom-call(s32[1]{0:T(128)} %bitcast.3.refs_0_, s32[16]{0:T(128)S(1)} %copy-done.21, bf16[256,3072]{1,0:T(8,128)(2,1)S(1)} %copy-done.12, bf16[256,576]{1,0:T(8,128)(2,1)S(1)} %copy-done.11, bf16[16,9216]{1,0:T(8,128)(2,1)S(1)} %copy-done.14, bf16[16,9216]{1,0:T(8,128)(2,1)S(1)} %copy-done.16, ...), custom_call_target="tpu_custom_call" | custom-call | flops 10737418240 | bytes 8388608 | tf_op jit(solution)/shard_map/attention/pallas_call | solution.py:103
  151.5 4.8 %project.5 = (f32[256,256]{1,0:T(8,128)S(1)}, f32[256,256]{1,0:T(8,128)S(1)}, bf16[2,256,256]{2,1,0:T(8,128)(2,1)S(1)}) custom-call(s32[2]{0:T(128)S(1)} %pad_add_fusion.route_ref, bf16[256,2048]{1,0:T(8,128)(2,1)S(1)} %attention.1.attended_ref, bf16[1280,2048]{1,0:T(8,128)(2,1)} %refs_0_.9, bf16[1280,2048]{1,0:T(8,128)(2,1)} %collective-permute-done.6.refs_1_, ...), custom_call_target="tpu_custom_call" | custom-call | flops 1073741824 | bytes 4194304 | tf_op jit(solution)/shard_map/project/pallas_call | solution.py:187
  156.3 4.8 %project.6 = (f32[256,256]{1,0:T(8,128)S(1)}, f32[256,256]{1,0:T(8,128)S(1)}, bf16[2,256,256]{2,1,0:T(8,128)(2,1)S(1)}) custom-call(s32[2]{0:T(128)S(1)} %pad_add_fusion.route_ref, bf16[256,2048]{1,0:T(8,128)(2,1)S(1)} %attention.1.attended_ref, bf16[1280,2048]{1,0:T(8,128)(2,1)} %refs_0_.9, bf16[1280,2048]{1,0:T(8,128)(2,1)} %collective-permute-done.6.refs_1_, ...), custom_call_target="tpu_custom_call" | custom-call | flops 1073741824 | bytes 4194304 | tf_op jit(solution)/shard_map/project/pallas_call | solution.py:187
  161.7 4.6 %project.7 = (f32[256,256]{1,0:T(8,128)S(1)}, f32[256,256]{1,0:T(8,128)S(1)}, bf16[2,256,256]{2,1,0:T(8,128)(2,1)S(1)}) custom-call(s32[2]{0:T(128)S(1)} %pad_add_fusion.route_ref, bf16[256,2048]{1,0:T(8,128)(2,1)S(1)} %attention.1.attended_ref, bf16[1280,2048]{1,0:T(8,128)(2,1)} %refs_0_.9, bf16[1280,2048]{1,0:T(8,128)(2,1)} %collective-permute-done.6.refs_1_, ...), custom_call_target="tpu_custom_call" | custom-call | flops 1073741824 | bytes 4194304 | tf_op jit(solution)/shard_map/project/pallas_call | solution.py:187
  168.5 4.6 %project.8 = (f32[256,256]{1,0:T(8,128)S(1)}, f32[256,256]{1,0:T(8,128)S(1)}, bf16[2,256,256]{2,1,0:T(8,128)(2,1)S(1)}) custom-call(s32[2]{0:T(128)S(1)} %pad_add_fusion.route_ref, bf16[256,2048]{1,0:T(8,128)(2,1)S(1)} %attention.1.attended_ref, bf16[1280,2048]{1,0:T(8,128)(2,1)} %refs_0_.9, bf16[1280,2048]{1,0:T(8,128)(2,1)} %collective-permute-done.6.refs_1_, ...), custom_call_target="tpu_custom_call" | custom-call | flops 1073741824 | bytes 4194304 | tf_op jit(solution)/shard_map/project/pallas_call | solution.py:187
  174.7 4.6 %project.9 = (f32[256,256]{1,0:T(8,128)S(1)}, f32[256,256]{1,0:T(8,128)S(1)}, bf16[2,256,256]{2,1,0:T(8,128)(2,1)S(1)}) custom-call(s32[2]{0:T(128)S(1)} %pad_add_fusion.route_ref, bf16[256,2048]{1,0:T(8,128)(2,1)S(1)} %attention.1.attended_ref, bf16[1280,2048]{1,0:T(8,128)(2,1)} %refs_0_.9, bf16[1280,2048]{1,0:T(8,128)(2,1)} %collective-permute-done.6.refs_1_, ...), custom_call_target="tpu_custom_call" | custom-call | flops 1073741824 | bytes 4194304 | tf_op jit(solution)/shard_map/project/pallas_call | solution.py:187
  180.6 2.3 %collective-permute-start.18 = (bf16[256,256]{1,0:T(8,128)(2,1)S(1)}, bf16[256,256]{1,0:T(8,128)(2,1)S(1)}, u32[]{:S(2)}, u32[]{:S(2)}) collective-permute-start(bf16[256,256]{1,0:T(8,128)(2,1)S(1)} %fusion.16), channel_id=1, source_target_pairs={{0,2},{1,3},{2,0},{3,1},{4,6},{5,7},{6,4},{7,5},{8,10},{9,11},{10,... | collective-permute-start | bytes 393224 | tf_op jit(solution)/shard_map/ppermute | solution.py:311
  183.7 11.7 %collective-permute-done.29 = bf16[2,256,256]{2,1,0:T(8,128)(2,1)S(1)} collective-permute-done((bf16[2,256,256]{2,1,0:T(8,128)(2,1)S(1)}, bf16[2,256,256]{2,1,0:T(8,128)(2,1)S(1)}, u32[]{:S(2)}, u32[]{:S(2)}) %collective-permute-start.29) | collective-permute-done | bytes 262176 | tf_op jit(solution)/shard_map/ppermute | solution.py:310
  195.6 5.0 %collective-permute-done.35 = bf16[2,256,256]{2,1,0:T(8,128)(2,1)S(1)} collective-permute-done((bf16[2,256,256]{2,1,0:T(8,128)(2,1)S(1)}, bf16[2,256,256]{2,1,0:T(8,128)(2,1)S(1)}, u32[]{:S(2)}, u32[]{:S(2)}) %collective-permute-start.35) | collective-permute-done | bytes 262176 | tf_op jit(solution)/shard_map/ppermute | solution.py:310
  200.9 7.9 %collective-permute-done.30 = bf16[256,256]{1,0:T(8,128)(2,1)S(1)} collective-permute-done((bf16[256,256]{1,0:T(8,128)(2,1)S(1)}, bf16[256,256]{1,0:T(8,128)(2,1)S(1)}, u32[]{:S(2)}, u32[]{:S(2)}) %collective-permute-start.30) | collective-permute-done | bytes 131104 | tf_op jit(solution)/shard_map/ppermute | solution.py:311
  208.8 2.7 %collective-permute-done.36 = bf16[256,256]{1,0:T(8,128)(2,1)S(1)} collective-permute-done((bf16[256,256]{1,0:T(8,128)(2,1)S(1)}, bf16[256,256]{1,0:T(8,128)(2,1)S(1)}, u32[]{:S(2)}, u32[]{:S(2)}) %collective-permute-start.36) | collective-permute-done | bytes 131104 | tf_op jit(solution)/shard_map/ppermute | solution.py:311
  (157 shorter events, 47.5 us)
Async XLA Ops:
  8.8 117.8 %collective-permute-start.6 = (bf16[1280,2048]{1,0:T(8,128)(2,1)}, bf16[1280,2048]{1,0:T(8,128)(2,1)}, u32[]{:S(2)}, u32[]{:S(2)}) collective-permute-start(bf16[1280,2048]{1,0:T(8,128)(2,1)} %refs_0_.9), channel_id=1, source_target_pairs={{0,4},{4,0},{8,12},{12,8},{1,5},{5,1},{9,13},{13,9},{2,6},{6,2},{1... | collective-permute-start | bytes 15728648 | tf_op jit(solution)/shard_map/ppermute | solution.py:278
  23.1 24.6 %collective-permute-start.13 = (bf16[128,2048]{1,0:T(8,128)(2,1)S(1)}, bf16[128,2048]{1,0:T(8,128)(2,1)S(1)}, u32[]{:S(2)}, u32[]{:S(2)}) collective-permute-start(bf16[128,2048]{1,0:T(8,128)(2,1)S(1)} %get-tuple-element.49), channel_id=1, source_target_pairs={{0,8},{4,12},{8,0},{12,4},{1,9},{5,13},{9,1},{13,5},{2,10},{6,14},... | collective-permute-start | bytes 1572872 | tf_op jit(solution)/shard_map/ppermute | solution.py:284
  31.1 27.7 %collective-permute-start.19 = (bf16[128,2048]{1,0:T(8,128)(2,1)S(1)}, bf16[128,2048]{1,0:T(8,128)(2,1)S(1)}, u32[]{:S(2)}, u32[]{:S(2)}) collective-permute-start(bf16[128,2048]{1,0:T(8,128)(2,1)S(1)} %get-tuple-element.48), channel_id=1, source_target_pairs={{0,8},{4,12},{8,0},{12,4},{1,9},{5,13},{9,1},{13,5},{2,10},{6,14},... | collective-permute-start | bytes 1572872 | tf_op jit(solution)/shard_map/ppermute | solution.py:284
  32.9 37.1 %collective-permute-start.25 = (bf16[128,2048]{1,0:T(8,128)(2,1)S(1)}, bf16[128,2048]{1,0:T(8,128)(2,1)S(1)}, u32[]{:S(2)}, u32[]{:S(2)}) collective-permute-start(bf16[128,2048]{1,0:T(8,128)(2,1)S(1)} %get-tuple-element.47), channel_id=1, source_target_pairs={{0,8},{4,12},{8,0},{12,4},{1,9},{5,13},{9,1},{13,5},{2,10},{6,14},... | collective-permute-start | bytes 1572872 | tf_op jit(solution)/shard_map/ppermute | solution.py:284
  36.4 43.4 %collective-permute-start.31 = (bf16[128,2048]{1,0:T(8,128)(2,1)S(1)}, bf16[128,2048]{1,0:T(8,128)(2,1)S(1)}, u32[]{:S(2)}, u32[]{:S(2)}) collective-permute-start(bf16[128,2048]{1,0:T(8,128)(2,1)S(1)} %get-tuple-element.46), channel_id=1, source_target_pairs={{0,8},{4,12},{8,0},{12,4},{1,9},{5,13},{9,1},{13,5},{2,10},{6,14},... | collective-permute-start | bytes 1572872 | tf_op jit(solution)/shard_map/ppermute | solution.py:284
  47.6 34.4 %collective-permute-start.8 = (bf16[128,2048]{1,0:T(8,128)(2,1)S(1)}, bf16[128,2048]{1,0:T(8,128)(2,1)}, u32[]{:S(2)}, u32[]{:S(2)}) collective-permute-start(bf16[128,2048]{1,0:T(8,128)(2,1)S(1)} %collective-permute-done.7.refs_2_), channel_id=1, source_target_pairs={{0,16},{16,0},{1,17},{17,1},{2,18},{18,2},{3,19},{19,3},{4,20},{20... | collective-permute-start | bytes 1572872 | tf_op jit(solution)/shard_map/ppermute | solution.py:285
  58.9 23.7 %collective-permute-start.9 = (bf16[128,2048]{1,0:T(8,128)(2,1)S(1)}, bf16[128,2048]{1,0:T(8,128)(2,1)S(1)}, u32[]{:S(2)}, u32[]{:S(2)}) collective-permute-start(bf16[128,2048]{1,0:T(8,128)(2,1)S(1)} %collective-permute-done.7.refs_2_), channel_id=1, source_target_pairs={{0,4},{4,0},{8,12},{12,8},{1,5},{5,1},{9,13},{13,9},{2,6},{6,2},{1... | collective-permute-start | bytes 1572872 | tf_op jit(solution)/shard_map/ppermute | solution.py:290
  82.0 23.9 %collective-permute-start.20 = (bf16[128,2048]{1,0:T(8,128)(2,1)S(1)}, bf16[128,2048]{1,0:T(8,128)(2,1)S(1)}, u32[]{:S(2)}, u32[]{:S(2)}) collective-permute-start(bf16[128,2048]{1,0:T(8,128)(2,1)S(1)} %collective-permute-done.19.refs_2_), channel_id=1, source_target_pairs={{0,16},{16,0},{1,17},{17,1},{2,18},{18,2},{3,19},{19,3},{4,20},{20... | collective-permute-start | bytes 1572872 | tf_op jit(solution)/shard_map/ppermute | solution.py:285
  83.3 22.6 %collective-permute-start.21 = (bf16[128,2048]{1,0:T(8,128)(2,1)S(1)}, bf16[128,2048]{1,0:T(8,128)(2,1)S(1)}, u32[]{:S(2)}, u32[]{:S(2)}) collective-permute-start(bf16[128,2048]{1,0:T(8,128)(2,1)S(1)} %collective-permute-done.19.refs_2_), channel_id=1, source_target_pairs={{0,4},{4,0},{8,12},{12,8},{1,5},{5,1},{9,13},{13,9},{2,6},{6,2},{1... | collective-permute-start | bytes 1572872 | tf_op jit(solution)/shard_map/ppermute | solution.py:290
  94.7 22.5 %collective-permute-start.26 = (bf16[128,2048]{1,0:T(8,128)(2,1)S(1)}, bf16[128,2048]{1,0:T(8,128)(2,1)}, u32[]{:S(2)}, u32[]{:S(2)}) collective-permute-start(bf16[128,2048]{1,0:T(8,128)(2,1)S(1)} %collective-permute-done.25.refs_2_), channel_id=1, source_target_pairs={{0,16},{16,0},{1,17},{17,1},{2,18},{18,2},{3,19},{19,3},{4,20},{20... | collective-permute-start | bytes 1572872 | tf_op jit(solution)/shard_map/ppermute | solution.py:285
  97.1 28.9 %collective-permute-start.32 = (bf16[128,2048]{1,0:T(8,128)(2,1)S(1)}, bf16[128,2048]{1,0:T(8,128)(2,1)}, u32[]{:S(2)}, u32[]{:S(2)}) collective-permute-start(bf16[128,2048]{1,0:T(8,128)(2,1)S(1)} %collective-permute-done.31.refs_2_), channel_id=1, source_target_pairs={{0,16},{16,0},{1,17},{17,1},{2,18},{18,2},{3,19},{19,3},{4,20},{20... | collective-permute-start | bytes 1572872 | tf_op jit(solution)/shard_map/ppermute | solution.py:285
  105.9 20.1 %collective-permute-start.10 = (bf16[128,2048]{1,0:T(8,128)(2,1)}, bf16[128,2048]{1,0:T(8,128)(2,1)}, u32[]{:S(2)}, u32[]{:S(2)}) collective-permute-start(bf16[128,2048]{1,0:T(8,128)(2,1)} %collective-permute-done.8.refs_3_), channel_id=1, source_target_pairs={{0,4},{4,0},{8,12},{12,8},{1,5},{5,1},{9,13},{13,9},{2,6},{6,2},{1... | collective-permute-start | bytes 1572872 | tf_op jit(solution)/shard_map/ppermute | solution.py:291
  107.5 19.0 %collective-permute-start.16 = (bf16[128,2048]{1,0:T(8,128)(2,1)}, bf16[128,2048]{1,0:T(8,128)(2,1)}, u32[]{:S(2)}, u32[]{:S(2)}) collective-permute-start(bf16[128,2048]{1,0:T(8,128)(2,1)} %collective-permute-done.14.refs_3_), channel_id=1, source_target_pairs={{0,4},{4,0},{8,12},{12,8},{1,5},{5,1},{9,13},{13,9},{2,6},{6,2},{1... | collective-permute-start | bytes 1572872 | tf_op jit(solution)/shard_map/ppermute | solution.py:291
  117.2 49.2 %collective-permute-start.27 = (bf16[128,2048]{1,0:T(8,128)(2,1)S(1)}, bf16[128,2048]{1,0:T(8,128)(2,1)S(1)}, u32[]{:S(2)}, u32[]{:S(2)}) collective-permute-start(bf16[128,2048]{1,0:T(8,128)(2,1)S(1)} %collective-permute-done.25.refs_2_), channel_id=1, source_target_pairs={{0,4},{4,0},{8,12},{12,8},{1,5},{5,1},{9,13},{13,9},{2,6},{6,2},{1... | collective-permute-start | bytes 1572872 | tf_op jit(solution)/shard_map/ppermute | solution.py:290
  126.0 47.1 %collective-permute-start.33 = (bf16[128,2048]{1,0:T(8,128)(2,1)S(1)}, bf16[128,2048]{1,0:T(8,128)(2,1)S(1)}, u32[]{:S(2)}, u32[]{:S(2)}) collective-permute-start(bf16[128,2048]{1,0:T(8,128)(2,1)S(1)} %collective-permute-done.31.refs_2_), channel_id=1, source_target_pairs={{0,4},{4,0},{8,12},{12,8},{1,5},{5,1},{9,13},{13,9},{2,6},{6,2},{1... | collective-permute-start | bytes 1572872 | tf_op jit(solution)/shard_map/ppermute | solution.py:290
  126.0 35.2 %collective-permute-start.22 = (bf16[128,2048]{1,0:T(8,128)(2,1)}, bf16[128,2048]{1,0:T(8,128)(2,1)S(1)}, u32[]{:S(2)}, u32[]{:S(2)}) collective-permute-start(bf16[128,2048]{1,0:T(8,128)(2,1)} %copy-done.5), channel_id=1, source_target_pairs={{0,4},{4,0},{8,12},{12,8},{1,5},{5,1},{9,13},{13,9},{2,6},{6,2},{1... | collective-permute-start | bytes 1572872 | tf_op jit(solution)/shard_map/ppermute | solution.py:291
  126.5 41.5 %collective-permute-start.28 = (bf16[128,2048]{1,0:T(8,128)(2,1)}, bf16[128,2048]{1,0:T(8,128)(2,1)S(1)}, u32[]{:S(2)}, u32[]{:S(2)}) collective-permute-start(bf16[128,2048]{1,0:T(8,128)(2,1)} %collective-permute-done.26.refs_3_), channel_id=1, source_target_pairs={{0,4},{4,0},{8,12},{12,8},{1,5},{5,1},{9,13},{13,9},{2,6},{6,2},{1... | collective-permute-start | bytes 1572872 | tf_op jit(solution)/shard_map/ppermute | solution.py:291
  126.6 48.2 %collective-permute-start.34 = (bf16[128,2048]{1,0:T(8,128)(2,1)}, bf16[128,2048]{1,0:T(8,128)(2,1)S(1)}, u32[]{:S(2)}, u32[]{:S(2)}) collective-permute-start(bf16[128,2048]{1,0:T(8,128)(2,1)} %collective-permute-done.32.refs_3_), channel_id=1, source_target_pairs={{0,4},{4,0},{8,12},{12,8},{1,5},{5,1},{9,13},{13,9},{2,6},{6,2},{1... | collective-permute-start | bytes 1572872 | tf_op jit(solution)/shard_map/ppermute | solution.py:291
  161.2 18.6 %collective-permute-start.11 = (bf16[2,256,256]{2,1,0:T(8,128)(2,1)S(1)}, bf16[2,256,256]{2,1,0:T(8,128)(2,1)S(1)}, u32[]{:S(2)}, u32[]{:S(2)}) collective-permute-start(bf16[2,256,256]{2,1,0:T(8,128)(2,1)S(1)} %get-tuple-element.22), channel_id=1, source_target_pairs={{0,1},{1,0},{2,3},{3,2},{4,5},{5,4},{6,7},{7,6},{8,9},{9,8},{10,11... | collective-permute-start | bytes 786440 | tf_op jit(solution)/shard_map/ppermute | solution.py:310
  173.1 22.4 %collective-permute-start.29 = (bf16[2,256,256]{2,1,0:T(8,128)(2,1)S(1)}, bf16[2,256,256]{2,1,0:T(8,128)(2,1)S(1)}, u32[]{:S(2)}, u32[]{:S(2)}) collective-permute-start(bf16[2,256,256]{2,1,0:T(8,128)(2,1)S(1)} %get-tuple-element.31), channel_id=1, source_target_pairs={{0,1},{1,0},{2,3},{3,2},{4,5},{5,4},{6,7},{7,6},{8,9},{9,8},{10,11... | collective-permute-start | bytes 786440 | tf_op jit(solution)/shard_map/ppermute | solution.py:310
  179.3 21.2 %collective-permute-start.35 = (bf16[2,256,256]{2,1,0:T(8,128)(2,1)S(1)}, bf16[2,256,256]{2,1,0:T(8,128)(2,1)S(1)}, u32[]{:S(2)}, u32[]{:S(2)}) collective-permute-start(bf16[2,256,256]{2,1,0:T(8,128)(2,1)S(1)} %get-tuple-element.34), channel_id=1, source_target_pairs={{0,1},{1,0},{2,3},{3,2},{4,5},{5,4},{6,7},{7,6},{8,9},{9,8},{10,11... | collective-permute-start | bytes 786440 | tf_op jit(solution)/shard_map/ppermute | solution.py:310
  179.9 20.8 %collective-permute-start.12 = (bf16[256,256]{1,0:T(8,128)(2,1)S(1)}, bf16[256,256]{1,0:T(8,128)(2,1)S(1)}, u32[]{:S(2)}, u32[]{:S(2)}) collective-permute-start(bf16[256,256]{1,0:T(8,128)(2,1)S(1)} %fusion.19), channel_id=1, source_target_pairs={{0,2},{1,3},{2,0},{3,1},{4,6},{5,7},{6,4},{7,5},{8,10},{9,11},{10,... | collective-permute-start | bytes 393224 | tf_op jit(solution)/shard_map/ppermute | solution.py:311
  180.6 20.1 %collective-permute-start.18 = (bf16[256,256]{1,0:T(8,128)(2,1)S(1)}, bf16[256,256]{1,0:T(8,128)(2,1)S(1)}, u32[]{:S(2)}, u32[]{:S(2)}) collective-permute-start(bf16[256,256]{1,0:T(8,128)(2,1)S(1)} %fusion.16), channel_id=1, source_target_pairs={{0,2},{1,3},{2,0},{3,1},{4,6},{5,7},{6,4},{7,5},{8,10},{9,11},{10,... | collective-permute-start | bytes 393224 | tf_op jit(solution)/shard_map/ppermute | solution.py:311
  183.0 17.8 %collective-permute-start.24 = (bf16[256,256]{1,0:T(8,128)(2,1)S(1)}, bf16[256,256]{1,0:T(8,128)(2,1)S(1)}, u32[]{:S(2)}, u32[]{:S(2)}) collective-permute-start(bf16[256,256]{1,0:T(8,128)(2,1)S(1)} %fusion.13), channel_id=1, source_target_pairs={{0,2},{1,3},{2,0},{3,1},{4,6},{5,7},{6,4},{7,5},{8,10},{9,11},{10,... | collective-permute-start | bytes 393224 | tf_op jit(solution)/shard_map/ppermute | solution.py:311
  (37 other events, 353.8 us)

commit v2 on v1

v2 whole, which is shorter than its diff:
```python
import math

import jax
import jax.numpy as jnp
from jax import lax
from jax.experimental import pallas as pl
from jax.experimental.pallas import tpu as pltpu
from jax.sharding import PartitionSpec as P

KVR = 512
NOPE = 128
VD = 128
BT = 64
STRETCH = 256
BLK = 16
LAT = 576
QKD = 192
ROPE = LAT - KVR
MASKED = -1e30
PIECES = (192, 288, 256, 256, 288)
STEPS = (2, 2, 1)
VMEM_BYTES = 60 * 1024 * 1024
SMALL_COST = pl.CostEstimate(flops=1024, bytes_accessed=1024, transcendentals=0)
BF16 = jnp.bfloat16
F32 = jnp.float32


def attention_kernel(blocks_ref, mask_ref, query_ref, stretch_ref, *refs, together, skipped):
    *pieces, key_ref, value_ref, out_ref, latent, rope = refs
    step = pl.program_id(0)
    piece_tokens = pieces[0].shape[1] // LAT
    prefix = len(pieces) * piece_tokens * BLK
    total = prefix + STRETCH

    @pl.when(step == 0)
    def _():
        lane = lax.broadcasted_iota(jnp.int32, (BLK, ROPE), 1)
        row = lax.broadcasted_iota(jnp.int32, (BLK, ROPE), 0)
        hidden = (lane == 0) & (row >= blocks_ref[0])
        extra = jnp.where(hidden, MASKED, 0.0).astype(BF16)
        for index, piece in enumerate(pieces):
            for token in range(piece_tokens):
                start = (index * piece_tokens + token) * BLK
                base = LAT * token
                latent[start : start + BLK, :] = piece[:, base : base + KVR]
                rope[start : start + BLK, :] = jnp.concatenate(
                    [piece[:, base + KVR : base + LAT], extra], axis=1
                )
        latent[prefix:total, :] = stretch_ref[:, :KVR]
        rope[prefix:total, :] = jnp.concatenate(
            [stretch_ref[:, KVR:], jnp.zeros((STRETCH, ROPE), BF16)], axis=1
        )

    compressed = latent[...]
    keys = jnp.dot(compressed, key_ref[...], preferred_element_type=F32).astype(BF16)
    values = jnp.dot(compressed, value_ref[...], preferred_element_type=F32).astype(BF16)
    key_rope = rope[...]
    ones = jnp.ones((total, VD), BF16)
    lane = lax.broadcasted_iota(jnp.int32, (STRETCH, ROPE), 1)
    query_extra = jnp.where(lane == 0, 1.0, 0.0).astype(BF16)
    scale = 1.0 / (math.sqrt(QKD) * math.log(2.0))
    causal = lax.broadcasted_iota(jnp.int32, (STRETCH, STRETCH), 1) <= lax.broadcasted_iota(
        jnp.int32, (STRETCH, STRETCH), 0
    )
    for part in range(together):
        here = slice(part * VD, (part + 1) * VD)
        query = jnp.concatenate(
            [query_ref[:, part * QKD : (part + 1) * QKD], query_extra], axis=1
        )
        key = jnp.concatenate([keys[:, here], key_rope], axis=1)
        scores = lax.dot_general(
            query, key, (((1,), (1,)), ((), ())), preferred_element_type=F32
        )
        before = scores[:, :prefix]
        own = jnp.where(causal, scores[:, prefix:], MASKED)
        largest = jnp.maximum(
            jnp.max(before, axis=1, keepdims=True), jnp.max(own, axis=1, keepdims=True)
        )
        weights = jnp.concatenate(
            [
                jnp.exp2((before - largest) * scale).astype(BF16),
                jnp.exp2((own - largest) * scale).astype(BF16),
            ],
            axis=1,
        )
        value = jnp.concatenate([values[:, here], ones], axis=1)
        summed = jnp.dot(weights, value, preferred_element_type=F32)
        attended = (summed[:, :VD] / summed[:, VD:]).astype(BF16)
        kept = mask_ref[together * (step + skipped) + part].astype(F32).astype(BF16)
        out_ref[:, here] = attended * kept


def attention(blocks, head_mask, query, latent, pieces, up_key, up_value, part=0, parts=1):
    heads = up_key.shape[1] // NOPE // parts
    together = math.gcd(heads, 4)
    skipped = part * (heads // together)
    piece_tokens = pieces[0].shape[1] // LAT
    total = len(pieces) * piece_tokens * BLK + STRETCH

    def whole(array):
        return pl.BlockSpec(array.shape, lambda step: (0, 0))

    def columns(rows, width):
        return pl.BlockSpec((rows, together * width), lambda step: (0, step + skipped))

    smem = pl.BlockSpec(memory_space=pltpu.SMEM)
    return pl.pallas_call(
        lambda *refs: attention_kernel(*refs, together=together, skipped=skipped),
        grid=(heads // together,),
        in_specs=[smem, smem, columns(STRETCH, QKD)]
        + [whole(array) for array in [latent, *pieces]]
        + [columns(KVR, NOPE), columns(KVR, VD)],
        out_specs=pl.BlockSpec((STRETCH, together * VD), lambda step: (0, step)),
        out_shape=jax.ShapeDtypeStruct((STRETCH, heads * VD), BF16),
        scratch_shapes=[
            pltpu.VMEM((total, KVR), BF16),
            pltpu.VMEM((total, 2 * ROPE), BF16),
        ],
        compiler_params=pltpu.CompilerParams(vmem_limit_bytes=VMEM_BYTES),
        cost_estimate=pl.CostEstimate(
            flops=18_000_000_000 // parts, bytes_accessed=4 * 1024 * 1024, transcendentals=0
        ),
        name="attention",
    )(blocks, head_mask, query, latent, *pieces, up_key, up_value)


def hit_tables(hit_slot, hit_owner, prefix_len, own_req, capacity, sources, stride):
    block_index = jnp.arange(BLK)
    in_prefix = block_index[None, :] < (prefix_len // BT)[:, None]
    own_hits = in_prefix & (hit_owner == own_req)
    rank = jnp.cumsum(own_hits.astype(jnp.int32), axis=1) - 1
    chosen = own_hits[:, None, :] & (rank[:, None, :] == jnp.arange(capacity)[None, :, None])
    slots = jnp.sum(jnp.where(chosen, hit_slot[:, None, :], 0), axis=2)
    length = lax.dynamic_index_in_dim(prefix_len, own_req, 0, False)
    owners = lax.dynamic_index_in_dim(hit_owner, own_req, 0, False)
    from_source = (owners[:, None] == sources[None, :]) & (block_index < length // BT)[:, None]
    ranks = jnp.cumsum(from_source.astype(jnp.int32), axis=0) - 1
    picks = from_source[:, :, None] & (ranks[:, :, None] == jnp.arange(stride)[None, None, :])
    return slots, picks.reshape(BLK, -1).astype(BF16), (length // BT).reshape(1)


def refs_by_piece(refs, counts):
    refs = list(refs)
    return [[refs.pop(0) for _ in range(count)] for count in counts]


def project_kernel(route_ref, *refs, start, rows, pair_counts):
    halves, weight_hbm, refs = refs[:4], refs[4], refs[5:]
    pieces = refs[:-5]
    out_ref, attended, weights, totals, sems = refs[-5:]
    turn, group = route_ref[0], route_ref[1]
    tokens, width = halves[0].shape
    copies = [
        (halves[0], attended.at[:tokens, :width]),
        (halves[1], attended.at[:tokens, width:]),
        (weight_hbm.at[pl.ds(start, rows)], weights.at[0]),
        (halves[2], attended.at[tokens:, :width]),
        (halves[3], attended.at[tokens:, width:]),
    ]
    place = 0
    for pair in refs_by_piece(pieces, pair_counts):
        size = sum(piece.shape[0] for piece in pair)
        for index, piece in enumerate(pair):
            half = piece.shape[0]
            offset = place + ((group if index == 0 else 1 - group) * half if len(pair) == 2 else 0)
            copies.append((piece, weights.at[1, pl.ds(pl.multiple_of(offset, 16), half)]))
        place += size
    copies = [
        pltpu.make_async_copy(source, target, sems.at[index])
        for index, (source, target) in enumerate(copies)
    ]
    last = tuple(range(5, len(copies)))
    needs = ((0, 0, (0, 1, 2), (3, 4) + last), (0, 1, (3, 4), ()), (1, 0, last, ()), (1, 1, (), ()))
    for index in needs[0][2]:
        copies[index].start()
    for unit, request, awaited, following in needs:
        for index in awaited:
            copies[index].wait()
        for index in following:
            copies[index].start()
        span = slice(request * tokens, (request + 1) * tokens)
        totals[unit ^ turn, :, span] = lax.dot_general(
            weights[unit], attended[span], (((1,), (1,)), ((), ())), preferred_element_type=F32
        )
    for slot in range(2):
        out_ref[slot] = totals[slot].astype(BF16)


def project(route, halves, weight, pieces, start, rows):
    tokens, width = halves[0].shape[0], weight.shape[1]
    flat = [piece for pair in pieces for piece in pair]
    hbm = pl.BlockSpec(memory_space=pl.ANY)
    return pl.pallas_call(
        lambda *refs: project_kernel(
            *refs, start=start, rows=rows, pair_counts=[len(pair) for pair in pieces]
        ),
        in_specs=[pl.BlockSpec(memory_space=pltpu.SMEM)] + [hbm] * (5 + len(flat)),
        out_specs=pl.BlockSpec(memory_space=pltpu.VMEM),
        out_shape=jax.ShapeDtypeStruct((2, rows, 2 * tokens), BF16),
        scratch_shapes=[
            pltpu.VMEM((2 * tokens, width), BF16),
            pltpu.VMEM((2, rows, width), BF16),
            pltpu.VMEM((2, rows, 2 * tokens), F32),
            pltpu.SemaphoreType.DMA((5 + len(flat),)),
        ],
        compiler_params=pltpu.CompilerParams(vmem_limit_bytes=VMEM_BYTES),
        cost_estimate=pl.CostEstimate(
            flops=5_000_000_000, bytes_accessed=4 * 1024 * 1024, transcendentals=0
        ),
        name="project",
    )(route, *halves, weight, *flat)


def finish_kernel(route_ref, *refs, starts, sizes):
    out_ref = refs[-1]
    kept = route_ref[2] == 1
    for index, (start, rows) in enumerate(zip(starts, sizes)):
        own, other = refs[2 * index : 2 * index + 2]

        @pl.when(kept)
        def _():
            out_ref[:, start : start + rows] = own[...].astype(F32).T.astype(BF16)

        @pl.when(jnp.logical_not(kept))
        def _():
            out_ref[:, start : start + rows] = other[...].astype(F32).T.astype(BF16)


def finish(route, sums, starts, sizes):
    vmem = pl.BlockSpec(memory_space=pltpu.VMEM)
    tokens = sums[0].shape[1]
    return pl.pallas_call(
        lambda *refs: finish_kernel(*refs, starts=starts, sizes=sizes),
        in_specs=[pl.BlockSpec(memory_space=pltpu.SMEM)] + [vmem] * len(sums),
        out_specs=vmem,
        out_shape=jax.ShapeDtypeStruct((tokens, sum(sizes)), BF16),
        compiler_params=pltpu.CompilerParams(vmem_limit_bytes=VMEM_BYTES),
        cost_estimate=SMALL_COST,
        name="finish",
    )(route, *sums)


def pick_kernel(self_ref, owner_ref, slot_ref, length_ref, pool_ref, *refs, capacity):
    outs, table = refs[:-1], refs[-1]
    requests = len(outs)
    own = self_ref[0]
    rows = pool_ref.shape[0]
    lane = lax.broadcasted_iota(jnp.int32, (8, rows), 1)
    row = lax.broadcasted_iota(jnp.int32, (8, rows), 0)
    for bit in range(requests):
        target = own ^ bit
        blocks = length_ref[target] // BT
        for rank in range(capacity):
            table[rank] = 0

        def note(block, count):
            owned = (owner_ref[target, block] == own) & (block < blocks)

            @pl.when(owned & (count < capacity))
            def _():
                table[count] = slot_ref[target, block]

            return count + owned.astype(jnp.int32)

        lax.fori_loop(0, BLK, note, jnp.int32(0), unroll=True)
        chosen = jnp.zeros((8, rows), F32)
        for rank in range(capacity):
            chosen = jnp.where((row == rank) & (lane == table[rank]), 1.0, chosen)
        outs[bit][...] = jnp.dot(
            chosen.astype(BF16), pool_ref[...], preferred_element_type=F32
        ).astype(BF16)


def pick(own_req, hit_owner, hit_slot, prefix_len, cache_pool, capacity):
    requests = hit_owner.shape[0]
    smem = pl.BlockSpec(memory_space=pltpu.SMEM)
    vmem = pl.BlockSpec(memory_space=pltpu.VMEM)
    return pl.pallas_call(
        lambda *refs: pick_kernel(*refs, capacity=capacity),
        in_specs=[smem] * 4 + [vmem],
        out_specs=[vmem] * requests,
        out_shape=[jax.ShapeDtypeStruct((8, cache_pool.shape[1]), BF16)] * requests,
        scratch_shapes=[pltpu.SMEM((capacity,), jnp.int32)],
        compiler_params=pltpu.CompilerParams(vmem_limit_bytes=VMEM_BYTES),
        cost_estimate=SMALL_COST,
        name="pick",
    )(own_req.reshape(1), hit_owner, hit_slot, prefix_len, cache_pool)


def after(value, *earlier):
    return lax.optimization_barrier((value, *earlier))[0] if earlier else value


def flip(size, bit):
    return [(index, index ^ bit) for index in range(size)]


def local(
    stretch_query,
    stretch_latent,
    cache_pool,
    hit_slot,
    hit_owner,
    prefix_len,
    head_mask,
    up_key,
    up_value,
    out_weight,
):
    groups = lax.axis_size("groups")
    req_count = lax.axis_size("req")
    head_count = lax.axis_size("head")
    capacity = max(2, (BLK + req_count - 1) // req_count * 3 // 2)
    own_req = lax.axis_index("req")
    own_head = lax.axis_index("head")
    paired = groups == 2 and req_count == 4 and head_count == 4 and sum(PIECES) == out_weight.shape[0]
    order = jnp.arange(req_count)
    partners = order ^ own_req if paired else order
    slots, picks, blocks = hit_tables(
        hit_slot, hit_owner, prefix_len, own_req, capacity, partners, 8 if paired else capacity
    )
    if not paired:
        outgoing = jnp.take(cache_pool, slots.reshape(-1), axis=0)
        incoming = lax.all_to_all(outgoing, "req", split_axis=0, concat_axis=0, tiled=True)
        prefix = jnp.dot(picks, incoming, preferred_element_type=F32).astype(BF16)
        gathered = lax.all_gather(prefix, "head", axis=0)
        pieces = [gathered[index] for index in range(head_count)]
        attended = attention(
            blocks, head_mask, stretch_query, stretch_latent, pieces, up_key, up_value
        )
        partial_out = lax.dot_general(
            attended,
            lax.all_gather(out_weight, "req", axis=0, tiled=True),
            (((1,), (1,)), ((), ())),
            preferred_element_type=F32,
        )
        return lax.psum_scatter(partial_out, "head", scatter_dimension=1, tiled=True).astype(BF16)

    own_group = lax.axis_index("groups")
    sizes = PIECES
    starts = [sum(sizes[:index]) for index in range(len(sizes))]

    def over_y(chunk, *earlier):
        size = sizes[chunk]
        weights = after(out_weight, *earlier)
        if chunk == len(sizes) - 1:
            piece = lax.slice_in_dim(weights, starts[chunk], starts[chunk] + size, axis=0)
        else:
            half = size // 2
            piece = lax.dynamic_slice_in_dim(weights, starts[chunk] + own_group * half, half, 0)
        return lax.ppermute(piece, "req", flip(req_count, 2))

    def over_x(piece, *earlier):
        return lax.ppermute(after(piece, *earlier), "groups", flip(groups, 1))

    def over_z(piece, bit):
        return lax.ppermute(piece, "head", flip(head_count, bit))

    outgoing = pick(own_req, hit_owner, hit_slot, prefix_len, cache_pool, capacity)
    incoming = [outgoing[0]] + [
        lax.ppermute(outgoing[bit], "req", flip(req_count, bit)) for bit in (1, 2, 3)
    ]
    y0 = over_y(0, *outgoing)
    y1 = over_y(1, incoming[1])
    prefix = jnp.dot(
        picks, jnp.concatenate(incoming, axis=0), preferred_element_type=F32
    ).astype(BF16)
    far = over_z(prefix, 2)
    near = over_z(prefix, 1)
    farther = over_z(after(far, near, y1), 1)
    x0 = over_x(y0, far)
    x1 = over_x(y1)
    y2 = over_y(2, y1)

    def attend(part, *earlier):
        return attention(
            blocks,
            head_mask,
            after(stretch_query, *earlier),
            stretch_latent,
            [prefix, near, far, farther],
            up_key,
            up_value,
            part,
            2,
        )

    def over_core(piece):
        return lax.ppermute(piece, "req", flip(req_count, 1))

    first = attend(0, x0)
    second = attend(1, first, x1, y2)
    beside = over_core(first)
    x2 = over_x(y2)
    y3 = over_y(3, y2)
    halves = (first, second, beside, over_core(after(second, beside)))

    core = own_req & 1
    keeper = (own_head & 1) == core
    route = jnp.stack([(own_head >> 1) ^ (own_req >> 1), own_group, keeper]).astype(jnp.int32)
    devices = [(req, head) for req in range(req_count) for head in range(head_count)]

    def place(req, head):
        return req * head_count + head

    to_keeper = [
        (place(req, head), place(req, head ^ 1)) for req, head in devices if (req ^ head) & 1
    ]
    to_far = [
        (place(req, head), place(req, head ^ 2)) for req, head in devices if not (req ^ head) & 1
    ]
    to_core = [
        (place(req, head), place(req ^ 1, head)) for req, head in devices if not (req ^ head) & 1
    ]
    axes = ("req", "head")

    bounds = [sum(STEPS[:index]) for index in range(len(STEPS) + 1)]
    spans = [
        (starts[first], sum(sizes[first:last])) for first, last in zip(bounds[:-1], bounds[1:])
    ]

    def send(chunk, pieces, *earlier):
        sums = project(after(route, *earlier), halves, out_weight, pieces, *spans[chunk])
        return sums, lax.ppermute(sums, axes, to_keeper)

    def halve(sums, received):
        total = (sums[1].astype(F32) + received[1].astype(F32)).astype(BF16)
        return total, lax.ppermute(total, axes, to_far)

    def settle(sums, received, passed):
        total = sums[0].astype(F32) + received[0].astype(F32) + passed.astype(F32)
        return total.astype(BF16)

    def split(total):
        own, other = total[:, :STRETCH], total[:, STRETCH:]
        return [own, lax.ppermute(other, axes, to_core)]

    sums0, got0 = send(0, [(y0, x0), (y1, x1)], x2)
    x3 = over_x(y3)
    y4 = over_y(4, y3)
    total0, passed0 = halve(sums0, got0)
    sums1, got1 = send(1, [(y2, x2), (y3, x3)], sums0)
    sums2, got2 = send(2, [(y4,)], sums1, total0)
    total1, passed1 = halve(sums1, after(got1, passed0))
    total2, passed2 = halve(sums2, got2)
    early = [settle(sums0, got0, passed0), settle(sums1, got1, passed1)]
    settled = split(jnp.concatenate(early, axis=0)) + split(settle(sums2, got2, passed2))
    return finish(route, settled, (0, spans[2][0]), spans[2])


def solution(mesh):
    placed = (
        P(("groups", "req"), "head"),
        P(("groups", "req"), None),
        P(("groups", "req"), "head"),
        P("groups", None),
        P("groups", None),
        P("groups"),
        P("head"),
        P(None, "head"),
        P(None, "head"),
        P("req", "head"),
    )
    return jax.shard_map(
        local, mesh=mesh, in_specs=placed, out_specs=P(("groups", "req"), "head"), check_vma=False
    )
```

time: 213 us -> 152 us (0.71)
  waiting for transfers between devices: 110 us -> 46.2 us
  local copies, waits for them, and re-layouts: 20.9 us -> 11.6 us
  starting transfers between devices: 31.4 us -> 39.4 us
  Pallas kernels: 41.7 us -> 46.5 us
    ppermute x34 -> x22, waiting for transfers between devices: 110 us -> 46.2 us  [the longest x5 14.4 us: over_y(): return lax.ppermute(piece, 'req', flip(req_count, 2))]
    unnamed x49 -> x41, local copies, waits for them, and re-layouts: 14.3 us -> 3.47 us
    ppermute x34 -> x22, starting transfers between devices: 28.1 us -> 36.3 us  [the longest x3 11.2 us: halve(): return (total, lax.ppermute(total, axes, to_far))]
    pallas_call x6 -> x7, Pallas kernels: 41.7 us -> 46.5 us  [the longest x3 20.8 us: project(): pl.pallas_call(lambda *refs: project_kernel(*refs, start=start, rows=rows...]
    gather x5 -> x0, local copies, waits for them, and re-layouts: 3.03 us -> none  [the longest x4 2.47 us: local(): jnp.take(cache_pool, slots[index], axis=0)]
    dynamic_slice x1 -> x4, local copies, waits for them, and re-layouts: 1.85 us -> 4.49 us  [over_y(): lax.dynamic_slice_in_dim(weights, starts[chunk] + own_group * half, half, 0)]
  transfers between devices with their start and end apart: 37 -> 25, of which waited for: 15 -> 11; matrix products, arithmetic and copies ran while one was open for 4% -> 9% of each run, Pallas kernels for 20% -> 27%
where the time goes in v2:
time: 152 us
  Pallas kernels  46.5 us (31%)
  waiting for transfers between devices  46.2 us (30%)
  starting transfers between devices  39.4 us (26%)
  local copies, waits for them, and re-layouts  11.6 us (8%)
  other arithmetic  4.63 us (3%)
  between operations  2.83 us (2%)
    pallas_call x3, Pallas kernels, project(): pl.pallas_call(lambda *refs: project_kernel(*refs, start=start, rows=rows...  20.8 us
    pallas_call x2, Pallas kernels, attention(): pl.pallas_call(lambda *refs: attention_kernel(*refs, together=together, s...  20.4 us
    ppermute x5, waiting for transfers between devices, over_y(): return lax.ppermute(piece, 'req', flip(req_count, 2))  14.4 us
    ppermute x3, waiting for transfers between devices, send(): return (sums, lax.ppermute(sums, axes, to_keeper))  13 us
    ppermute x3, starting transfers between devices, halve(): return (total, lax.ppermute(total, axes, to_far))  11.2 us
    ppermute x3, waiting for transfers between devices, over_z(): return lax.ppermute(piece, 'head', flip(head_count, bit))  10.7 us
    ppermute x3, starting transfers between devices, over_z(): return lax.ppermute(piece, 'head', flip(head_count, bit))  6.22 us
    ppermute x4, starting transfers between devices, over_x(): return lax.ppermute(after(piece, *earlier), 'groups', flip(groups, 1))  6.03 us
  transfers between devices with their start and end apart: 25, of which 11 were waited for; matrix products, arithmetic and copies ran while one was open for 9% of the time, Pallas kernels for 27%

profile of v2, /device:TPU:0, one launch (start us, length us, event | category | flops | bytes accessed | tf_op | source)
XLA Modules:
  0.0 151.5 jit_solution(14044319852203464545)
XLA Ops:
  0.0 2.8 %pick.1 = (bf16[8,9216]{1,0:T(8,128)(2,1)}, bf16[8,9216]{1,0:T(8,128)(2,1)}, bf16[8,9216]{1,0:T(8,128)(2,1)}, bf16[8,9216]{1,0:T(8,128)(2,1)}) custom-call(s32[1]{0:T(128)} %bitcast.3.refs_0_, s32[4,16]{1,0:T(4,128)} %refs_1_.3, s32[4,16]{1,0:T(4,128)} %refs_2_.1, s32[4]{0:T(128)} %refs_3_.3, bf16[64,9216]{1,0:T(8,128)(2,1)} %refs_4_.1), custom_call_target="tpu_custom_call" | custom-call | flops 1024 | bytes 1024 | tf_op jit(solution)/shard_map/pick/pallas_call | solution.py:278
  3.2 2.6 %collective-permute-start.5 = (bf16[8,9216]{1,0:T(8,128)(2,1)}, bf16[8,9216]{1,0:T(8,128)(2,1)S(1)}, u32[]{:S(2)}, u32[]{:S(2)}) collective-permute-start(bf16[8,9216]{1,0:T(8,128)(2,1)} %get-tuple-element.28), channel_id=1, source_target_pairs={{0,8},{4,12},{8,0},{12,4},{1,9},{5,13},{9,1},{13,5},{2,10},{6,14},... | collective-permute-start | bytes 442376 | tf_op jit(solution)/shard_map/ppermute | solution.py:361
  6.9 1.8 %collective-permute-start.4 = (bf16[96,2048]{1,0:T(8,128)(2,1)S(1)}, bf16[96,2048]{1,0:T(8,128)(2,1)S(1)}, u32[]{:S(2)}, u32[]{:S(2)}) collective-permute-start(bf16[96,2048]{1,0:T(8,128)(2,1)S(1)} %constant_dynamic-slice_fusion.2), channel_id=1, source_target_pairs={{0,8},{4,12},{8,0},{12,4},{1,9},{5,13},{9,1},{13,5},{2,10},{6,14},... | collective-permute-start | bytes 1179656 | tf_op jit(solution)/shard_map/ppermute | solution.py:351
  14.7 2.8 %collective-permute-start.7 = (bf16[16,9216]{1,0:T(8,128)(2,1)S(1)}, bf16[16,9216]{1,0:T(8,128)(2,1)S(1)}, u32[]{:S(2)}, u32[]{:S(2)}) collective-permute-start(bf16[16,9216]{1,0:T(8,128)(2,1)S(1)} %convolution_convert_fusion.refs_4_), channel_id=1, source_target_pairs={{0,2},{1,3},{2,0},{3,1},{4,6},{5,7},{6,4},{7,5},{8,10},{9,11},{10,... | collective-permute-start | bytes 884744 | tf_op jit(solution)/shard_map/ppermute | solution.py:357
  19.2 3.1 %collective-permute-done.4.refs_6_ = bf16[96,2048]{1,0:T(8,128)(2,1)S(1)} collective-permute-done((bf16[96,2048]{1,0:T(8,128)(2,1)S(1)}, bf16[96,2048]{1,0:T(8,128)(2,1)S(1)}, u32[]{:S(2)}, u32[]{:S(2)}) %collective-permute-start.4) | collective-permute-done | bytes 393248 | tf_op jit(solution)/shard_map/ppermute | solution.py:351
  22.3 8.7 %collective-permute-done.7.refs_6_ = bf16[16,9216]{1,0:T(8,128)(2,1)S(1)} collective-permute-done((bf16[16,9216]{1,0:T(8,128)(2,1)S(1)}, bf16[16,9216]{1,0:T(8,128)(2,1)S(1)}, u32[]{:S(2)}, u32[]{:S(2)}) %collective-permute-start.7) | collective-permute-done | bytes 294944 | tf_op jit(solution)/shard_map/ppermute | solution.py:357
  32.5 2.2 %collective-permute-done.1.refs_8_ = bf16[144,2048]{1,0:T(8,128)(2,1)S(1)} collective-permute-done((bf16[144,2048]{1,0:T(8,128)(2,1)S(1)}, bf16[144,2048]{1,0:T(8,128)(2,1)S(1)}, u32[]{:S(2)}, u32[]{:S(2)}) %collective-permute-start.1) | collective-permute-done | bytes 589856 | tf_op jit(solution)/shard_map/ppermute | solution.py:351
  34.7 1.8 %collective-permute-start.10 = (bf16[16,9216]{1,0:T(8,128)(2,1)S(1)}, bf16[16,9216]{1,0:T(8,128)(2,1)}, u32[]{:S(2)}, u32[]{:S(2)}) collective-permute-start(bf16[16,9216]{1,0:T(8,128)(2,1)S(1)} %collective-permute-done.7.refs_6_), channel_id=1, source_target_pairs={{0,1},{1,0},{2,3},{3,2},{4,5},{5,4},{6,7},{7,6},{8,9},{9,8},{10,11... | collective-permute-start | bytes 884744 | tf_op jit(solution)/shard_map/ppermute | solution.py:357
  41.6 2.0 %collective-permute-done.10.refs_7_ = bf16[16,9216]{1,0:T(8,128)(2,1)} collective-permute-done((bf16[16,9216]{1,0:T(8,128)(2,1)S(1)}, bf16[16,9216]{1,0:T(8,128)(2,1)}, u32[]{:S(2)}, u32[]{:S(2)}) %collective-permute-start.10) | collective-permute-done | bytes 294944 | tf_op jit(solution)/shard_map/ppermute | solution.py:357
  43.6 10.2 %attention.2.refs_1_ = bf16[256,1024]{1,0:T(8,128)(2,1)} custom-call(s32[1]{0:T(128)} %bitcast.5.refs_0_, s32[16]{0:T(128)} %refs_1_.5, bf16[256,3072]{1,0:T(8,128)(2,1)} %refs_2_.3, bf16[256,576]{1,0:T(8,128)(2,1)} %copy.15.refs_3_, bf16[16,9216]{1,0:T(8,128)(2,1)} %copy-done.16, bf16[16,9216]{1,0:T(8,128)(2,1)} %copy-done.18, bf16[16,9216]{1,0:T(8,128)(2,1)} %copy-done.17, ...), custom_call_target="tpu_custom_call" | custom-call | flops 8999999488 | bytes 4194304 | tf_op jit(solution)/shard_map/attention/pallas_call | solution.py:107
  55.1 1.6 %collective-permute-start.16 = (bf16[128,2048]{1,0:T(8,128)(2,1)S(1)}, bf16[128,2048]{1,0:T(8,128)(2,1)}, u32[]{:S(2)}, u32[]{:S(2)}) collective-permute-start(bf16[128,2048]{1,0:T(8,128)(2,1)S(1)} %constant_dynamic-slice_fusion), channel_id=1, source_target_pairs={{0,8},{4,12},{8,0},{12,4},{1,9},{5,13},{9,1},{13,5},{2,10},{6,14},... | collective-permute-start | bytes 1572872 | tf_op jit(solution)/shard_map/ppermute | solution.py:351
  58.2 10.2 %attention.3.refs_2_ = bf16[256,1024]{1,0:T(8,128)(2,1)} custom-call(s32[1]{0:T(128)} %bitcast.5.refs_0_, s32[16]{0:T(128)} %refs_1_.5, bf16[256,3072]{1,0:T(8,128)(2,1)} %refs_2_.3, bf16[256,576]{1,0:T(8,128)(2,1)} %copy.15.refs_3_, bf16[16,9216]{1,0:T(8,128)(2,1)} %copy-done.16, bf16[16,9216]{1,0:T(8,128)(2,1)} %copy-done.18, bf16[16,9216]{1,0:T(8,128)(2,1)} %copy-done.17, ...), custom_call_target="tpu_custom_call" | custom-call | flops 8999999488 | bytes 4194304 | tf_op jit(solution)/shard_map/attention/pallas_call | solution.py:107
  69.2 1.7 %collective-permute-done.3.refs_7_ = bf16[128,2048]{1,0:T(8,128)(2,1)} collective-permute-done((bf16[128,2048]{1,0:T(8,128)(2,1)S(1)}, bf16[128,2048]{1,0:T(8,128)(2,1)}, u32[]{:S(2)}, u32[]{:S(2)}) %collective-permute-start.3) | collective-permute-done | bytes 524320 | tf_op jit(solution)/shard_map/ppermute | solution.py:354
  73.2 7.3 %project.3 = bf16[2,480,512]{2,1,0:T(8,128)(2,1)} custom-call(s32[3]{0:T(128)} %pad_add_fusion.refs_0_, bf16[256,1024]{1,0:T(8,128)(2,1)} %attention.2.refs_1_, bf16[256,1024]{1,0:T(8,128)(2,1)} %attention.3.refs_2_, bf16[256,1024]{1,0:T(8,128)(2,1)} %copy-done.10, bf16[256,1024]{1,0:T(8,128)(2,1)} %copy-done.12, bf16[1280,2048]{1,0:T(8,128)(2,1)} %refs_5_.5, ...), custom_call_target="tpu_custom_call" | custom-call | flops 5000000000 | bytes 4194304 | tf_op jit(solution)/shard_map/project/pallas_call | solution.py:193
  85.1 7.6 %project.4 = bf16[2,512,512]{2,1,0:T(8,128)(2,1)} custom-call(s32[3]{0:T(128)} %pad_add_fusion.refs_0_, bf16[256,1024]{1,0:T(8,128)(2,1)} %attention.2.refs_1_, bf16[256,1024]{1,0:T(8,128)(2,1)} %attention.3.refs_2_, bf16[256,1024]{1,0:T(8,128)(2,1)} %copy-done.10, bf16[256,1024]{1,0:T(8,128)(2,1)} %copy-done.12, bf16[1280,2048]{1,0:T(8,128)(2,1)} %refs_5_.5, ...), custom_call_target="tpu_custom_call" | custom-call | flops 5000000000 | bytes 4194304 | tf_op jit(solution)/shard_map/project/pallas_call | solution.py:193
  93.9 2.8 %collective-permute-done.14 = bf16[2,480,512]{2,1,0:T(8,128)(2,1)} collective-permute-done((bf16[2,480,512]{2,1,0:T(8,128)(2,1)}, bf16[2,480,512]{2,1,0:T(8,128)(2,1)}, u32[]{:S(2)}, u32[]{:S(2)}) %collective-permute-start.14) | collective-permute-done | bytes 983072 | tf_op jit(solution)/shard_map/ppermute | solution.py:424
  97.9 4.6 %collective-permute-start.15 = (bf16[480,512]{1,0:T(8,128)(2,1)S(1)}, bf16[480,512]{1,0:T(8,128)(2,1)}, u32[]{:S(2)}, u32[]{:S(2)}) collective-permute-start(bf16[480,512]{1,0:T(8,128)(2,1)S(1)} %fusion.12), channel_id=1, source_target_pairs={{0,2},{2,0},{5,7},{7,5},{8,10},{10,8},{13,15},{15,13},{16,18},{18,... | collective-permute-start | bytes 1474568 | tf_op jit(solution)/shard_map/ppermute | solution.py:428
  102.6 9.1 %collective-permute-done.21.refs_6_ = bf16[288,2048]{1,0:T(8,128)(2,1)} collective-permute-done((bf16[288,2048]{1,0:T(8,128)(2,1)S(1)}, bf16[288,2048]{1,0:T(8,128)(2,1)}, u32[]{:S(2)}, u32[]{:S(2)}) %collective-permute-start.21) | collective-permute-done | bytes 1179680 | tf_op jit(solution)/shard_map/ppermute | solution.py:351
  111.7 6.0 %project.5 = bf16[2,288,512]{2,1,0:T(8,128)(2,1)} custom-call(s32[3]{0:T(128)} %pad_add_fusion.refs_0_, bf16[256,1024]{1,0:T(8,128)(2,1)} %attention.2.refs_1_, bf16[256,1024]{1,0:T(8,128)(2,1)} %attention.3.refs_2_, bf16[256,1024]{1,0:T(8,128)(2,1)} %copy-done.10, bf16[256,1024]{1,0:T(8,128)(2,1)} %copy-done.12, bf16[1280,2048]{1,0:T(8,128)(2,1)} %refs_5_.5, ...), custom_call_target="tpu_custom_call" | custom-call | flops 5000000000 | bytes 4194304 | tf_op jit(solution)/shard_map/project/pallas_call | solution.py:193
  119.3 4.6 %collective-permute-start.19 = (bf16[512,512]{1,0:T(8,128)(2,1)S(1)}, bf16[512,512]{1,0:T(8,128)(2,1)S(1)}, u32[]{:S(2)}, u32[]{:S(2)}) collective-permute-start(bf16[512,512]{1,0:T(8,128)(2,1)S(1)} %fusion.10), channel_id=1, source_target_pairs={{0,2},{2,0},{5,7},{7,5},{8,10},{10,8},{13,15},{15,13},{16,18},{18,... | collective-permute-start | bytes 1572872 | tf_op jit(solution)/shard_map/ppermute | solution.py:428
  125.3 10.1 %collective-permute-done.22 = bf16[2,288,512]{2,1,0:T(8,128)(2,1)S(1)} collective-permute-done((bf16[2,288,512]{2,1,0:T(8,128)(2,1)}, bf16[2,288,512]{2,1,0:T(8,128)(2,1)S(1)}, u32[]{:S(2)}, u32[]{:S(2)}) %collective-permute-start.22) | collective-permute-done | bytes 589856 | tf_op jit(solution)/shard_map/ppermute | solution.py:424
  135.5 1.9 %collective-permute-start.23 = (bf16[288,512]{1,0:T(8,128)(2,1)S(1)}, bf16[288,512]{1,0:T(8,128)(2,1)S(1)}, u32[]{:S(2)}, u32[]{:S(2)}) collective-permute-start(bf16[288,512]{1,0:T(8,128)(2,1)S(1)} %fusion.13), channel_id=1, source_target_pairs={{0,2},{2,0},{5,7},{7,5},{8,10},{10,8},{13,15},{15,13},{16,18},{18,... | collective-permute-start | bytes 884744 | tf_op jit(solution)/shard_map/ppermute | solution.py:428
  139.8 5.2 %collective-permute-done.23 = bf16[288,512]{1,0:T(8,128)(2,1)S(1)} collective-permute-done((bf16[288,512]{1,0:T(8,128)(2,1)S(1)}, bf16[288,512]{1,0:T(8,128)(2,1)S(1)}, u32[]{:S(2)}, u32[]{:S(2)}) %collective-permute-start.23) | collective-permute-done | bytes 294944 | tf_op jit(solution)/shard_map/ppermute | solution.py:428
  149.0 2.6 %finish.1 = bf16[256,1280]{1,0:T(8,128)(2,1)} custom-call(s32[3]{0:T(128)} %pad_add_fusion.refs_0_, bf16[992,256]{1,0:T(8,128)(2,1)} %get-tuple-element.42.refs_1_, bf16[992,256]{1,0:T(8,128)(2,1)} %copy-done.4, bf16[288,256]{1,0:T(8,128)(2,1)} %get-tuple-element.44.refs_3_, bf16[288,256]{1,0:T(8,128)(2,1)} %copy-done.6), custom_call_target="tpu_custom_call" | custom-call | flops 1024 | bytes 1024 | tf_op jit(solution)/shard_map/finish/pallas_call | solution.py:232
  (100 shorter events, 35.5 us)
Async XLA Ops:
  2.8 10.1 %collective-permute-start = (bf16[8,9216]{1,0:T(8,128)(2,1)}, bf16[8,9216]{1,0:T(8,128)(2,1)S(1)}, u32[]{:S(2)}, u32[]{:S(2)}) collective-permute-start(bf16[8,9216]{1,0:T(8,128)(2,1)} %get-tuple-element.23), channel_id=1, source_target_pairs={{0,4},{4,0},{8,12},{12,8},{1,5},{5,1},{9,13},{13,9},{2,6},{6,2},{1... | collective-permute-start | bytes 442376 | tf_op jit(solution)/shard_map/ppermute | solution.py:361
  3.2 11.1 %collective-permute-start.5 = (bf16[8,9216]{1,0:T(8,128)(2,1)}, bf16[8,9216]{1,0:T(8,128)(2,1)S(1)}, u32[]{:S(2)}, u32[]{:S(2)}) collective-permute-start(bf16[8,9216]{1,0:T(8,128)(2,1)} %get-tuple-element.28), channel_id=1, source_target_pairs={{0,8},{4,12},{8,0},{12,4},{1,9},{5,13},{9,1},{13,5},{2,10},{6,14},... | collective-permute-start | bytes 442376 | tf_op jit(solution)/shard_map/ppermute | solution.py:361
  5.8 8.6 %collective-permute-start.6 = (bf16[8,9216]{1,0:T(8,128)(2,1)}, bf16[8,9216]{1,0:T(8,128)(2,1)S(1)}, u32[]{:S(2)}, u32[]{:S(2)}) collective-permute-start(bf16[8,9216]{1,0:T(8,128)(2,1)} %get-tuple-element.29), channel_id=1, source_target_pairs={{0,12},{4,8},{8,4},{12,0},{1,13},{5,9},{9,5},{13,1},{2,14},{6,10},... | collective-permute-start | bytes 442376 | tf_op jit(solution)/shard_map/ppermute | solution.py:361
  6.9 15.4 %collective-permute-start.4 = (bf16[96,2048]{1,0:T(8,128)(2,1)S(1)}, bf16[96,2048]{1,0:T(8,128)(2,1)S(1)}, u32[]{:S(2)}, u32[]{:S(2)}) collective-permute-start(bf16[96,2048]{1,0:T(8,128)(2,1)S(1)} %constant_dynamic-slice_fusion.2), channel_id=1, source_target_pairs={{0,8},{4,12},{8,0},{12,4},{1,9},{5,13},{9,1},{13,5},{2,10},{6,14},... | collective-permute-start | bytes 1179656 | tf_op jit(solution)/shard_map/ppermute | solution.py:351
  14.0 20.7 %collective-permute-start.1 = (bf16[144,2048]{1,0:T(8,128)(2,1)S(1)}, bf16[144,2048]{1,0:T(8,128)(2,1)S(1)}, u32[]{:S(2)}, u32[]{:S(2)}) collective-permute-start(bf16[144,2048]{1,0:T(8,128)(2,1)S(1)} %constant_dynamic-slice_fusion.4), channel_id=1, source_target_pairs={{0,8},{4,12},{8,0},{12,4},{1,9},{5,13},{9,1},{13,5},{2,10},{6,14},... | collective-permute-start | bytes 1769480 | tf_op jit(solution)/shard_map/ppermute | solution.py:351
  14.7 16.2 %collective-permute-start.7 = (bf16[16,9216]{1,0:T(8,128)(2,1)S(1)}, bf16[16,9216]{1,0:T(8,128)(2,1)S(1)}, u32[]{:S(2)}, u32[]{:S(2)}) collective-permute-start(bf16[16,9216]{1,0:T(8,128)(2,1)S(1)} %convolution_convert_fusion.refs_4_), channel_id=1, source_target_pairs={{0,2},{1,3},{2,0},{3,1},{4,6},{5,7},{6,4},{7,5},{8,10},{9,11},{10,... | collective-permute-start | bytes 884744 | tf_op jit(solution)/shard_map/ppermute | solution.py:357
  17.6 14.9 %collective-permute-start.9 = (bf16[16,9216]{1,0:T(8,128)(2,1)S(1)}, bf16[16,9216]{1,0:T(8,128)(2,1)S(1)}, u32[]{:S(2)}, u32[]{:S(2)}) collective-permute-start(bf16[16,9216]{1,0:T(8,128)(2,1)S(1)} %convolution_convert_fusion.refs_4_), channel_id=1, source_target_pairs={{0,1},{1,0},{2,3},{3,2},{4,5},{5,4},{6,7},{7,6},{8,9},{9,8},{10,11... | collective-permute-start | bytes 884744 | tf_op jit(solution)/shard_map/ppermute | solution.py:357
  31.0 10.6 %collective-permute-start.8 = (bf16[96,2048]{1,0:T(8,128)(2,1)S(1)}, bf16[96,2048]{1,0:T(8,128)(2,1)S(1)}, u32[]{:S(2)}, u32[]{:S(2)}) collective-permute-start(bf16[96,2048]{1,0:T(8,128)(2,1)S(1)} %collective-permute-done.4.refs_6_), channel_id=1, source_target_pairs={{0,16},{16,0},{1,17},{17,1},{2,18},{18,2},{3,19},{19,3},{4,20},{20... | collective-permute-start | bytes 1179656 | tf_op jit(solution)/shard_map/ppermute | solution.py:354
  34.7 8.9 %collective-permute-start.10 = (bf16[16,9216]{1,0:T(8,128)(2,1)S(1)}, bf16[16,9216]{1,0:T(8,128)(2,1)}, u32[]{:S(2)}, u32[]{:S(2)}) collective-permute-start(bf16[16,9216]{1,0:T(8,128)(2,1)S(1)} %collective-permute-done.7.refs_6_), channel_id=1, source_target_pairs={{0,1},{1,0},{2,3},{3,2},{4,5},{5,4},{6,7},{7,6},{8,9},{9,8},{10,11... | collective-permute-start | bytes 884744 | tf_op jit(solution)/shard_map/ppermute | solution.py:357
  38.5 15.3 %collective-permute-start.2 = (bf16[128,2048]{1,0:T(8,128)(2,1)S(1)}, bf16[128,2048]{1,0:T(8,128)(2,1)S(1)}, u32[]{:S(2)}, u32[]{:S(2)}) collective-permute-start(bf16[128,2048]{1,0:T(8,128)(2,1)S(1)} %constant_dynamic-slice_fusion.3), channel_id=1, source_target_pairs={{0,8},{4,12},{8,0},{12,4},{1,9},{5,13},{9,1},{13,5},{2,10},{6,14},... | collective-permute-start | bytes 1572872 | tf_op jit(solution)/shard_map/ppermute | solution.py:351
  40.1 18.1 %collective-permute-start.11 = (bf16[144,2048]{1,0:T(8,128)(2,1)S(1)}, bf16[144,2048]{1,0:T(8,128)(2,1)S(1)}, u32[]{:S(2)}, u32[]{:S(2)}) collective-permute-start(bf16[144,2048]{1,0:T(8,128)(2,1)S(1)} %collective-permute-done.1.refs_8_), channel_id=1, source_target_pairs={{0,16},{16,0},{1,17},{17,1},{2,18},{18,2},{3,19},{19,3},{4,20},{20... | collective-permute-start | bytes 1769480 | tf_op jit(solution)/shard_map/ppermute | solution.py:354
  53.7 14.7 %collective-permute-start.12 = (bf16[256,1024]{1,0:T(8,128)(2,1)}, bf16[256,1024]{1,0:T(8,128)(2,1)S(1)}, u32[]{:S(2)}, u32[]{:S(2)}) collective-permute-start(bf16[256,1024]{1,0:T(8,128)(2,1)} %attention.2.refs_1_), channel_id=1, source_target_pairs={{0,4},{4,0},{8,12},{12,8},{1,5},{5,1},{9,13},{13,9},{2,6},{6,2},{1... | collective-permute-start | bytes 1572872 | tf_op jit(solution)/shard_map/ppermute | solution.py:389
  55.1 15.7 %collective-permute-start.16 = (bf16[128,2048]{1,0:T(8,128)(2,1)S(1)}, bf16[128,2048]{1,0:T(8,128)(2,1)}, u32[]{:S(2)}, u32[]{:S(2)}) collective-permute-start(bf16[128,2048]{1,0:T(8,128)(2,1)S(1)} %constant_dynamic-slice_fusion), channel_id=1, source_target_pairs={{0,8},{4,12},{8,0},{12,4},{1,9},{5,13},{9,1},{13,5},{2,10},{6,14},... | collective-permute-start | bytes 1572872 | tf_op jit(solution)/shard_map/ppermute | solution.py:351
  56.7 14.1 %collective-permute-start.3 = (bf16[128,2048]{1,0:T(8,128)(2,1)S(1)}, bf16[128,2048]{1,0:T(8,128)(2,1)}, u32[]{:S(2)}, u32[]{:S(2)}) collective-permute-start(bf16[128,2048]{1,0:T(8,128)(2,1)S(1)} %collective-permute-done.2.refs_6_), channel_id=1, source_target_pairs={{0,16},{16,0},{1,17},{17,1},{2,18},{18,2},{3,19},{19,3},{4,20},{20... | collective-permute-start | bytes 1572872 | tf_op jit(solution)/shard_map/ppermute | solution.py:354
  68.5 3.9 %collective-permute-start.13 = (bf16[256,1024]{1,0:T(8,128)(2,1)}, bf16[256,1024]{1,0:T(8,128)(2,1)S(1)}, u32[]{:S(2)}, u32[]{:S(2)}) collective-permute-start(bf16[256,1024]{1,0:T(8,128)(2,1)} %attention.3.refs_2_), channel_id=1, source_target_pairs={{0,4},{4,0},{8,12},{12,8},{1,5},{5,1},{9,13},{13,9},{2,6},{6,2},{1... | collective-permute-start | bytes 1572872 | tf_op jit(solution)/shard_map/ppermute | solution.py:389
  70.9 13.4 %collective-permute-start.17 = (bf16[128,2048]{1,0:T(8,128)(2,1)}, bf16[128,2048]{1,0:T(8,128)(2,1)S(1)}, u32[]{:S(2)}, u32[]{:S(2)}) collective-permute-start(bf16[128,2048]{1,0:T(8,128)(2,1)} %collective-permute-done.16.refs_8_), channel_id=1, source_target_pairs={{0,16},{16,0},{1,17},{17,1},{2,18},{18,2},{3,19},{19,3},{4,20},{20... | collective-permute-start | bytes 1572872 | tf_op jit(solution)/shard_map/ppermute | solution.py:354
  80.5 16.3 %collective-permute-start.14 = (bf16[2,480,512]{2,1,0:T(8,128)(2,1)}, bf16[2,480,512]{2,1,0:T(8,128)(2,1)}, u32[]{:S(2)}, u32[]{:S(2)}) collective-permute-start(bf16[2,480,512]{2,1,0:T(8,128)(2,1)} %project.3), channel_id=1, source_target_pairs={{1,0},{3,2},{4,5},{6,7},{9,8},{11,10},{12,13},{14,15},{17,16},{19,... | collective-permute-start | bytes 2949128 | tf_op jit(solution)/shard_map/ppermute | solution.py:424
  83.4 28.3 %collective-permute-start.21 = (bf16[288,2048]{1,0:T(8,128)(2,1)S(1)}, bf16[288,2048]{1,0:T(8,128)(2,1)}, u32[]{:S(2)}, u32[]{:S(2)}) collective-permute-start(bf16[288,2048]{1,0:T(8,128)(2,1)S(1)} %slice.61), channel_id=1, source_target_pairs={{0,8},{4,12},{8,0},{12,4},{1,9},{5,13},{9,1},{13,5},{2,10},{6,14},... | collective-permute-start | bytes 3538952 | tf_op jit(solution)/shard_map/ppermute | solution.py:351
  92.6 26.5 %collective-permute-start.18 = (bf16[2,512,512]{2,1,0:T(8,128)(2,1)}, bf16[2,512,512]{2,1,0:T(8,128)(2,1)S(1)}, u32[]{:S(2)}, u32[]{:S(2)}) collective-permute-start(bf16[2,512,512]{2,1,0:T(8,128)(2,1)} %project.4), channel_id=1, source_target_pairs={{1,0},{3,2},{4,5},{6,7},{9,8},{11,10},{12,13},{14,15},{17,16},{19,... | collective-permute-start | bytes 3145736 | tf_op jit(solution)/shard_map/ppermute | solution.py:424
  97.9 21.2 %collective-permute-start.15 = (bf16[480,512]{1,0:T(8,128)(2,1)S(1)}, bf16[480,512]{1,0:T(8,128)(2,1)}, u32[]{:S(2)}, u32[]{:S(2)}) collective-permute-start(bf16[480,512]{1,0:T(8,128)(2,1)S(1)} %fusion.12), channel_id=1, source_target_pairs={{0,2},{2,0},{5,7},{7,5},{8,10},{10,8},{13,15},{15,13},{16,18},{18,... | collective-permute-start | bytes 1474568 | tf_op jit(solution)/shard_map/ppermute | solution.py:428
  117.7 17.7 %collective-permute-start.22 = (bf16[2,288,512]{2,1,0:T(8,128)(2,1)}, bf16[2,288,512]{2,1,0:T(8,128)(2,1)S(1)}, u32[]{:S(2)}, u32[]{:S(2)}) collective-permute-start(bf16[2,288,512]{2,1,0:T(8,128)(2,1)} %project.5), channel_id=1, source_target_pairs={{1,0},{3,2},{4,5},{6,7},{9,8},{11,10},{12,13},{14,15},{17,16},{19,... | collective-permute-start | bytes 1769480 | tf_op jit(solution)/shard_map/ppermute | solution.py:424
  119.3 18.1 %collective-permute-start.19 = (bf16[512,512]{1,0:T(8,128)(2,1)S(1)}, bf16[512,512]{1,0:T(8,128)(2,1)S(1)}, u32[]{:S(2)}, u32[]{:S(2)}) collective-permute-start(bf16[512,512]{1,0:T(8,128)(2,1)S(1)} %fusion.10), channel_id=1, source_target_pairs={{0,2},{2,0},{5,7},{7,5},{8,10},{10,8},{13,15},{15,13},{16,18},{18,... | collective-permute-start | bytes 1572872 | tf_op jit(solution)/shard_map/ppermute | solution.py:428
  135.5 9.5 %collective-permute-start.23 = (bf16[288,512]{1,0:T(8,128)(2,1)S(1)}, bf16[288,512]{1,0:T(8,128)(2,1)S(1)}, u32[]{:S(2)}, u32[]{:S(2)}) collective-permute-start(bf16[288,512]{1,0:T(8,128)(2,1)S(1)} %fusion.13), channel_id=1, source_target_pairs={{0,2},{2,0},{5,7},{7,5},{8,10},{10,8},{13,15},{15,13},{16,18},{18,... | collective-permute-start | bytes 884744 | tf_op jit(solution)/shard_map/ppermute | solution.py:428
  138.5 9.6 %collective-permute-start.20 = (bf16[992,256]{1,0:T(8,128)(2,1)S(1)}, bf16[992,256]{1,0:T(8,128)(2,1)S(1)}, u32[]{:S(2)}, u32[]{:S(2)}) collective-permute-start(bf16[992,256]{1,0:T(8,128)(2,1)S(1)} %get-tuple-element.41), channel_id=1, source_target_pairs={{0,4},{2,6},{5,1},{7,3},{8,12},{10,14},{13,9},{15,11},{16,20},{18,... | collective-permute-start | bytes 1523720 | tf_op jit(solution)/shard_map/ppermute | solution.py:436
  (21 other events, 233.9 us)

commit v3 on v2

--- a/solution.py
+++ b/solution.py
@@ -17,9 +17,11 @@
 QKD = 192
 ROPE = LAT - KVR
 MASKED = -1e30
-PIECES = (192, 288, 256, 256, 288)
-STEPS = (2, 2, 1)
+PIECES = (448, 416, 224, 192)
+STEPS = (1, 1, 1, 1)
+WHOLE = 2
 VMEM_BYTES = 60 * 1024 * 1024
+LESS_VMEM_BYTES = 20 * 1024 * 1024
 SMALL_COST = pl.CostEstimate(flops=1024, bytes_accessed=1024, transcendentals=0)
 BF16 = jnp.bfloat16
 F32 = jnp.float32
@@ -144,18 +146,16 @@
     return [[refs.pop(0) for _ in range(count)] for count in counts]
 
 
-def project_kernel(route_ref, *refs, start, rows, pair_counts):
-    halves, weight_hbm, refs = refs[:4], refs[4], refs[5:]
+def project_kernel(route_ref, *refs, rows, pair_counts):
+    own, beside, weight_hbm, refs = refs[0], refs[1], refs[2], refs[3:]
     pieces = refs[:-5]
     out_ref, attended, weights, totals, sems = refs[-5:]
     turn, group = route_ref[0], route_ref[1]
-    tokens, width = halves[0].shape
+    tokens = own.shape[0]
     copies = [
-        (halves[0], attended.at[:tokens, :width]),
-        (halves[1], attended.at[:tokens, width:]),
-        (weight_hbm.at[pl.ds(start, rows)], weights.at[0]),
-        (halves[2], attended.at[tokens:, :width]),
-        (halves[3], attended.at[tokens:, width:]),
+        (own, attended.at[:tokens]),
+        (weight_hbm, weights.at[0]),
+        (beside, attended.at[tokens:]),
     ]
     place = 0
     for pair in refs_by_piece(pieces, pair_counts):
@@ -169,8 +169,8 @@
         pltpu.make_async_copy(source, target, sems.at[index])
         for index, (source, target) in enumerate(copies)
     ]
-    last = tuple(range(5, len(copies)))
-    needs = ((0, 0, (0, 1, 2), (3, 4) + last), (0, 1, (3, 4), ()), (1, 0, last, ()), (1, 1, (), ()))
+    last = tuple(range(3, len(copies)))
+    needs = ((0, 0, (0, 1), (2,) + last), (0, 1, (2,), ()), (1, 0, last, ()), (1, 1, (), ()))
     for index in needs[0][2]:
         copies[index].start()
     for unit, request, awaited, following in needs:
@@ -186,29 +186,30 @@
         out_ref[slot] = totals[slot].astype(BF16)
 
 
-def project(route, halves, weight, pieces, start, rows):
-    tokens, width = halves[0].shape[0], weight.shape[1]
+def project(route, own, beside, weight, pieces):
+    tokens, width = own.shape
+    rows = weight.shape[0]
     flat = [piece for pair in pieces for piece in pair]
     hbm = pl.BlockSpec(memory_space=pl.ANY)
     return pl.pallas_call(
         lambda *refs: project_kernel(
-            *refs, start=start, rows=rows, pair_counts=[len(pair) for pair in pieces]
+            *refs, rows=rows, pair_counts=[len(pair) for pair in pieces]
         ),
-        in_specs=[pl.BlockSpec(memory_space=pltpu.SMEM)] + [hbm] * (5 + len(flat)),
+        in_specs=[pl.BlockSpec(memory_space=pltpu.SMEM)] + [hbm] * (3 + len(flat)),
         out_specs=pl.BlockSpec(memory_space=pltpu.VMEM),
         out_shape=jax.ShapeDtypeStruct((2, rows, 2 * tokens), BF16),
         scratch_shapes=[
             pltpu.VMEM((2 * tokens, width), BF16),
             pltpu.VMEM((2, rows, width), BF16),
             pltpu.VMEM((2, rows, 2 * tokens), F32),
-            pltpu.SemaphoreType.DMA((5 + len(flat),)),
+            pltpu.SemaphoreType.DMA((3 + len(flat),)),
         ],
-        compiler_params=pltpu.CompilerParams(vmem_limit_bytes=VMEM_BYTES),
+        compiler_params=pltpu.CompilerParams(vmem_limit_bytes=LESS_VMEM_BYTES),
         cost_estimate=pl.CostEstimate(
-            flops=5_000_000_000, bytes_accessed=4 * 1024 * 1024, transcendentals=0
+            flops=2_000_000_000, bytes_accessed=4 * 1024 * 1024, transcendentals=0
         ),
         name="project",
-    )(route, *halves, weight, *flat)
+    )(route, own, beside, weight, *flat)
 
 
 def finish_kernel(route_ref, *refs, starts, sizes):
@@ -234,7 +235,7 @@
         in_specs=[pl.BlockSpec(memory_space=pltpu.SMEM)] + [vmem] * len(sums),
         out_specs=vmem,
         out_shape=jax.ShapeDtypeStruct((tokens, sum(sizes)), BF16),
-        compiler_params=pltpu.CompilerParams(vmem_limit_bytes=VMEM_BYTES),
+        compiler_params=pltpu.CompilerParams(vmem_limit_bytes=LESS_VMEM_BYTES),
         cost_estimate=SMALL_COST,
         name="finish",
     )(route, *sums)
@@ -340,15 +341,16 @@
     sizes = PIECES
     starts = [sum(sizes[:index]) for index in range(len(sizes))]
 
-    def over_y(chunk, *earlier):
+    def cut(chunk, *earlier):
         size = sizes[chunk]
         weights = after(out_weight, *earlier)
-        if chunk == len(sizes) - 1:
-            piece = lax.slice_in_dim(weights, starts[chunk], starts[chunk] + size, axis=0)
-        else:
-            half = size // 2
-            piece = lax.dynamic_slice_in_dim(weights, starts[chunk] + own_group * half, half, 0)
-        return lax.ppermute(piece, "req", flip(req_count, 2))
+        if chunk >= WHOLE:
+            return lax.slice_in_dim(weights, starts[chunk], starts[chunk] + size, axis=0)
+        half = size // 2
+        return lax.dynamic_slice_in_dim(weights, starts[chunk] + own_group * half, half, 0)
+
+    def over_y(piece, *earlier):
+        return lax.ppermute(after(piece, *earlier), "req", flip(req_count, 2))
 
     def over_x(piece, *earlier):
         return lax.ppermute(after(piece, *earlier), "groups", flip(groups, 1))
@@ -360,44 +362,41 @@
     incoming = [outgoing[0]] + [
         lax.ppermute(outgoing[bit], "req", flip(req_count, bit)) for bit in (1, 2, 3)
     ]
-    y0 = over_y(0, *outgoing)
-    y1 = over_y(1, incoming[1])
+    y0 = over_y(cut(0, *outgoing))
+    cuts = [cut(chunk, incoming[1]) for chunk in range(1, len(sizes))]
+    owned = [
+        cuts[chunk - 1]
+        if chunk >= WHOLE
+        else lax.slice_in_dim(
+            after(out_weight, incoming[1]), starts[chunk], starts[chunk] + sizes[chunk], axis=0
+        )
+        for chunk in range(len(sizes))
+    ]
+    core = own_req & 1
+    keeper = (own_head & 1) == core
+    route = jnp.stack([(own_head >> 1) ^ (own_req >> 1), own_group, keeper]).astype(jnp.int32)
     prefix = jnp.dot(
-        picks, jnp.concatenate(incoming, axis=0), preferred_element_type=F32
+        after(picks, route), jnp.concatenate(incoming, axis=0), preferred_element_type=F32
     ).astype(BF16)
     far = over_z(prefix, 2)
     near = over_z(prefix, 1)
-    farther = over_z(after(far, near, y1), 1)
+    farther = over_z(after(far, near, *cuts, *owned), 1)
     x0 = over_x(y0, far)
-    x1 = over_x(y1)
-    y2 = over_y(2, y1)
-
-    def attend(part, *earlier):
-        return attention(
-            blocks,
-            head_mask,
-            after(stretch_query, *earlier),
-            stretch_latent,
-            [prefix, near, far, farther],
-            up_key,
-            up_value,
-            part,
-            2,
-        )
-
-    def over_core(piece):
-        return lax.ppermute(piece, "req", flip(req_count, 1))
-
-    first = attend(0, x0)
-    second = attend(1, first, x1, y2)
-    beside = over_core(first)
-    x2 = over_x(y2)
-    y3 = over_y(3, y2)
-    halves = (first, second, beside, over_core(after(second, beside)))
-
-    core = own_req & 1
-    keeper = (own_head & 1) == core
-    route = jnp.stack([(own_head >> 1) ^ (own_req >> 1), own_group, keeper]).astype(jnp.int32)
+    y1 = over_y(cuts[0], far)
+    attended = attention(
+        blocks,
+        head_mask,
+        stretch_query,
+        stretch_latent,
+        [prefix, near, far, farther],
+        up_key,
+        up_value,
+    )
+    beside = lax.ppermute(after(attended, x0, y1), "req", flip(req_count, 1))
+    x1 = over_x(y1, attended)
+    y2 = over_y(cuts[1], attended)
+    y3 = over_y(cuts[2], attended)
+
     devices = [(req, head) for req in range(req_count) for head in range(head_count)]
 
     def place(req, head):
@@ -420,12 +419,14 @@
     ]
 
     def send(chunk, pieces, *earlier):
-        sums = project(after(route, *earlier), halves, out_weight, pieces, *spans[chunk])
+        sums = project(after(route, *earlier), attended, beside, owned[chunk], pieces)
         return sums, lax.ppermute(sums, axes, to_keeper)
 
     def halve(sums, received):
-        total = (sums[1].astype(F32) + received[1].astype(F32)).astype(BF16)
-        return total, lax.ppermute(total, axes, to_far)
+        return (sums[1].astype(F32) + received[1].astype(F32)).astype(BF16)
+
+    def pass_on(total):
+        return lax.ppermute(total, axes, to_far)
 
     def settle(sums, received, passed):
         total = sums[0].astype(F32) + received[0].astype(F32) + passed.astype(F32)
@@ -435,17 +436,27 @@
         own, other = total[:, :STRETCH], total[:, STRETCH:]
         return [own, lax.ppermute(other, axes, to_core)]
 
-    sums0, got0 = send(0, [(y0, x0), (y1, x1)], x2)
-    x3 = over_x(y3)
-    y4 = over_y(4, y3)
-    total0, passed0 = halve(sums0, got0)
-    sums1, got1 = send(1, [(y2, x2), (y3, x3)], sums0)
-    sums2, got2 = send(2, [(y4,)], sums1, total0)
-    total1, passed1 = halve(sums1, after(got1, passed0))
-    total2, passed2 = halve(sums2, got2)
-    early = [settle(sums0, got0, passed0), settle(sums1, got1, passed1)]
-    settled = split(jnp.concatenate(early, axis=0)) + split(settle(sums2, got2, passed2))
-    return finish(route, settled, (0, spans[2][0]), spans[2])
+    sums0, got0 = send(0, [(y0, x0)])
+    total0 = halve(sums0, got0)
+    middle = sizes[0] // 2
+    passed0 = [pass_on(total0[:middle]), pass_on(total0[middle:])]
+    sums1, got1 = send(1, [(y1, x1)], sums0, y2)
+    sums2, got2 = send(2, [(y2,)], sums1, total0)
+    sums3, got3 = send(3, [(y3,)], sums2, passed0[0])
+    total1 = halve(sums1, after(got1, sums3, passed0[1]))
+    passed1 = pass_on(total1)
+    total2 = halve(sums2, after(got2, total1))
+    passed2 = pass_on(total2)
+    total3 = halve(sums3, after(got3, total2))
+    passed3 = pass_on(total3)
+    passed0 = jnp.concatenate(passed0, axis=0)
+    early = [
+        settle(sums0, got0, after(passed0, total3)),
+        settle(sums1, got1, after(passed1, total3)),
+        settle(sums2, got2, after(passed2, total3)),
+    ]
+    settled = split(jnp.concatenate(early, axis=0)) + split(settle(sums3, got3, passed3))
+    return finish(route, settled, (0, spans[3][0]), (spans[3][0], spans[3][1]))
 
 
 def solution(mesh):

time: 152 us -> 133 us (0.88)
  waiting for transfers between devices: 46.2 us -> 27.8 us
  Pallas kernels: 46.5 us -> 36.9 us
  starting transfers between devices: 39.4 us -> 46.2 us
  local copies, waits for them, and re-layouts: 11.6 us -> 16.7 us
  other arithmetic: 4.63 us -> 1.22 us
    ppermute x10, starting transfers between devices: 17.2 us -> 27.6 us  [the longest x5 23.1 us: pass_on(): return lax.ppermute(total, axes, to_far)]
    ppermute x3 -> x4, waiting for transfers between devices: 13 us -> 4.37 us  [send(): return (sums, lax.ppermute(sums, axes, to_keeper))]
    slice x1 -> x5, local copies, waits for them, and re-layouts: 1.39 us -> 7.52 us  [the longest x2 4.3 us: cut(): lax.slice_in_dim(weights, starts[chunk], starts[chunk] + size, axis=0)]
    pallas_call x3 -> x4, Pallas kernels: 20.8 us -> 15.4 us  [project(): pl.pallas_call(lambda *refs: project_kernel(*refs, rows=rows, pair_counts...]
    ppermute x3, waiting for transfers between devices: 10.7 us -> 5.78 us  [over_z(): return lax.ppermute(piece, 'head', flip(head_count, bit))]
    ppermute x10, waiting for transfers between devices: 19.6 us -> 15.9 us  [the longest x4 12.9 us: over_y(): return lax.ppermute(after(piece, *earlier), 'req', flip(req_count, 2))]
    pallas_call x2 -> x1, Pallas kernels: 20.4 us -> 17 us  [attention(): pl.pallas_call(lambda *refs: attention_kernel(*refs, together=together, s...]
    ppermute x4 -> x2, starting transfers between devices: 6.03 us -> 2.98 us  [over_x(): return lax.ppermute(after(piece, *earlier), 'groups', flip(groups, 1))]
  transfers between devices with their start and end apart: 25 -> 24, of which waited for: 11 -> 12; matrix products, arithmetic and copies ran while one was open for 9% -> 13% of each run, Pallas kernels for 27% -> 24%
where the time goes in v3:
time: 133 us
  starting transfers between devices  46.2 us (35%)
  Pallas kernels  36.9 us (28%)
  waiting for transfers between devices  27.8 us (21%)
  local copies, waits for them, and re-layouts  16.7 us (13%)
  between operations  2.84 us (2%)
    ppermute x5, starting transfers between devices, pass_on(): return lax.ppermute(total, axes, to_far)  23.1 us
    pallas_call x1, Pallas kernels, attention(): pl.pallas_call(lambda *refs: attention_kernel(*refs, together=together, s...  17 us
    pallas_call x4, Pallas kernels, project(): pl.pallas_call(lambda *refs: project_kernel(*refs, rows=rows, pair_counts...  15.4 us
    ppermute x4, waiting for transfers between devices, over_y(): return lax.ppermute(after(piece, *earlier), 'req', flip(req_count, 2))  12.9 us
    ppermute x3, waiting for transfers between devices, over_z(): return lax.ppermute(piece, 'head', flip(head_count, bit))  5.78 us
    ppermute x4, starting transfers between devices, send(): return (sums, lax.ppermute(sums, axes, to_keeper))  5.3 us
    ppermute x3, starting transfers between devices, over_z(): return lax.ppermute(piece, 'head', flip(head_count, bit))  4.6 us
    ppermute x4, starting transfers between devices, over_y(): return lax.ppermute(after(piece, *earlier), 'req', flip(req_count, 2))  4.47 us
  transfers between devices with their start and end apart: 24, of which 12 were waited for; matrix products, arithmetic and copies ran while one was open for 13% of the time, Pallas kernels for 24%

profile of v3, /device:TPU:0, one launch (start us, length us, event | category | flops | bytes accessed | tf_op | source)
XLA Modules:
  0.0 132.6 jit_solution(9316317442118249032)
XLA Ops:
  0.0 2.8 %pick.1 = (bf16[8,9216]{1,0:T(8,128)(2,1)}, bf16[8,9216]{1,0:T(8,128)(2,1)}, bf16[8,9216]{1,0:T(8,128)(2,1)}, bf16[8,9216]{1,0:T(8,128)(2,1)}) custom-call(s32[1]{0:T(128)} %bitcast.8.refs_0_, s32[4,16]{1,0:T(4,128)} %refs_1_.2, s32[4,16]{1,0:T(4,128)} %refs_2_.2, s32[4]{0:T(128)} %refs_3_.2, bf16[64,9216]{1,0:T(8,128)(2,1)} %refs_4_.1), custom_call_target="tpu_custom_call" | custom-call | flops 1024 | bytes 1024 | tf_op jit(solution)/shard_map/pick/pallas_call | solution.py:279
  2.8 2.4 %collective-permute-start.2 = (bf16[8,9216]{1,0:T(8,128)(2,1)}, bf16[8,9216]{1,0:T(8,128)(2,1)S(1)}, u32[]{:S(2)}, u32[]{:S(2)}) collective-permute-start(bf16[8,9216]{1,0:T(8,128)(2,1)} %get-tuple-element.32), channel_id=1, source_target_pairs={{0,12},{4,8},{8,4},{12,0},{1,13},{5,9},{9,5},{13,1},{2,14},{6,10},... | collective-permute-start | bytes 442376 | tf_op jit(solution)/shard_map/ppermute | solution.py:363
  5.8 2.2 %constant_dynamic-slice_fusion = bf16[224,2048]{1,0:T(8,128)(2,1)} fusion(bf16[1280,2048]{1,0:T(8,128)(2,1)} %param.19, s32[]{:T(128)S(6)} %select_n.21), kind=kLoop, calls=%fused_computation.32 | loop fusion | bytes 1835012 | tf_op jit(solution)/shard_map/dynamic_slice | solution.py:350
  16.8 2.6 %collective-permute-start.4 = (bf16[16,9216]{1,0:T(8,128)(2,1)}, bf16[16,9216]{1,0:T(8,128)(2,1)}, u32[]{:S(2)}, u32[]{:S(2)}) collective-permute-start(bf16[16,9216]{1,0:T(8,128)(2,1)} %convolution_convert_fusion.refs_4_), channel_id=1, source_target_pairs={{0,2},{1,3},{2,0},{3,1},{4,6},{5,7},{6,4},{7,5},{8,10},{9,11},{10,... | collective-permute-start | bytes 884744 | tf_op jit(solution)/shard_map/ppermute | solution.py:359
  19.4 2.2 %slice.84.refs_3_ = bf16[224,2048]{1,0:T(8,128)(2,1)} slice(bf16[1280,2048]{1,0:T(8,128)(2,1)} %param.19), slice={[864:1088], [0:2048]} | slice | bytes 1835008 | tf_op jit(solution)/shard_map/slice | solution.py:348
  21.6 2.1 %slice.85.refs_3_ = bf16[192,2048]{1,0:T(8,128)(2,1)} slice(bf16[1280,2048]{1,0:T(8,128)(2,1)} %param.19), slice={[1088:1280], [0:2048]} | slice | bytes 1572864 | tf_op jit(solution)/shard_map/slice | solution.py:348
  26.9 2.2 %constant_dynamic-slice_fusion.1 = bf16[208,2048]{1,0:T(8,128)(2,1)} fusion(bf16[1280,2048]{1,0:T(8,128)(2,1)} %param.19, s32[]{:T(128)S(6)} %select_n.20), kind=kLoop, calls=%fused_computation.33 | loop fusion | bytes 1703940 | tf_op jit(solution)/shard_map/dynamic_slice | solution.py:350
  30.5 2.4 %collective-permute-done.4.refs_6_ = bf16[16,9216]{1,0:T(8,128)(2,1)} collective-permute-done((bf16[16,9216]{1,0:T(8,128)(2,1)}, bf16[16,9216]{1,0:T(8,128)(2,1)}, u32[]{:S(2)}, u32[]{:S(2)}) %collective-permute-start.4) | collective-permute-done | bytes 294944 | tf_op jit(solution)/shard_map/ppermute | solution.py:359
  33.3 1.9 %copy.14.refs_3_ = bf16[256,576]{1,0:T(8,128)(2,1)} copy(bf16[256,576]{0,1:T(8,128)(2,1)} %param.11) | data formatting | bytes 589824 | tf_op args[1]
  37.9 2.0 %collective-permute-done.5.refs_7_ = bf16[16,9216]{1,0:T(8,128)(2,1)} collective-permute-done((bf16[16,9216]{1,0:T(8,128)(2,1)}, bf16[16,9216]{1,0:T(8,128)(2,1)}, u32[]{:S(2)}, u32[]{:S(2)}) %collective-permute-start.5) | collective-permute-done | bytes 294944 | tf_op jit(solution)/shard_map/ppermute | solution.py:359
  39.9 17.0 %attention.1.refs_1_ = bf16[256,2048]{1,0:T(8,128)(2,1)} custom-call(s32[1]{0:T(128)} %bitcast.4.refs_0_, s32[16]{0:T(128)} %refs_1_.3, bf16[256,3072]{1,0:T(8,128)(2,1)} %refs_2_.3, bf16[256,576]{1,0:T(8,128)(2,1)} %copy.14.refs_3_, bf16[16,9216]{1,0:T(8,128)(2,1)} %convolution_convert_fusion.refs_4_, bf16[16,9216]{1,0:T(8,128)(2,1)} %collective-permute-done.3.refs_5_, ...), custom_call_target="tpu_custom_call" | custom-call | flops 17999998976 | bytes 4194304 | tf_op jit(solution)/shard_map/attention/pallas_call | solution.py:109
  61.8 4.3 %project.4 = bf16[2,448,512]{2,1,0:T(8,128)(2,1)S(1)} custom-call(s32[3]{0:T(128)S(1)} %pad_add_fusion.refs_0_, bf16[256,2048]{1,0:T(8,128)(2,1)S(1)} %copy-done.2, bf16[256,2048]{1,0:T(8,128)(2,1)S(1)} %collective-permute-done.9.refs_2_, bf16[448,2048]{1,0:T(8,128)(2,1)S(1)} %slice.86.refs_3_, bf16[224,2048]{1,0:T(8,128)(2,1)} %collective-permute-done.6.refs_4_, ...), custom_call_target="tpu_custom_call" | custom-call | flops 2000000000 | bytes 4194304 | tf_op jit(solution)/shard_map/project/pallas_call | solution.py:194
  68.1 12.9 %collective-permute-done.13.refs_4_ = bf16[224,2048]{1,0:T(8,128)(2,1)S(1)} collective-permute-done((bf16[224,2048]{1,0:T(8,128)(2,1)}, bf16[224,2048]{1,0:T(8,128)(2,1)S(1)}, u32[]{:S(2)}, u32[]{:S(2)}) %collective-permute-start.13) | collective-permute-done | bytes 917536 | tf_op jit(solution)/shard_map/ppermute | solution.py:353
  81.0 4.4 %project.5 = bf16[2,416,512]{2,1,0:T(8,128)(2,1)S(1)} custom-call(s32[3]{0:T(128)S(1)} %pad_add_fusion.refs_0_, bf16[256,2048]{1,0:T(8,128)(2,1)S(1)} %copy-done.2, bf16[256,2048]{1,0:T(8,128)(2,1)S(1)} %collective-permute-done.9.refs_2_, bf16[416,2048]{1,0:T(8,128)(2,1)S(1)} %slice.87.refs_3_, bf16[208,2048]{1,0:T(8,128)(2,1)} %collective-permute-done.8.refs_4_, ...), custom_call_target="tpu_custom_call" | custom-call | flops 2000000000 | bytes 4194304 | tf_op jit(solution)/shard_map/project/pallas_call | solution.py:194
  87.1 4.3 %collective-permute-start.11 = (bf16[224,512]{1,0:T(8,128)(2,1)S(1)}, bf16[224,512]{1,0:T(8,128)(2,1)S(1)}, u32[]{:S(2)}, u32[]{:S(2)}) collective-permute-start(bf16[224,512]{1,0:T(8,128)(2,1)S(1)} %get-tuple-element.54), channel_id=1, source_target_pairs={{0,2},{2,0},{5,7},{7,5},{8,10},{10,8},{13,15},{15,13},{16,18},{18,... | collective-permute-start | bytes 688136 | tf_op jit(solution)/shard_map/ppermute | solution.py:429
  91.4 2.6 %collective-permute-start.12 = (bf16[224,512]{1,0:T(8,128)(2,1)S(1)}, bf16[224,512]{1,0:T(8,128)(2,1)S(1)}, u32[]{:S(2)}, u32[]{:S(2)}) collective-permute-start(bf16[224,512]{1,0:T(8,128)(2,1)S(1)} %get-tuple-element.53), channel_id=1, source_target_pairs={{0,2},{2,0},{5,7},{7,5},{8,10},{10,8},{13,15},{15,13},{16,18},{18,... | collective-permute-start | bytes 688136 | tf_op jit(solution)/shard_map/ppermute | solution.py:429
  94.0 3.4 %project.6 = bf16[2,224,512]{2,1,0:T(8,128)(2,1)S(1)} custom-call(s32[3]{0:T(128)S(1)} %pad_add_fusion.refs_0_, bf16[256,2048]{1,0:T(8,128)(2,1)S(1)} %copy-done.3, bf16[256,2048]{1,0:T(8,128)(2,1)S(1)} %collective-permute-done.9.refs_2_, bf16[224,2048]{1,0:T(8,128)(2,1)S(1)} %copy-done, bf16[224,2048]{1,0:T(8,128)(2,1)S(1)} %collective-permute-done.13.refs_4_), custom_call_target="tpu_custom_call" | custom-call | flops 2000000000 | bytes 4194304 | tf_op jit(solution)/shard_map/project/pallas_call | solution.py:194
  98.8 3.2 %project.7 = bf16[2,192,512]{2,1,0:T(8,128)(2,1)S(1)} custom-call(s32[3]{0:T(128)S(1)} %pad_add_fusion.refs_0_, bf16[256,2048]{1,0:T(8,128)(2,1)S(1)} %copy-done.3, bf16[256,2048]{1,0:T(8,128)(2,1)S(1)} %collective-permute-done.9.refs_2_, bf16[192,2048]{1,0:T(8,128)(2,1)S(1)} %copy-done.1, bf16[192,2048]{1,0:T(8,128)(2,1)S(1)} %collective-permute-done.15.refs_4_), custom_call_target="tpu_custom_call" | custom-call | flops 2000000000 | bytes 4194304 | tf_op jit(solution)/shard_map/project/pallas_call | solution.py:194
  103.3 1.8 %collective-permute-done.18 = bf16[2,416,512]{2,1,0:T(8,128)(2,1)S(1)} collective-permute-done((bf16[2,416,512]{2,1,0:T(8,128)(2,1)S(1)}, bf16[2,416,512]{2,1,0:T(8,128)(2,1)S(1)}, u32[]{:S(2)}, u32[]{:S(2)}) %collective-permute-start.18) | collective-permute-done | bytes 852000 | tf_op jit(solution)/shard_map/ppermute | solution.py:423
  105.2 3.4 %collective-permute-start.19 = (bf16[416,512]{1,0:T(8,128)(2,1)S(1)}, bf16[416,512]{1,0:T(8,128)(2,1)S(1)}, u32[]{:S(2)}, u32[]{:S(2)}) collective-permute-start(bf16[416,512]{1,0:T(8,128)(2,1)S(1)} %fusion.10), channel_id=1, source_target_pairs={{0,2},{2,0},{5,7},{7,5},{8,10},{10,8},{13,15},{15,13},{16,18},{18,... | collective-permute-start | bytes 1277960 | tf_op jit(solution)/shard_map/ppermute | solution.py:429
  110.1 5.6 %collective-permute-start.20 = (bf16[224,512]{1,0:T(8,128)(2,1)S(1)}, bf16[224,512]{1,0:T(8,128)(2,1)S(1)}, u32[]{:S(2)}, u32[]{:S(2)}) collective-permute-start(bf16[224,512]{1,0:T(8,128)(2,1)S(1)} %fusion.12), channel_id=1, source_target_pairs={{0,2},{2,0},{5,7},{7,5},{8,10},{10,8},{13,15},{15,13},{16,18},{18,... | collective-permute-start | bytes 688136 | tf_op jit(solution)/shard_map/ppermute | solution.py:429
  116.9 7.2 %collective-permute-start.22 = (bf16[192,512]{1,0:T(8,128)(2,1)S(1)}, bf16[192,512]{1,0:T(8,128)(2,1)S(1)}, u32[]{:S(2)}, u32[]{:S(2)}) collective-permute-start(bf16[192,512]{1,0:T(8,128)(2,1)S(1)} %fusion.13), channel_id=1, source_target_pairs={{0,2},{2,0},{5,7},{7,5},{8,10},{10,8},{13,15},{15,13},{16,18},{18,... | collective-permute-start | bytes 589832 | tf_op jit(solution)/shard_map/ppermute | solution.py:429
  124.1 2.2 %collective-permute-done.20 = bf16[224,512]{1,0:T(8,128)(2,1)S(1)} collective-permute-done((bf16[224,512]{1,0:T(8,128)(2,1)S(1)}, bf16[224,512]{1,0:T(8,128)(2,1)S(1)}, u32[]{:S(2)}, u32[]{:S(2)}) %collective-permute-start.20) | collective-permute-done | bytes 229408 | tf_op jit(solution)/shard_map/ppermute | solution.py:429
  130.8 1.8 %finish.1 = bf16[256,1280]{1,0:T(8,128)(2,1)} custom-call(s32[3]{0:T(128)S(1)} %pad_add_fusion.refs_0_, bf16[1088,256]{1,0:T(8,128)(2,1)S(1)} %get-tuple-element.52.refs_1_, bf16[1088,256]{1,0:T(8,128)(2,1)S(1)} %collective-permute-done.21.refs_2_, bf16[192,256]{1,0:T(8,128)(2,1)S(1)} %get-tuple-element.56.refs_3_, ...), custom_call_target="tpu_custom_call" | custom-call | flops 1024 | bytes 1024 | tf_op jit(solution)/shard_map/finish/pallas_call | solution.py:233
  (77 shorter events, 32.9 us)
Async XLA Ops:
  2.8 11.4 %collective-permute-start.2 = (bf16[8,9216]{1,0:T(8,128)(2,1)}, bf16[8,9216]{1,0:T(8,128)(2,1)S(1)}, u32[]{:S(2)}, u32[]{:S(2)}) collective-permute-start(bf16[8,9216]{1,0:T(8,128)(2,1)} %get-tuple-element.32), channel_id=1, source_target_pairs={{0,12},{4,8},{8,4},{12,0},{1,13},{5,9},{9,5},{13,1},{2,14},{6,10},... | collective-permute-start | bytes 442376 | tf_op jit(solution)/shard_map/ppermute | solution.py:363
  5.2 9.0 %collective-permute-start.1 = (bf16[8,9216]{1,0:T(8,128)(2,1)}, bf16[8,9216]{1,0:T(8,128)(2,1)S(1)}, u32[]{:S(2)}, u32[]{:S(2)}) collective-permute-start(bf16[8,9216]{1,0:T(8,128)(2,1)} %get-tuple-element.31), channel_id=1, source_target_pairs={{0,8},{4,12},{8,0},{12,4},{1,9},{5,13},{9,1},{13,5},{2,10},{6,14},... | collective-permute-start | bytes 442376 | tf_op jit(solution)/shard_map/ppermute | solution.py:363
  5.8 8.4 %collective-permute-start = (bf16[8,9216]{1,0:T(8,128)(2,1)}, bf16[8,9216]{1,0:T(8,128)(2,1)S(1)}, u32[]{:S(2)}, u32[]{:S(2)}) collective-permute-start(bf16[8,9216]{1,0:T(8,128)(2,1)} %get-tuple-element.30), channel_id=1, source_target_pairs={{0,4},{4,0},{8,12},{12,8},{1,5},{5,1},{9,13},{13,9},{2,6},{6,2},{1... | collective-permute-start | bytes 442376 | tf_op jit(solution)/shard_map/ppermute | solution.py:363
  8.1 28.4 %collective-permute-start.6 = (bf16[224,2048]{1,0:T(8,128)(2,1)}, bf16[224,2048]{1,0:T(8,128)(2,1)}, u32[]{:S(2)}, u32[]{:S(2)}) collective-permute-start(bf16[224,2048]{1,0:T(8,128)(2,1)} %constant_dynamic-slice_fusion), channel_id=1, source_target_pairs={{0,8},{4,12},{8,0},{12,4},{1,9},{5,13},{9,1},{13,5},{2,10},{6,14},... | collective-permute-start | bytes 2752520 | tf_op jit(solution)/shard_map/ppermute | solution.py:353
  15.2 15.3 %collective-permute-start.3 = (bf16[16,9216]{1,0:T(8,128)(2,1)}, bf16[16,9216]{1,0:T(8,128)(2,1)}, u32[]{:S(2)}, u32[]{:S(2)}) collective-permute-start(bf16[16,9216]{1,0:T(8,128)(2,1)} %convolution_convert_fusion.refs_4_), channel_id=1, source_target_pairs={{0,1},{1,0},{2,3},{3,2},{4,5},{5,4},{6,7},{7,6},{8,9},{9,8},{10,11... | collective-permute-start | bytes 884744 | tf_op jit(solution)/shard_map/ppermute | solution.py:359
  16.8 16.1 %collective-permute-start.4 = (bf16[16,9216]{1,0:T(8,128)(2,1)}, bf16[16,9216]{1,0:T(8,128)(2,1)}, u32[]{:S(2)}, u32[]{:S(2)}) collective-permute-start(bf16[16,9216]{1,0:T(8,128)(2,1)} %convolution_convert_fusion.refs_4_), channel_id=1, source_target_pairs={{0,2},{1,3},{2,0},{3,1},{4,6},{5,7},{6,4},{7,5},{8,10},{9,11},{10,... | collective-permute-start | bytes 884744 | tf_op jit(solution)/shard_map/ppermute | solution.py:359
  32.9 7.0 %collective-permute-start.5 = (bf16[16,9216]{1,0:T(8,128)(2,1)}, bf16[16,9216]{1,0:T(8,128)(2,1)}, u32[]{:S(2)}, u32[]{:S(2)}) collective-permute-start(bf16[16,9216]{1,0:T(8,128)(2,1)} %collective-permute-done.4.refs_6_), channel_id=1, source_target_pairs={{0,1},{1,0},{2,3},{3,2},{4,5},{5,4},{6,7},{7,6},{8,9},{9,8},{10,11... | collective-permute-start | bytes 884744 | tf_op jit(solution)/shard_map/ppermute | solution.py:359
  35.2 21.7 %collective-permute-start.8 = (bf16[208,2048]{1,0:T(8,128)(2,1)}, bf16[208,2048]{1,0:T(8,128)(2,1)}, u32[]{:S(2)}, u32[]{:S(2)}) collective-permute-start(bf16[208,2048]{1,0:T(8,128)(2,1)} %constant_dynamic-slice_fusion.1), channel_id=1, source_target_pairs={{0,8},{4,12},{8,0},{12,4},{1,9},{5,13},{9,1},{13,5},{2,10},{6,14},... | collective-permute-start | bytes 2555912 | tf_op jit(solution)/shard_map/ppermute | solution.py:353
  36.5 21.2 %collective-permute-start.7 = (bf16[224,2048]{1,0:T(8,128)(2,1)}, bf16[224,2048]{1,0:T(8,128)(2,1)}, u32[]{:S(2)}, u32[]{:S(2)}) collective-permute-start(bf16[224,2048]{1,0:T(8,128)(2,1)} %collective-permute-done.6.refs_4_), channel_id=1, source_target_pairs={{0,16},{16,0},{1,17},{17,1},{2,18},{18,2},{3,19},{19,3},{4,20},{20... | collective-permute-start | bytes 2752520 | tf_op jit(solution)/shard_map/ppermute | solution.py:356
  57.7 2.9 %collective-permute-start.9 = (bf16[256,2048]{1,0:T(8,128)(2,1)}, bf16[256,2048]{1,0:T(8,128)(2,1)S(1)}, u32[]{:S(2)}, u32[]{:S(2)}) collective-permute-start(bf16[256,2048]{1,0:T(8,128)(2,1)} %attention.1.refs_1_), channel_id=1, source_target_pairs={{0,4},{4,0},{8,12},{12,8},{1,5},{5,1},{9,13},{13,9},{2,6},{6,2},{1... | collective-permute-start | bytes 3145736 | tf_op jit(solution)/shard_map/ppermute | solution.py:395
  57.7 23.4 %collective-permute-start.13 = (bf16[224,2048]{1,0:T(8,128)(2,1)}, bf16[224,2048]{1,0:T(8,128)(2,1)S(1)}, u32[]{:S(2)}, u32[]{:S(2)}) collective-permute-start(bf16[224,2048]{1,0:T(8,128)(2,1)} %slice.84.refs_3_), channel_id=1, source_target_pairs={{0,8},{4,12},{8,0},{12,4},{1,9},{5,13},{9,1},{13,5},{2,10},{6,14},... | collective-permute-start | bytes 2752520 | tf_op jit(solution)/shard_map/ppermute | solution.py:353
  58.4 22.6 %collective-permute-start.14 = (bf16[208,2048]{1,0:T(8,128)(2,1)}, bf16[208,2048]{1,0:T(8,128)(2,1)S(1)}, u32[]{:S(2)}, u32[]{:S(2)}) collective-permute-start(bf16[208,2048]{1,0:T(8,128)(2,1)} %collective-permute-done.8.refs_4_), channel_id=1, source_target_pairs={{0,16},{16,0},{1,17},{17,1},{2,18},{18,2},{3,19},{19,3},{4,20},{20... | collective-permute-start | bytes 2555912 | tf_op jit(solution)/shard_map/ppermute | solution.py:356
  66.1 20.8 %collective-permute-start.10 = (bf16[2,448,512]{2,1,0:T(8,128)(2,1)S(1)}, bf16[2,448,512]{2,1,0:T(8,128)(2,1)S(1)}, u32[]{:S(2)}, u32[]{:S(2)}) collective-permute-start(bf16[2,448,512]{2,1,0:T(8,128)(2,1)S(1)} %project.4), channel_id=1, source_target_pairs={{1,0},{3,2},{4,5},{6,7},{9,8},{11,10},{12,13},{14,15},{17,16},{19,... | collective-permute-start | bytes 2752520 | tf_op jit(solution)/shard_map/ppermute | solution.py:423
  67.4 31.4 %collective-permute-start.15 = (bf16[192,2048]{1,0:T(8,128)(2,1)S(1)}, bf16[192,2048]{1,0:T(8,128)(2,1)S(1)}, u32[]{:S(2)}, u32[]{:S(2)}) collective-permute-start(bf16[192,2048]{1,0:T(8,128)(2,1)S(1)} %copy-done.1), channel_id=1, source_target_pairs={{0,8},{4,12},{8,0},{12,4},{1,9},{5,13},{9,1},{13,5},{2,10},{6,14},... | collective-permute-start | bytes 2359304 | tf_op jit(solution)/shard_map/ppermute | solution.py:353
  85.5 19.6 %collective-permute-start.18 = (bf16[2,416,512]{2,1,0:T(8,128)(2,1)S(1)}, bf16[2,416,512]{2,1,0:T(8,128)(2,1)S(1)}, u32[]{:S(2)}, u32[]{:S(2)}) collective-permute-start(bf16[2,416,512]{2,1,0:T(8,128)(2,1)S(1)} %project.5), channel_id=1, source_target_pairs={{1,0},{3,2},{4,5},{6,7},{9,8},{11,10},{12,13},{14,15},{17,16},{19,... | collective-permute-start | bytes 2555912 | tf_op jit(solution)/shard_map/ppermute | solution.py:423
  87.1 11.7 %collective-permute-start.11 = (bf16[224,512]{1,0:T(8,128)(2,1)S(1)}, bf16[224,512]{1,0:T(8,128)(2,1)S(1)}, u32[]{:S(2)}, u32[]{:S(2)}) collective-permute-start(bf16[224,512]{1,0:T(8,128)(2,1)S(1)} %get-tuple-element.54), channel_id=1, source_target_pairs={{0,2},{2,0},{5,7},{7,5},{8,10},{10,8},{13,15},{15,13},{16,18},{18,... | collective-permute-start | bytes 688136 | tf_op jit(solution)/shard_map/ppermute | solution.py:429
  91.4 13.7 %collective-permute-start.12 = (bf16[224,512]{1,0:T(8,128)(2,1)S(1)}, bf16[224,512]{1,0:T(8,128)(2,1)S(1)}, u32[]{:S(2)}, u32[]{:S(2)}) collective-permute-start(bf16[224,512]{1,0:T(8,128)(2,1)S(1)} %get-tuple-element.53), channel_id=1, source_target_pairs={{0,2},{2,0},{5,7},{7,5},{8,10},{10,8},{13,15},{15,13},{16,18},{18,... | collective-permute-start | bytes 688136 | tf_op jit(solution)/shard_map/ppermute | solution.py:429
  97.5 12.6 %collective-permute-start.17 = (bf16[2,224,512]{2,1,0:T(8,128)(2,1)S(1)}, bf16[2,224,512]{2,1,0:T(8,128)(2,1)S(1)}, u32[]{:S(2)}, u32[]{:S(2)}) collective-permute-start(bf16[2,224,512]{2,1,0:T(8,128)(2,1)S(1)} %project.6), channel_id=1, source_target_pairs={{1,0},{3,2},{4,5},{6,7},{9,8},{11,10},{12,13},{14,15},{17,16},{19,... | collective-permute-start | bytes 1376264 | tf_op jit(solution)/shard_map/ppermute | solution.py:423
  102.0 14.9 %collective-permute-start.16 = (bf16[2,192,512]{2,1,0:T(8,128)(2,1)S(1)}, bf16[2,192,512]{2,1,0:T(8,128)(2,1)S(1)}, u32[]{:S(2)}, u32[]{:S(2)}) collective-permute-start(bf16[2,192,512]{2,1,0:T(8,128)(2,1)S(1)} %project.7), channel_id=1, source_target_pairs={{1,0},{3,2},{4,5},{6,7},{9,8},{11,10},{12,13},{14,15},{17,16},{19,... | collective-permute-start | bytes 1179656 | tf_op jit(solution)/shard_map/ppermute | solution.py:423
  105.2 21.4 %collective-permute-start.19 = (bf16[416,512]{1,0:T(8,128)(2,1)S(1)}, bf16[416,512]{1,0:T(8,128)(2,1)S(1)}, u32[]{:S(2)}, u32[]{:S(2)}) collective-permute-start(bf16[416,512]{1,0:T(8,128)(2,1)S(1)} %fusion.10), channel_id=1, source_target_pairs={{0,2},{2,0},{5,7},{7,5},{8,10},{10,8},{13,15},{15,13},{16,18},{18,... | collective-permute-start | bytes 1277960 | tf_op jit(solution)/shard_map/ppermute | solution.py:429
  110.1 16.3 %collective-permute-start.20 = (bf16[224,512]{1,0:T(8,128)(2,1)S(1)}, bf16[224,512]{1,0:T(8,128)(2,1)S(1)}, u32[]{:S(2)}, u32[]{:S(2)}) collective-permute-start(bf16[224,512]{1,0:T(8,128)(2,1)S(1)} %fusion.12), channel_id=1, source_target_pairs={{0,2},{2,0},{5,7},{7,5},{8,10},{10,8},{13,15},{15,13},{16,18},{18,... | collective-permute-start | bytes 688136 | tf_op jit(solution)/shard_map/ppermute | solution.py:429
  116.9 11.5 %collective-permute-start.22 = (bf16[192,512]{1,0:T(8,128)(2,1)S(1)}, bf16[192,512]{1,0:T(8,128)(2,1)S(1)}, u32[]{:S(2)}, u32[]{:S(2)}) collective-permute-start(bf16[192,512]{1,0:T(8,128)(2,1)S(1)} %fusion.13), channel_id=1, source_target_pairs={{0,2},{2,0},{5,7},{7,5},{8,10},{10,8},{13,15},{15,13},{16,18},{18,... | collective-permute-start | bytes 589832 | tf_op jit(solution)/shard_map/ppermute | solution.py:429
  127.0 3.8 %collective-permute-start.21 = (bf16[1088,256]{1,0:T(8,128)(2,1)S(1)}, bf16[1088,256]{1,0:T(8,128)(2,1)S(1)}, u32[]{:S(2)}, u32[]{:S(2)}) collective-permute-start(bf16[1088,256]{1,0:T(8,128)(2,1)S(1)} %get-tuple-element.51), channel_id=1, source_target_pairs={{0,4},{2,6},{5,1},{7,3},{8,12},{10,14},{13,9},{15,11},{16,20},{18,... | collective-permute-start | bytes 1671176 | tf_op jit(solution)/shard_map/ppermute | solution.py:437
  128.6 2.2 %collective-permute-start.23 = (bf16[192,256]{1,0:T(8,128)(2,1)S(1)}, bf16[192,256]{1,0:T(8,128)(2,1)S(1)}, u32[]{:S(2)}, u32[]{:S(2)}) collective-permute-start(bf16[192,256]{1,0:T(8,128)(2,1)S(1)} %get-tuple-element.55), channel_id=1, source_target_pairs={{0,4},{2,6},{5,1},{7,3},{8,12},{10,14},{13,9},{15,11},{16,20},{18,... | collective-permute-start | bytes 294920 | tf_op jit(solution)/shard_map/ppermute | solution.py:437
  (6 other events, 47.4 us)

commit v4 on v3

--- a/solution.py
+++ b/solution.py
@@ -17,7 +17,7 @@
 QKD = 192
 ROPE = LAT - KVR
 MASKED = -1e30
-PIECES = (448, 416, 224, 192)
+PIECES = (448, 416, 208, 208)
 STEPS = (1, 1, 1, 1)
 WHOLE = 2
 VMEM_BYTES = 60 * 1024 * 1024
@@ -30,8 +30,7 @@
 def attention_kernel(blocks_ref, mask_ref, query_ref, stretch_ref, *refs, together, skipped):
     *pieces, key_ref, value_ref, out_ref, latent, rope = refs
     step = pl.program_id(0)
-    piece_tokens = pieces[0].shape[1] // LAT
-    prefix = len(pieces) * piece_tokens * BLK
+    prefix = sum(piece.shape[1] // LAT for piece in pieces) * BLK
     total = prefix + STRETCH
 
     @pl.when(step == 0)
@@ -40,14 +39,14 @@
         row = lax.broadcasted_iota(jnp.int32, (BLK, ROPE), 0)
         hidden = (lane == 0) & (row >= blocks_ref[0])
         extra = jnp.where(hidden, MASKED, 0.0).astype(BF16)
-        for index, piece in enumerate(pieces):
-            for token in range(piece_tokens):
-                start = (index * piece_tokens + token) * BLK
-                base = LAT * token
-                latent[start : start + BLK, :] = piece[:, base : base + KVR]
-                rope[start : start + BLK, :] = jnp.concatenate(
-                    [piece[:, base + KVR : base + LAT], extra], axis=1
-                )
+        places = [(piece, token) for piece in pieces for token in range(piece.shape[1] // LAT)]
+        for index, (piece, token) in enumerate(places):
+            start = index * BLK
+            base = LAT * token
+            latent[start : start + BLK, :] = piece[:, base : base + KVR]
+            rope[start : start + BLK, :] = jnp.concatenate(
+                [piece[:, base + KVR : base + LAT], extra], axis=1
+            )
         latent[prefix:total, :] = stretch_ref[:, :KVR]
         rope[prefix:total, :] = jnp.concatenate(
             [stretch_ref[:, KVR:], jnp.zeros((STRETCH, ROPE), BF16)], axis=1
@@ -94,10 +93,9 @@
 
 def attention(blocks, head_mask, query, latent, pieces, up_key, up_value, part=0, parts=1):
     heads = up_key.shape[1] // NOPE // parts
-    together = math.gcd(heads, 4)
+    together = math.gcd(heads, 8)
     skipped = part * (heads // together)
-    piece_tokens = pieces[0].shape[1] // LAT
-    total = len(pieces) * piece_tokens * BLK + STRETCH
+    total = sum(piece.shape[1] // LAT for piece in pieces) * BLK + STRETCH
 
     def whole(array):
         return pl.BlockSpec(array.shape, lambda step: (0, 0))
@@ -375,20 +373,27 @@
     core = own_req & 1
     keeper = (own_head & 1) == core
     route = jnp.stack([(own_head >> 1) ^ (own_req >> 1), own_group, keeper]).astype(jnp.int32)
-    prefix = jnp.dot(
-        after(picks, route), jnp.concatenate(incoming, axis=0), preferred_element_type=F32
-    ).astype(BF16)
-    far = over_z(prefix, 2)
-    near = over_z(prefix, 1)
-    farther = over_z(after(far, near, *cuts, *owned), 1)
-    x0 = over_x(y0, far)
-    y1 = over_y(cuts[0], far)
+    picks = after(picks, route)
+    gathered = jnp.concatenate(incoming, axis=0)
+    width = gathered.shape[1] // 2
+    prefix = [
+        jnp.dot(picks, part, preferred_element_type=F32).astype(BF16)
+        for part in (gathered[:, :width], gathered[:, width:])
+    ]
+    far = [over_z(part, 2) for part in prefix]
+    near = [over_z(part, 1) for part in prefix]
+    farther = [
+        over_z(after(far[0], *cuts), 1),
+        over_z(after(far[1], *near, *cuts, *owned), 1),
+    ]
+    x0 = over_x(y0, far[1])
+    y1 = over_y(cuts[0], far[1])
     attended = attention(
         blocks,
         head_mask,
         stretch_query,
         stretch_latent,
-        [prefix, near, far, farther],
+        [*prefix, *near, *far, *farther],
         up_key,
         up_value,
     )
@@ -443,7 +448,7 @@
     sums1, got1 = send(1, [(y1, x1)], sums0, y2)
     sums2, got2 = send(2, [(y2,)], sums1, total0)
     sums3, got3 = send(3, [(y3,)], sums2, passed0[0])
-    total1 = halve(sums1, after(got1, sums3, passed0[1]))
+    total1 = halve(sums1, after(got1, sums3))
     passed1 = pass_on(total1)
     total2 = halve(sums2, after(got2, total1))
     passed2 = pass_on(total2)
@@ -451,8 +456,8 @@
     passed3 = pass_on(total3)
     passed0 = jnp.concatenate(passed0, axis=0)
     early = [
-        settle(sums0, got0, after(passed0, total3)),
-        settle(sums1, got1, after(passed1, total3)),
+        settle(sums0, got0, passed0),
+        settle(sums1, got1, passed1),
         settle(sums2, got2, after(passed2, total3)),
     ]
     settled = split(jnp.concatenate(early, axis=0)) + split(settle(sums3, got3, passed3))

time: 133 us -> 131 us (0.985)
  local copies, waits for them, and re-layouts: 16.7 us -> 12 us
  starting transfers between devices: 46.2 us -> 48.4 us
  waiting for transfers between devices: 27.8 us -> 29.4 us
    ppermute x3 -> x6, starting transfers between devices: 4.6 us -> 7.91 us  [over_z(): return lax.ppermute(piece, 'head', flip(head_count, bit))]
    slice x2, local copies, waits for them, and re-layouts: 3.18 us -> 0.23 us  [local(): lax.slice_in_dim(after(out_weight, incoming[1]), starts[chunk], starts[ch...]
    dynamic_slice x2 -> x1, local copies, waits for them, and re-layouts: 4.38 us -> 2.21 us  [cut(): lax.dynamic_slice_in_dim(weights, starts[chunk] + own_group * half, half, 0)]
    ppermute x5, starting transfers between devices: 23.1 us -> 21.1 us  [pass_on(): return lax.ppermute(total, axes, to_far)]
    ppermute x4, waiting for transfers between devices: 12.9 us -> 11.1 us  [over_y(): return lax.ppermute(after(piece, *earlier), 'req', flip(req_count, 2))]
    ppermute x2, waiting for transfers between devices: 0.78 us -> 2.49 us  [over_x(): return lax.ppermute(after(piece, *earlier), 'groups', flip(groups, 1))]
    ppermute x3 -> x6, waiting for transfers between devices: 5.78 us -> 6.87 us  [over_z(): return lax.ppermute(piece, 'head', flip(head_count, bit))]
    unnamed x13 -> x24, local copies, waits for them, and re-layouts: 3.1 us -> 4.06 us
  transfers between devices with their start and end apart: 24 -> 27, of which waited for: 12 -> 13; matrix products, arithmetic and copies ran while one was open for 13% -> 9% of each run, Pallas kernels for 24% -> 24%
where the time goes in v4:
time: 131 us
  starting transfers between devices  48.4 us (37%)
  Pallas kernels  36.3 us (28%)
  waiting for transfers between devices  29.4 us (22%)
  local copies, waits for them, and re-layouts  12 us (9%)
  between operations  2.95 us (2%)
    ppermute x5, starting transfers between devices, pass_on(): return lax.ppermute(total, axes, to_far)  21.1 us
    pallas_call x1, Pallas kernels, attention(): pl.pallas_call(lambda *refs: attention_kernel(*refs, together=together, s...  16.4 us
    pallas_call x4, Pallas kernels, project(): pl.pallas_call(lambda *refs: project_kernel(*refs, rows=rows, pair_counts...  15.4 us
    ppermute x4, waiting for transfers between devices, over_y(): return lax.ppermute(after(piece, *earlier), 'req', flip(req_count, 2))  11.1 us
    ppermute x6, starting transfers between devices, over_z(): return lax.ppermute(piece, 'head', flip(head_count, bit))  7.91 us
    ppermute x6, waiting for transfers between devices, over_z(): return lax.ppermute(piece, 'head', flip(head_count, bit))  6.87 us
    ppermute x4, waiting for transfers between devices, send(): return (sums, lax.ppermute(sums, axes, to_keeper))  5.69 us
    ppermute x4, starting transfers between devices, send(): return (sums, lax.ppermute(sums, axes, to_keeper))  5.48 us
  transfers between devices with their start and end apart: 27, of which 13 were waited for; matrix products, arithmetic and copies ran while one was open for 9% of the time, Pallas kernels for 24%

profile of v4, /device:TPU:0, one launch (start us, length us, event | category | flops | bytes accessed | tf_op | source)
XLA Modules:
  0.0 130.7 jit_solution(6685945360767213434)
XLA Ops:
  0.0 2.8 %pick.1 = (bf16[8,9216]{1,0:T(8,128)(2,1)}, bf16[8,9216]{1,0:T(8,128)(2,1)}, bf16[8,9216]{1,0:T(8,128)(2,1)}, bf16[8,9216]{1,0:T(8,128)(2,1)}) custom-call(s32[1]{0:T(128)} %bitcast.8.refs_0_, s32[4,16]{1,0:T(4,128)} %refs_1_.2, s32[4,16]{1,0:T(4,128)} %refs_2_.2, s32[4]{0:T(128)} %refs_3_.2, bf16[64,9216]{1,0:T(8,128)(2,1)} %refs_4_.1), custom_call_target="tpu_custom_call" | custom-call | flops 1024 | bytes 1024 | tf_op jit(solution)/shard_map/pick/pallas_call | solution.py:277
  3.2 2.5 %collective-permute-start.1 = (bf16[8,9216]{1,0:T(8,128)(2,1)}, bf16[8,9216]{1,0:T(8,128)(2,1)S(1)}, u32[]{:S(2)}, u32[]{:S(2)}) collective-permute-start(bf16[8,9216]{1,0:T(8,128)(2,1)} %get-tuple-element.30), channel_id=1, source_target_pairs={{0,8},{4,12},{8,0},{12,4},{1,9},{5,13},{9,1},{13,5},{2,10},{6,14},... | collective-permute-start | bytes 442376 | tf_op jit(solution)/shard_map/ppermute | solution.py:361
  5.9 2.2 %constant_dynamic-slice_fusion = bf16[224,2048]{1,0:T(8,128)(2,1)} fusion(bf16[1280,2048]{1,0:T(8,128)(2,1)} %param.19, s32[]{:T(128)S(6)} %select_n.21), kind=kLoop, calls=%fused_computation.31 | loop fusion | bytes 1835012 | tf_op jit(solution)/shard_map/dynamic_slice | solution.py:348
  8.1 1.7 %collective-permute-start.9 = (bf16[224,2048]{1,0:T(8,128)(2,1)}, bf16[224,2048]{1,0:T(8,128)(2,1)}, u32[]{:S(2)}, u32[]{:S(2)}) collective-permute-start(bf16[224,2048]{1,0:T(8,128)(2,1)} %constant_dynamic-slice_fusion), channel_id=1, source_target_pairs={{0,8},{4,12},{8,0},{12,4},{1,9},{5,13},{9,1},{13,5},{2,10},{6,14},... | collective-permute-start | bytes 2752520 | tf_op jit(solution)/shard_map/ppermute | solution.py:351
  17.2 2.6 %collective-permute-start.5 = (bf16[16,4608]{1,0:T(8,128)(2,1)S(1)}, bf16[16,4608]{1,0:T(8,128)(2,1)}, u32[]{:S(2)}, u32[]{:S(2)}) collective-permute-start(bf16[16,4608]{1,0:T(8,128)(2,1)S(1)} %convolution_convert_fusion.1.refs_4_), channel_id=1, source_target_pairs={{0,2},{1,3},{2,0},{3,1},{4,6},{5,7},{6,4},{7,5},{8,10},{9,11},{10,... | collective-permute-start | bytes 442376 | tf_op jit(solution)/shard_map/ppermute | solution.py:357
  20.8 3.8 %fusion.13 = (bf16[208,2048]{1,0:T(8,128)(2,1)}, bf16[208,2048]{1,0:T(8,128)(2,1)}, bf16[208,2048]{1,0:T(8,128)(2,1)}) fusion(bf16[1280,2048]{1,0:T(8,128)(2,1)} %param.19, s32[]{:T(128)S(6)} %select_n.20), kind=kLoop, calls=%fused_computation.39 | loop fusion | bytes 5111812 | tf_op jit(solution)/shard_map/slice | solution.py:346
  24.9 2.7 %collective-permute-done.5.refs_8_ = bf16[16,4608]{1,0:T(8,128)(2,1)} collective-permute-done((bf16[16,4608]{1,0:T(8,128)(2,1)S(1)}, bf16[16,4608]{1,0:T(8,128)(2,1)}, u32[]{:S(2)}, u32[]{:S(2)}) %collective-permute-start.5) | collective-permute-done | bytes 147488 | tf_op jit(solution)/shard_map/ppermute | solution.py:357
  28.2 3.3 %collective-permute-done.4.refs_7_ = bf16[16,4608]{1,0:T(8,128)(2,1)S(1)} collective-permute-done((bf16[16,4608]{1,0:T(8,128)(2,1)S(1)}, bf16[16,4608]{1,0:T(8,128)(2,1)S(1)}, u32[]{:S(2)}, u32[]{:S(2)}) %collective-permute-start.4) | collective-permute-done | bytes 147488 | tf_op jit(solution)/shard_map/ppermute | solution.py:357
  32.4 2.1 %collective-permute-start.8 = (bf16[16,4608]{1,0:T(8,128)(2,1)}, bf16[16,4608]{1,0:T(8,128)(2,1)}, u32[]{:S(2)}, u32[]{:S(2)}) collective-permute-start(bf16[16,4608]{1,0:T(8,128)(2,1)} %collective-permute-done.6.refs_9_), channel_id=1, source_target_pairs={{0,1},{1,0},{2,3},{3,2},{4,5},{5,4},{6,7},{7,6},{8,9},{9,8},{10,11... | collective-permute-start | bytes 442376 | tf_op jit(solution)/shard_map/ppermute | solution.py:357
  34.6 1.9 %copy.14.refs_3_ = bf16[256,576]{1,0:T(8,128)(2,1)} copy(bf16[256,576]{0,1:T(8,128)(2,1)} %param.11) | data formatting | bytes 589824 | tf_op args[1]
  38.4 16.4 %attention.1.refs_1_ = bf16[256,2048]{1,0:T(8,128)(2,1)} custom-call(s32[1]{0:T(128)} %bitcast.4.refs_0_, s32[16]{0:T(128)} %refs_1_.3, bf16[256,3072]{1,0:T(8,128)(2,1)} %refs_2_.3, bf16[256,576]{1,0:T(8,128)(2,1)} %copy.14.refs_3_, bf16[16,4608]{1,0:T(8,128)(2,1)} %copy-done.5, bf16[16,4608]{1,0:T(8,128)(2,1)} %copy-done.6, bf16[16,4608]{1,0:T(8,128)(2,1)} %copy-done.8, ...), custom_call_target="tpu_custom_call" | custom-call | flops 17999998976 | bytes 4194304 | tf_op jit(solution)/shard_map/attention/pallas_call | solution.py:107
  61.4 4.4 %project.4 = bf16[2,448,512]{2,1,0:T(8,128)(2,1)S(1)} custom-call(s32[3]{0:T(128)S(1)} %pad_add_fusion.refs_0_, bf16[256,2048]{1,0:T(8,128)(2,1)S(1)} %copy-done.2, bf16[256,2048]{1,0:T(8,128)(2,1)S(1)} %collective-permute-done.12.refs_2_, bf16[448,2048]{1,0:T(8,128)(2,1)S(1)} %slice.94.refs_3_, bf16[224,2048]{1,0:T(8,128)(2,1)} %collective-permute-done.9.refs_4_, ...), custom_call_target="tpu_custom_call" | custom-call | flops 2000000000 | bytes 4194304 | tf_op jit(solution)/shard_map/project/pallas_call | solution.py:192
  68.7 10.4 %collective-permute-done.16.refs_4_ = bf16[208,2048]{1,0:T(8,128)(2,1)S(1)} collective-permute-done((bf16[208,2048]{1,0:T(8,128)(2,1)}, bf16[208,2048]{1,0:T(8,128)(2,1)S(1)}, u32[]{:S(2)}, u32[]{:S(2)}) %collective-permute-start.16) | collective-permute-done | bytes 852000 | tf_op jit(solution)/shard_map/ppermute | solution.py:351
  79.9 4.4 %project.5 = bf16[2,416,512]{2,1,0:T(8,128)(2,1)S(1)} custom-call(s32[3]{0:T(128)S(1)} %pad_add_fusion.refs_0_, bf16[256,2048]{1,0:T(8,128)(2,1)S(1)} %copy-done.2, bf16[256,2048]{1,0:T(8,128)(2,1)S(1)} %collective-permute-done.12.refs_2_, bf16[416,2048]{1,0:T(8,128)(2,1)S(1)} %slice.95.refs_3_, bf16[208,2048]{1,0:T(8,128)(2,1)} %collective-permute-done.11.refs_4_, ...), custom_call_target="tpu_custom_call" | custom-call | flops 2000000000 | bytes 4194304 | tf_op jit(solution)/shard_map/project/pallas_call | solution.py:192
  86.0 3.7 %collective-permute-start.14 = (bf16[224,512]{1,0:T(8,128)(2,1)S(1)}, bf16[224,512]{1,0:T(8,128)(2,1)S(1)}, u32[]{:S(2)}, u32[]{:S(2)}) collective-permute-start(bf16[224,512]{1,0:T(8,128)(2,1)S(1)} %get-tuple-element.55), channel_id=1, source_target_pairs={{0,2},{2,0},{5,7},{7,5},{8,10},{10,8},{13,15},{15,13},{16,18},{18,... | collective-permute-start | bytes 688136 | tf_op jit(solution)/shard_map/ppermute | solution.py:434
  89.7 3.3 %project.6 = bf16[2,208,512]{2,1,0:T(8,128)(2,1)S(1)} custom-call(s32[3]{0:T(128)S(1)} %pad_add_fusion.refs_0_, bf16[256,2048]{1,0:T(8,128)(2,1)S(1)} %copy-done.3, bf16[256,2048]{1,0:T(8,128)(2,1)S(1)} %collective-permute-done.12.refs_2_, bf16[208,2048]{1,0:T(8,128)(2,1)S(1)} %copy-done.1, bf16[208,2048]{1,0:T(8,128)(2,1)S(1)} %collective-permute-done.16.refs_4_), custom_call_target="tpu_custom_call" | custom-call | flops 2000000000 | bytes 4194304 | tf_op jit(solution)/shard_map/project/pallas_call | solution.py:192
  94.3 3.0 %collective-permute-start.15 = (bf16[224,512]{1,0:T(8,128)(2,1)S(1)}, bf16[224,512]{1,0:T(8,128)(2,1)S(1)}, u32[]{:S(2)}, u32[]{:S(2)}) collective-permute-start(bf16[224,512]{1,0:T(8,128)(2,1)S(1)} %get-tuple-element.54), channel_id=1, source_target_pairs={{0,2},{2,0},{5,7},{7,5},{8,10},{10,8},{13,15},{15,13},{16,18},{18,... | collective-permute-start | bytes 688136 | tf_op jit(solution)/shard_map/ppermute | solution.py:434
  97.4 3.3 %project.7 = bf16[2,208,512]{2,1,0:T(8,128)(2,1)S(1)} custom-call(s32[3]{0:T(128)S(1)} %pad_add_fusion.refs_0_, bf16[256,2048]{1,0:T(8,128)(2,1)S(1)} %copy-done.3, bf16[256,2048]{1,0:T(8,128)(2,1)S(1)} %collective-permute-done.12.refs_2_, bf16[208,2048]{1,0:T(8,128)(2,1)S(1)} %copy-done, bf16[208,2048]{1,0:T(8,128)(2,1)S(1)} %collective-permute-done.19.refs_4_), custom_call_target="tpu_custom_call" | custom-call | flops 2000000000 | bytes 4194304 | tf_op jit(solution)/shard_map/project/pallas_call | solution.py:192
  102.6 4.7 %collective-permute-start.20 = (bf16[416,512]{1,0:T(8,128)(2,1)S(1)}, bf16[416,512]{1,0:T(8,128)(2,1)S(1)}, u32[]{:S(2)}, u32[]{:S(2)}) collective-permute-start(bf16[416,512]{1,0:T(8,128)(2,1)S(1)} %fusion.2), channel_id=1, source_target_pairs={{0,2},{2,0},{5,7},{7,5},{8,10},{10,8},{13,15},{15,13},{16,18},{18,... | collective-permute-start | bytes 1277960 | tf_op jit(solution)/shard_map/ppermute | solution.py:434
  108.7 4.7 %collective-permute-start.22 = (bf16[208,512]{1,0:T(8,128)(2,1)S(1)}, bf16[208,512]{1,0:T(8,128)(2,1)S(1)}, u32[]{:S(2)}, u32[]{:S(2)}) collective-permute-start(bf16[208,512]{1,0:T(8,128)(2,1)S(1)} %fusion.7), channel_id=1, source_target_pairs={{0,2},{2,0},{5,7},{7,5},{8,10},{10,8},{13,15},{15,13},{16,18},{18,... | collective-permute-start | bytes 638984 | tf_op jit(solution)/shard_map/ppermute | solution.py:434
  113.5 3.9 %collective-permute-done.23 = bf16[2,208,512]{2,1,0:T(8,128)(2,1)S(1)} collective-permute-done((bf16[2,208,512]{2,1,0:T(8,128)(2,1)S(1)}, bf16[2,208,512]{2,1,0:T(8,128)(2,1)S(1)}, u32[]{:S(2)}, u32[]{:S(2)}) %collective-permute-start.23) | collective-permute-done | bytes 426016 | tf_op jit(solution)/shard_map/ppermute | solution.py:428
  117.5 5.0 %collective-permute-start.25 = (bf16[208,512]{1,0:T(8,128)(2,1)S(1)}, bf16[208,512]{1,0:T(8,128)(2,1)S(1)}, u32[]{:S(2)}, u32[]{:S(2)}) collective-permute-start(bf16[208,512]{1,0:T(8,128)(2,1)S(1)} %fusion.8), channel_id=1, source_target_pairs={{0,2},{2,0},{5,7},{7,5},{8,10},{10,8},{13,15},{15,13},{16,18},{18,... | collective-permute-start | bytes 638984 | tf_op jit(solution)/shard_map/ppermute | solution.py:434
  122.5 1.8 %collective-permute-done.22 = bf16[208,512]{1,0:T(8,128)(2,1)S(1)} collective-permute-done((bf16[208,512]{1,0:T(8,128)(2,1)S(1)}, bf16[208,512]{1,0:T(8,128)(2,1)S(1)}, u32[]{:S(2)}, u32[]{:S(2)}) %collective-permute-start.22) | collective-permute-done | bytes 213024 | tf_op jit(solution)/shard_map/ppermute | solution.py:434
  128.9 1.8 %finish.1 = bf16[256,1280]{1,0:T(8,128)(2,1)} custom-call(s32[3]{0:T(128)S(1)} %pad_add_fusion.refs_0_, bf16[1072,256]{1,0:T(8,128)(2,1)S(1)} %get-tuple-element.53.refs_1_, bf16[1072,256]{1,0:T(8,128)(2,1)S(1)} %collective-permute-done.24.refs_2_, bf16[208,256]{1,0:T(8,128)(2,1)S(1)} %get-tuple-element.57.refs_3_, ...), custom_call_target="tpu_custom_call" | custom-call | flops 1024 | bytes 1024 | tf_op jit(solution)/shard_map/finish/pallas_call | solution.py:231
  (93 shorter events, 31.5 us)
Async XLA Ops:
  2.8 12.4 %collective-permute-start = (bf16[8,9216]{1,0:T(8,128)(2,1)}, bf16[8,9216]{1,0:T(8,128)(2,1)S(1)}, u32[]{:S(2)}, u32[]{:S(2)}) collective-permute-start(bf16[8,9216]{1,0:T(8,128)(2,1)} %get-tuple-element.29), channel_id=1, source_target_pairs={{0,4},{4,0},{8,12},{12,8},{1,5},{5,1},{9,13},{13,9},{2,6},{6,2},{1... | collective-permute-start | bytes 442376 | tf_op jit(solution)/shard_map/ppermute | solution.py:361
  3.2 12.0 %collective-permute-start.1 = (bf16[8,9216]{1,0:T(8,128)(2,1)}, bf16[8,9216]{1,0:T(8,128)(2,1)S(1)}, u32[]{:S(2)}, u32[]{:S(2)}) collective-permute-start(bf16[8,9216]{1,0:T(8,128)(2,1)} %get-tuple-element.30), channel_id=1, source_target_pairs={{0,8},{4,12},{8,0},{12,4},{1,9},{5,13},{9,1},{13,5},{2,10},{6,14},... | collective-permute-start | bytes 442376 | tf_op jit(solution)/shard_map/ppermute | solution.py:361
  5.7 9.5 %collective-permute-start.2 = (bf16[8,9216]{1,0:T(8,128)(2,1)}, bf16[8,9216]{1,0:T(8,128)(2,1)S(1)}, u32[]{:S(2)}, u32[]{:S(2)}) collective-permute-start(bf16[8,9216]{1,0:T(8,128)(2,1)} %get-tuple-element.31), channel_id=1, source_target_pairs={{0,12},{4,8},{8,4},{12,0},{1,13},{5,9},{9,5},{13,1},{2,14},{6,10},... | collective-permute-start | bytes 442376 | tf_op jit(solution)/shard_map/ppermute | solution.py:361
  8.1 28.8 %collective-permute-start.9 = (bf16[224,2048]{1,0:T(8,128)(2,1)}, bf16[224,2048]{1,0:T(8,128)(2,1)}, u32[]{:S(2)}, u32[]{:S(2)}) collective-permute-start(bf16[224,2048]{1,0:T(8,128)(2,1)} %constant_dynamic-slice_fusion), channel_id=1, source_target_pairs={{0,8},{4,12},{8,0},{12,4},{1,9},{5,13},{9,1},{13,5},{2,10},{6,14},... | collective-permute-start | bytes 2752520 | tf_op jit(solution)/shard_map/ppermute | solution.py:351
  15.5 12.7 %collective-permute-start.3 = (bf16[16,4608]{1,0:T(8,128)(2,1)S(1)}, bf16[16,4608]{1,0:T(8,128)(2,1)S(1)}, u32[]{:S(2)}, u32[]{:S(2)}) collective-permute-start(bf16[16,4608]{1,0:T(8,128)(2,1)S(1)} %convolution_convert_fusion.1.refs_4_), channel_id=1, source_target_pairs={{0,1},{1,0},{2,3},{3,2},{4,5},{5,4},{6,7},{7,6},{8,9},{9,8},{10,11... | collective-permute-start | bytes 442376 | tf_op jit(solution)/shard_map/ppermute | solution.py:357
  17.2 10.4 %collective-permute-start.5 = (bf16[16,4608]{1,0:T(8,128)(2,1)S(1)}, bf16[16,4608]{1,0:T(8,128)(2,1)}, u32[]{:S(2)}, u32[]{:S(2)}) collective-permute-start(bf16[16,4608]{1,0:T(8,128)(2,1)S(1)} %convolution_convert_fusion.1.refs_4_), channel_id=1, source_target_pairs={{0,2},{1,3},{2,0},{3,1},{4,6},{5,7},{6,4},{7,5},{8,10},{9,11},{10,... | collective-permute-start | bytes 442376 | tf_op jit(solution)/shard_map/ppermute | solution.py:357
  20.0 11.5 %collective-permute-start.4 = (bf16[16,4608]{1,0:T(8,128)(2,1)S(1)}, bf16[16,4608]{1,0:T(8,128)(2,1)S(1)}, u32[]{:S(2)}, u32[]{:S(2)}) collective-permute-start(bf16[16,4608]{1,0:T(8,128)(2,1)S(1)} %convolution_convert_fusion.refs_5_), channel_id=1, source_target_pairs={{0,1},{1,0},{2,3},{3,2},{4,5},{5,4},{6,7},{7,6},{8,9},{9,8},{10,11... | collective-permute-start | bytes 442376 | tf_op jit(solution)/shard_map/ppermute | solution.py:357
  20.5 11.9 %collective-permute-start.6 = (bf16[16,4608]{1,0:T(8,128)(2,1)S(1)}, bf16[16,4608]{1,0:T(8,128)(2,1)}, u32[]{:S(2)}, u32[]{:S(2)}) collective-permute-start(bf16[16,4608]{1,0:T(8,128)(2,1)S(1)} %convolution_convert_fusion.refs_5_), channel_id=1, source_target_pairs={{0,2},{1,3},{2,0},{3,1},{4,6},{5,7},{6,4},{7,5},{8,10},{9,11},{10,... | collective-permute-start | bytes 442376 | tf_op jit(solution)/shard_map/ppermute | solution.py:357
  27.5 10.9 %collective-permute-start.7 = (bf16[16,4608]{1,0:T(8,128)(2,1)}, bf16[16,4608]{1,0:T(8,128)(2,1)}, u32[]{:S(2)}, u32[]{:S(2)}) collective-permute-start(bf16[16,4608]{1,0:T(8,128)(2,1)} %collective-permute-done.5.refs_8_), channel_id=1, source_target_pairs={{0,1},{1,0},{2,3},{3,2},{4,5},{5,4},{6,7},{7,6},{8,9},{9,8},{10,11... | collective-permute-start | bytes 442376 | tf_op jit(solution)/shard_map/ppermute | solution.py:357
  32.4 6.0 %collective-permute-start.8 = (bf16[16,4608]{1,0:T(8,128)(2,1)}, bf16[16,4608]{1,0:T(8,128)(2,1)}, u32[]{:S(2)}, u32[]{:S(2)}) collective-permute-start(bf16[16,4608]{1,0:T(8,128)(2,1)} %collective-permute-done.6.refs_9_), channel_id=1, source_target_pairs={{0,1},{1,0},{2,3},{3,2},{4,5},{5,4},{6,7},{7,6},{8,9},{9,8},{10,11... | collective-permute-start | bytes 442376 | tf_op jit(solution)/shard_map/ppermute | solution.py:357
  36.4 19.1 %collective-permute-start.11 = (bf16[208,2048]{1,0:T(8,128)(2,1)}, bf16[208,2048]{1,0:T(8,128)(2,1)}, u32[]{:S(2)}, u32[]{:S(2)}) collective-permute-start(bf16[208,2048]{1,0:T(8,128)(2,1)} %get-tuple-element.37), channel_id=1, source_target_pairs={{0,8},{4,12},{8,0},{12,4},{1,9},{5,13},{9,1},{13,5},{2,10},{6,14},... | collective-permute-start | bytes 2555912 | tf_op jit(solution)/shard_map/ppermute | solution.py:351
  36.9 20.2 %collective-permute-start.10 = (bf16[224,2048]{1,0:T(8,128)(2,1)}, bf16[224,2048]{1,0:T(8,128)(2,1)}, u32[]{:S(2)}, u32[]{:S(2)}) collective-permute-start(bf16[224,2048]{1,0:T(8,128)(2,1)} %collective-permute-done.9.refs_4_), channel_id=1, source_target_pairs={{0,16},{16,0},{1,17},{17,1},{2,18},{18,2},{3,19},{19,3},{4,20},{20... | collective-permute-start | bytes 2752520 | tf_op jit(solution)/shard_map/ppermute | solution.py:354
  57.1 22.0 %collective-permute-start.16 = (bf16[208,2048]{1,0:T(8,128)(2,1)}, bf16[208,2048]{1,0:T(8,128)(2,1)S(1)}, u32[]{:S(2)}, u32[]{:S(2)}) collective-permute-start(bf16[208,2048]{1,0:T(8,128)(2,1)} %get-tuple-element.39.refs_3_), channel_id=1, source_target_pairs={{0,8},{4,12},{8,0},{12,4},{1,9},{5,13},{9,1},{13,5},{2,10},{6,14},... | collective-permute-start | bytes 2555912 | tf_op jit(solution)/shard_map/ppermute | solution.py:351
  58.7 21.3 %collective-permute-start.17 = (bf16[208,2048]{1,0:T(8,128)(2,1)}, bf16[208,2048]{1,0:T(8,128)(2,1)S(1)}, u32[]{:S(2)}, u32[]{:S(2)}) collective-permute-start(bf16[208,2048]{1,0:T(8,128)(2,1)} %collective-permute-done.11.refs_4_), channel_id=1, source_target_pairs={{0,16},{16,0},{1,17},{17,1},{2,18},{18,2},{3,19},{19,3},{4,20},{20... | collective-permute-start | bytes 2555912 | tf_op jit(solution)/shard_map/ppermute | solution.py:354
  65.7 20.1 %collective-permute-start.13 = (bf16[2,448,512]{2,1,0:T(8,128)(2,1)S(1)}, bf16[2,448,512]{2,1,0:T(8,128)(2,1)S(1)}, u32[]{:S(2)}, u32[]{:S(2)}) collective-permute-start(bf16[2,448,512]{2,1,0:T(8,128)(2,1)S(1)} %project.4), channel_id=1, source_target_pairs={{1,0},{3,2},{4,5},{6,7},{9,8},{11,10},{12,13},{14,15},{17,16},{19,... | collective-permute-start | bytes 2752520 | tf_op jit(solution)/shard_map/ppermute | solution.py:428
  67.2 30.2 %collective-permute-start.19 = (bf16[208,2048]{1,0:T(8,128)(2,1)S(1)}, bf16[208,2048]{1,0:T(8,128)(2,1)S(1)}, u32[]{:S(2)}, u32[]{:S(2)}) collective-permute-start(bf16[208,2048]{1,0:T(8,128)(2,1)S(1)} %copy-done), channel_id=1, source_target_pairs={{0,8},{4,12},{8,0},{12,4},{1,9},{5,13},{9,1},{13,5},{2,10},{6,14},... | collective-permute-start | bytes 2555912 | tf_op jit(solution)/shard_map/ppermute | solution.py:351
  84.4 18.1 %collective-permute-start.18 = (bf16[2,416,512]{2,1,0:T(8,128)(2,1)S(1)}, bf16[2,416,512]{2,1,0:T(8,128)(2,1)S(1)}, u32[]{:S(2)}, u32[]{:S(2)}) collective-permute-start(bf16[2,416,512]{2,1,0:T(8,128)(2,1)S(1)} %project.5), channel_id=1, source_target_pairs={{1,0},{3,2},{4,5},{6,7},{9,8},{11,10},{12,13},{14,15},{17,16},{19,... | collective-permute-start | bytes 2555912 | tf_op jit(solution)/shard_map/ppermute | solution.py:428
  86.0 11.4 %collective-permute-start.14 = (bf16[224,512]{1,0:T(8,128)(2,1)S(1)}, bf16[224,512]{1,0:T(8,128)(2,1)S(1)}, u32[]{:S(2)}, u32[]{:S(2)}) collective-permute-start(bf16[224,512]{1,0:T(8,128)(2,1)S(1)} %get-tuple-element.55), channel_id=1, source_target_pairs={{0,2},{2,0},{5,7},{7,5},{8,10},{10,8},{13,15},{15,13},{16,18},{18,... | collective-permute-start | bytes 688136 | tf_op jit(solution)/shard_map/ppermute | solution.py:434
  93.0 15.6 %collective-permute-start.21 = (bf16[2,208,512]{2,1,0:T(8,128)(2,1)S(1)}, bf16[2,208,512]{2,1,0:T(8,128)(2,1)S(1)}, u32[]{:S(2)}, u32[]{:S(2)}) collective-permute-start(bf16[2,208,512]{2,1,0:T(8,128)(2,1)S(1)} %project.6), channel_id=1, source_target_pairs={{1,0},{3,2},{4,5},{6,7},{9,8},{11,10},{12,13},{14,15},{17,16},{19,... | collective-permute-start | bytes 1277960 | tf_op jit(solution)/shard_map/ppermute | solution.py:428
  94.3 19.0 %collective-permute-start.15 = (bf16[224,512]{1,0:T(8,128)(2,1)S(1)}, bf16[224,512]{1,0:T(8,128)(2,1)S(1)}, u32[]{:S(2)}, u32[]{:S(2)}) collective-permute-start(bf16[224,512]{1,0:T(8,128)(2,1)S(1)} %get-tuple-element.54), channel_id=1, source_target_pairs={{0,2},{2,0},{5,7},{7,5},{8,10},{10,8},{13,15},{15,13},{16,18},{18,... | collective-permute-start | bytes 688136 | tf_op jit(solution)/shard_map/ppermute | solution.py:434
  100.7 16.7 %collective-permute-start.23 = (bf16[2,208,512]{2,1,0:T(8,128)(2,1)S(1)}, bf16[2,208,512]{2,1,0:T(8,128)(2,1)S(1)}, u32[]{:S(2)}, u32[]{:S(2)}) collective-permute-start(bf16[2,208,512]{2,1,0:T(8,128)(2,1)S(1)} %project.7), channel_id=1, source_target_pairs={{1,0},{3,2},{4,5},{6,7},{9,8},{11,10},{12,13},{14,15},{17,16},{19,... | collective-permute-start | bytes 1277960 | tf_op jit(solution)/shard_map/ppermute | solution.py:428
  102.6 21.8 %collective-permute-start.20 = (bf16[416,512]{1,0:T(8,128)(2,1)S(1)}, bf16[416,512]{1,0:T(8,128)(2,1)S(1)}, u32[]{:S(2)}, u32[]{:S(2)}) collective-permute-start(bf16[416,512]{1,0:T(8,128)(2,1)S(1)} %fusion.2), channel_id=1, source_target_pairs={{0,2},{2,0},{5,7},{7,5},{8,10},{10,8},{13,15},{15,13},{16,18},{18,... | collective-permute-start | bytes 1277960 | tf_op jit(solution)/shard_map/ppermute | solution.py:434
  108.7 15.6 %collective-permute-start.22 = (bf16[208,512]{1,0:T(8,128)(2,1)S(1)}, bf16[208,512]{1,0:T(8,128)(2,1)S(1)}, u32[]{:S(2)}, u32[]{:S(2)}) collective-permute-start(bf16[208,512]{1,0:T(8,128)(2,1)S(1)} %fusion.7), channel_id=1, source_target_pairs={{0,2},{2,0},{5,7},{7,5},{8,10},{10,8},{13,15},{15,13},{16,18},{18,... | collective-permute-start | bytes 638984 | tf_op jit(solution)/shard_map/ppermute | solution.py:434
  117.5 9.1 %collective-permute-start.25 = (bf16[208,512]{1,0:T(8,128)(2,1)S(1)}, bf16[208,512]{1,0:T(8,128)(2,1)S(1)}, u32[]{:S(2)}, u32[]{:S(2)}) collective-permute-start(bf16[208,512]{1,0:T(8,128)(2,1)S(1)} %fusion.8), channel_id=1, source_target_pairs={{0,2},{2,0},{5,7},{7,5},{8,10},{10,8},{13,15},{15,13},{16,18},{18,... | collective-permute-start | bytes 638984 | tf_op jit(solution)/shard_map/ppermute | solution.py:434
  (13 other events, 67.4 us)

commit v5 on v4

--- a/solution.py
+++ b/solution.py
@@ -383,7 +383,7 @@
     far = [over_z(part, 2) for part in prefix]
     near = [over_z(part, 1) for part in prefix]
     farther = [
-        over_z(after(far[0], *cuts), 1),
+        over_z(far[0], 1),
         over_z(after(far[1], *near, *cuts, *owned), 1),
     ]
     x0 = over_x(y0, far[1])

time: 131 us -> 133 us (1.015)
  starting transfers between devices: 48.4 us -> 53.3 us
  waiting for transfers between devices: 29.4 us -> 25.8 us
    ppermute x5, starting transfers between devices: 21.1 us -> 26.8 us  [pass_on(): return lax.ppermute(total, axes, to_far)]
    ppermute x4, waiting for transfers between devices: 5.69 us -> 1.4 us  [send(): return (sums, lax.ppermute(sums, axes, to_keeper))]
    ppermute x6, waiting for transfers between devices: 6.87 us -> 9.5 us  [over_z(): return lax.ppermute(piece, 'head', flip(head_count, bit))]
  transfers between devices with their start and end apart: 27 -> 27, of which waited for: 13 -> 12; matrix products, arithmetic and copies ran while one was open for 9% -> 9% of each run, Pallas kernels for 24% -> 24%
where the time goes in v5:
time: 133 us; the launch traced here: 132 us
  starting transfers between devices  53.3 us (40%)
  Pallas kernels  36.3 us (27%)
  waiting for transfers between devices  25.8 us (19%)
  local copies, waits for them, and re-layouts  12 us (9%)
  between operations  2.96 us (2%)
    ppermute x5, starting transfers between devices, pass_on(): return lax.ppermute(total, axes, to_far)  26.8 us
    pallas_call x1, Pallas kernels, attention(): pl.pallas_call(lambda *refs: attention_kernel(*refs, together=together, s...  16.3 us
    pallas_call x4, Pallas kernels, project(): pl.pallas_call(lambda *refs: project_kernel(*refs, rows=rows, pair_counts...  15.3 us
    ppermute x4, waiting for transfers between devices, over_y(): return lax.ppermute(after(piece, *earlier), 'req', flip(req_count, 2))  10.4 us
    ppermute x6, waiting for transfers between devices, over_z(): return lax.ppermute(piece, 'head', flip(head_count, bit))  9.5 us
    ppermute x6, starting transfers between devices, over_z(): return lax.ppermute(piece, 'head', flip(head_count, bit))  7.11 us
    ppermute x4, starting transfers between devices, send(): return (sums, lax.ppermute(sums, axes, to_keeper))  5.48 us
    ppermute x4, starting transfers between devices, over_y(): return lax.ppermute(after(piece, *earlier), 'req', flip(req_count, 2))  5.17 us
  transfers between devices with their start and end apart: 27, of which 12 were waited for; matrix products, arithmetic and copies ran while one was open for 9% of the time, Pallas kernels for 24%

profile of v5, /device:TPU:0, one launch (start us, length us, event | category | flops | bytes accessed | tf_op | source)
XLA Modules:
  0.0 131.9 jit_solution(9658051564830859494)
XLA Ops:
  0.0 2.8 %pick.1 = (bf16[8,9216]{1,0:T(8,128)(2,1)}, bf16[8,9216]{1,0:T(8,128)(2,1)}, bf16[8,9216]{1,0:T(8,128)(2,1)}, bf16[8,9216]{1,0:T(8,128)(2,1)}) custom-call(s32[1]{0:T(128)} %bitcast.8.refs_0_, s32[4,16]{1,0:T(4,128)} %refs_1_.2, s32[4,16]{1,0:T(4,128)} %refs_2_.2, s32[4]{0:T(128)} %refs_3_.2, bf16[64,9216]{1,0:T(8,128)(2,1)} %refs_4_.1), custom_call_target="tpu_custom_call" | custom-call | flops 1024 | bytes 1024 | tf_op jit(solution)/shard_map/pick/pallas_call | solution.py:277
  3.2 2.5 %collective-permute-start.1 = (bf16[8,9216]{1,0:T(8,128)(2,1)}, bf16[8,9216]{1,0:T(8,128)(2,1)S(1)}, u32[]{:S(2)}, u32[]{:S(2)}) collective-permute-start(bf16[8,9216]{1,0:T(8,128)(2,1)} %get-tuple-element.29), channel_id=1, source_target_pairs={{0,8},{4,12},{8,0},{12,4},{1,9},{5,13},{9,1},{13,5},{2,10},{6,14},... | collective-permute-start | bytes 442376 | tf_op jit(solution)/shard_map/ppermute | solution.py:361
  5.9 2.2 %constant_dynamic-slice_fusion = bf16[224,2048]{1,0:T(8,128)(2,1)} fusion(bf16[1280,2048]{1,0:T(8,128)(2,1)} %param.19, s32[]{:T(128)S(6)} %select_n.21), kind=kLoop, calls=%fused_computation.31 | loop fusion | bytes 1835012 | tf_op jit(solution)/shard_map/dynamic_slice | solution.py:348
  8.1 1.7 %collective-permute-start.9 = (bf16[224,2048]{1,0:T(8,128)(2,1)}, bf16[224,2048]{1,0:T(8,128)(2,1)}, u32[]{:S(2)}, u32[]{:S(2)}) collective-permute-start(bf16[224,2048]{1,0:T(8,128)(2,1)} %constant_dynamic-slice_fusion), channel_id=1, source_target_pairs={{0,8},{4,12},{8,0},{12,4},{1,9},{5,13},{9,1},{13,5},{2,10},{6,14},... | collective-permute-start | bytes 2752520 | tf_op jit(solution)/shard_map/ppermute | solution.py:351
  15.5 1.6 %collective-permute-start.3 = (bf16[16,4608]{1,0:T(8,128)(2,1)S(1)}, bf16[16,4608]{1,0:T(8,128)(2,1)S(1)}, u32[]{:S(2)}, u32[]{:S(2)}) collective-permute-start(bf16[16,4608]{1,0:T(8,128)(2,1)S(1)} %convolution_convert_fusion.1.refs_4_), channel_id=1, source_target_pairs={{0,1},{1,0},{2,3},{3,2},{4,5},{5,4},{6,7},{7,6},{8,9},{9,8},{10,11... | collective-permute-start | bytes 442376 | tf_op jit(solution)/shard_map/ppermute | solution.py:357
  17.2 2.6 %collective-permute-start.5 = (bf16[16,4608]{1,0:T(8,128)(2,1)S(1)}, bf16[16,4608]{1,0:T(8,128)(2,1)}, u32[]{:S(2)}, u32[]{:S(2)}) collective-permute-start(bf16[16,4608]{1,0:T(8,128)(2,1)S(1)} %convolution_convert_fusion.1.refs_4_), channel_id=1, source_target_pairs={{0,2},{1,3},{2,0},{3,1},{4,6},{5,7},{6,4},{7,5},{8,10},{9,11},{10,... | collective-permute-start | bytes 442376 | tf_op jit(solution)/shard_map/ppermute | solution.py:357
  20.8 3.8 %fusion.13 = (bf16[208,2048]{1,0:T(8,128)(2,1)}, bf16[208,2048]{1,0:T(8,128)(2,1)}, bf16[208,2048]{1,0:T(8,128)(2,1)}) fusion(bf16[1280,2048]{1,0:T(8,128)(2,1)} %param.19, s32[]{:T(128)S(6)} %select_n.20), kind=kLoop, calls=%fused_computation.39 | loop fusion | bytes 5111812 | tf_op jit(solution)/shard_map/slice | solution.py:346
  25.2 5.3 %collective-permute-done.4.refs_7_ = bf16[16,4608]{1,0:T(8,128)(2,1)S(1)} collective-permute-done((bf16[16,4608]{1,0:T(8,128)(2,1)S(1)}, bf16[16,4608]{1,0:T(8,128)(2,1)S(1)}, u32[]{:S(2)}, u32[]{:S(2)}) %collective-permute-start.4) | collective-permute-done | bytes 147488 | tf_op jit(solution)/shard_map/ppermute | solution.py:357
  30.5 2.7 %collective-permute-done.6.refs_9_ = bf16[16,4608]{1,0:T(8,128)(2,1)} collective-permute-done((bf16[16,4608]{1,0:T(8,128)(2,1)S(1)}, bf16[16,4608]{1,0:T(8,128)(2,1)}, u32[]{:S(2)}, u32[]{:S(2)}) %collective-permute-start.6) | collective-permute-done | bytes 147488 | tf_op jit(solution)/shard_map/ppermute | solution.py:357
  33.7 1.6 %collective-permute-start.8 = (bf16[16,4608]{1,0:T(8,128)(2,1)}, bf16[16,4608]{1,0:T(8,128)(2,1)}, u32[]{:S(2)}, u32[]{:S(2)}) collective-permute-start(bf16[16,4608]{1,0:T(8,128)(2,1)} %collective-permute-done.6.refs_9_), channel_id=1, source_target_pairs={{0,1},{1,0},{2,3},{3,2},{4,5},{5,4},{6,7},{7,6},{8,9},{9,8},{10,11... | collective-permute-start | bytes 442376 | tf_op jit(solution)/shard_map/ppermute | solution.py:357
  35.2 1.9 %copy.14.refs_3_ = bf16[256,576]{1,0:T(8,128)(2,1)} copy(bf16[256,576]{0,1:T(8,128)(2,1)} %param.11) | data formatting | bytes 589824 | tf_op args[1]
  40.3 16.3 %attention.1.refs_1_ = bf16[256,2048]{1,0:T(8,128)(2,1)} custom-call(s32[1]{0:T(128)} %bitcast.4.refs_0_, s32[16]{0:T(128)} %refs_1_.3, bf16[256,3072]{1,0:T(8,128)(2,1)} %refs_2_.3, bf16[256,576]{1,0:T(8,128)(2,1)} %copy.14.refs_3_, bf16[16,4608]{1,0:T(8,128)(2,1)} %copy-done.5, bf16[16,4608]{1,0:T(8,128)(2,1)} %copy-done.6, bf16[16,4608]{1,0:T(8,128)(2,1)} %copy-done.8, ...), custom_call_target="tpu_custom_call" | custom-call | flops 17999998976 | bytes 4194304 | tf_op jit(solution)/shard_map/attention/pallas_call | solution.py:107
  57.2 1.5 %collective-permute-start.16 = (bf16[208,2048]{1,0:T(8,128)(2,1)}, bf16[208,2048]{1,0:T(8,128)(2,1)S(1)}, u32[]{:S(2)}, u32[]{:S(2)}) collective-permute-start(bf16[208,2048]{1,0:T(8,128)(2,1)} %get-tuple-element.37.refs_3_), channel_id=1, source_target_pairs={{0,8},{4,12},{8,0},{12,4},{1,9},{5,13},{9,1},{13,5},{2,10},{6,14},... | collective-permute-start | bytes 2555912 | tf_op jit(solution)/shard_map/ppermute | solution.py:351
  61.5 4.4 %project.4 = bf16[2,448,512]{2,1,0:T(8,128)(2,1)S(1)} custom-call(s32[3]{0:T(128)S(1)} %pad_add_fusion.refs_0_, bf16[256,2048]{1,0:T(8,128)(2,1)S(1)} %copy-done.2, bf16[256,2048]{1,0:T(8,128)(2,1)S(1)} %collective-permute-done.12.refs_2_, bf16[448,2048]{1,0:T(8,128)(2,1)S(1)} %slice.94.refs_3_, bf16[224,2048]{1,0:T(8,128)(2,1)} %collective-permute-done.9.refs_4_, ...), custom_call_target="tpu_custom_call" | custom-call | flops 2000000000 | bytes 4194304 | tf_op jit(solution)/shard_map/project/pallas_call | solution.py:192
  68.8 10.4 %collective-permute-done.16.refs_4_ = bf16[208,2048]{1,0:T(8,128)(2,1)S(1)} collective-permute-done((bf16[208,2048]{1,0:T(8,128)(2,1)}, bf16[208,2048]{1,0:T(8,128)(2,1)S(1)}, u32[]{:S(2)}, u32[]{:S(2)}) %collective-permute-start.16) | collective-permute-done | bytes 852000 | tf_op jit(solution)/shard_map/ppermute | solution.py:351
  80.0 4.4 %project.5 = bf16[2,416,512]{2,1,0:T(8,128)(2,1)S(1)} custom-call(s32[3]{0:T(128)S(1)} %pad_add_fusion.refs_0_, bf16[256,2048]{1,0:T(8,128)(2,1)S(1)} %copy-done.2, bf16[256,2048]{1,0:T(8,128)(2,1)S(1)} %collective-permute-done.12.refs_2_, bf16[416,2048]{1,0:T(8,128)(2,1)S(1)} %slice.95.refs_3_, bf16[208,2048]{1,0:T(8,128)(2,1)} %collective-permute-done.11.refs_4_, ...), custom_call_target="tpu_custom_call" | custom-call | flops 2000000000 | bytes 4194304 | tf_op jit(solution)/shard_map/project/pallas_call | solution.py:192
  86.1 4.4 %collective-permute-start.14 = (bf16[224,512]{1,0:T(8,128)(2,1)S(1)}, bf16[224,512]{1,0:T(8,128)(2,1)S(1)}, u32[]{:S(2)}, u32[]{:S(2)}) collective-permute-start(bf16[224,512]{1,0:T(8,128)(2,1)S(1)} %get-tuple-element.53), channel_id=1, source_target_pairs={{0,2},{2,0},{5,7},{7,5},{8,10},{10,8},{13,15},{15,13},{16,18},{18,... | collective-permute-start | bytes 688136 | tf_op jit(solution)/shard_map/ppermute | solution.py:434
  90.5 3.3 %project.6 = bf16[2,208,512]{2,1,0:T(8,128)(2,1)S(1)} custom-call(s32[3]{0:T(128)S(1)} %pad_add_fusion.refs_0_, bf16[256,2048]{1,0:T(8,128)(2,1)S(1)} %copy-done.3, bf16[256,2048]{1,0:T(8,128)(2,1)S(1)} %collective-permute-done.12.refs_2_, bf16[208,2048]{1,0:T(8,128)(2,1)S(1)} %copy-done.1, bf16[208,2048]{1,0:T(8,128)(2,1)S(1)} %collective-permute-done.16.refs_4_), custom_call_target="tpu_custom_call" | custom-call | flops 2000000000 | bytes 4194304 | tf_op jit(solution)/shard_map/project/pallas_call | solution.py:192
  95.1 2.4 %collective-permute-start.15 = (bf16[224,512]{1,0:T(8,128)(2,1)S(1)}, bf16[224,512]{1,0:T(8,128)(2,1)S(1)}, u32[]{:S(2)}, u32[]{:S(2)}) collective-permute-start(bf16[224,512]{1,0:T(8,128)(2,1)S(1)} %get-tuple-element.52), channel_id=1, source_target_pairs={{0,2},{2,0},{5,7},{7,5},{8,10},{10,8},{13,15},{15,13},{16,18},{18,... | collective-permute-start | bytes 688136 | tf_op jit(solution)/shard_map/ppermute | solution.py:434
  97.5 3.3 %project.7 = bf16[2,208,512]{2,1,0:T(8,128)(2,1)S(1)} custom-call(s32[3]{0:T(128)S(1)} %pad_add_fusion.refs_0_, bf16[256,2048]{1,0:T(8,128)(2,1)S(1)} %copy-done.3, bf16[256,2048]{1,0:T(8,128)(2,1)S(1)} %collective-permute-done.12.refs_2_, bf16[208,2048]{1,0:T(8,128)(2,1)S(1)} %copy-done, bf16[208,2048]{1,0:T(8,128)(2,1)S(1)} %collective-permute-done.19.refs_4_), custom_call_target="tpu_custom_call" | custom-call | flops 2000000000 | bytes 4194304 | tf_op jit(solution)/shard_map/project/pallas_call | solution.py:192
  102.2 6.4 %collective-permute-start.20 = (bf16[416,512]{1,0:T(8,128)(2,1)S(1)}, bf16[416,512]{1,0:T(8,128)(2,1)S(1)}, u32[]{:S(2)}, u32[]{:S(2)}) collective-permute-start(bf16[416,512]{1,0:T(8,128)(2,1)S(1)} %fusion.2), channel_id=1, source_target_pairs={{0,2},{2,0},{5,7},{7,5},{8,10},{10,8},{13,15},{15,13},{16,18},{18,... | collective-permute-start | bytes 1277960 | tf_op jit(solution)/shard_map/ppermute | solution.py:434
  108.7 6.1 %collective-permute-start.22 = (bf16[208,512]{1,0:T(8,128)(2,1)S(1)}, bf16[208,512]{1,0:T(8,128)(2,1)S(1)}, u32[]{:S(2)}, u32[]{:S(2)}) collective-permute-start(bf16[208,512]{1,0:T(8,128)(2,1)S(1)} %fusion.7), channel_id=1, source_target_pairs={{0,2},{2,0},{5,7},{7,5},{8,10},{10,8},{13,15},{15,13},{16,18},{18,... | collective-permute-start | bytes 638984 | tf_op jit(solution)/shard_map/ppermute | solution.py:434
  116.4 7.5 %collective-permute-start.25 = (bf16[208,512]{1,0:T(8,128)(2,1)S(1)}, bf16[208,512]{1,0:T(8,128)(2,1)S(1)}, u32[]{:S(2)}, u32[]{:S(2)}) collective-permute-start(bf16[208,512]{1,0:T(8,128)(2,1)S(1)} %fusion.8), channel_id=1, source_target_pairs={{0,2},{2,0},{5,7},{7,5},{8,10},{10,8},{13,15},{15,13},{16,18},{18,... | collective-permute-start | bytes 638984 | tf_op jit(solution)/shard_map/ppermute | solution.py:434
  130.1 1.8 %finish.1 = bf16[256,1280]{1,0:T(8,128)(2,1)} custom-call(s32[3]{0:T(128)S(1)} %pad_add_fusion.refs_0_, bf16[1072,256]{1,0:T(8,128)(2,1)S(1)} %get-tuple-element.51.refs_1_, bf16[1072,256]{1,0:T(8,128)(2,1)S(1)} %collective-permute-done.24.refs_2_, bf16[208,256]{1,0:T(8,128)(2,1)S(1)} %get-tuple-element.55.refs_3_, ...), custom_call_target="tpu_custom_call" | custom-call | flops 1024 | bytes 1024 | tf_op jit(solution)/shard_map/finish/pallas_call | solution.py:231
  (93 shorter events, 28.1 us)
Async XLA Ops:
  2.8 12.4 %collective-permute-start = (bf16[8,9216]{1,0:T(8,128)(2,1)}, bf16[8,9216]{1,0:T(8,128)(2,1)S(1)}, u32[]{:S(2)}, u32[]{:S(2)}) collective-permute-start(bf16[8,9216]{1,0:T(8,128)(2,1)} %get-tuple-element.28), channel_id=1, source_target_pairs={{0,4},{4,0},{8,12},{12,8},{1,5},{5,1},{9,13},{13,9},{2,6},{6,2},{1... | collective-permute-start | bytes 442376 | tf_op jit(solution)/shard_map/ppermute | solution.py:361
  3.2 12.0 %collective-permute-start.1 = (bf16[8,9216]{1,0:T(8,128)(2,1)}, bf16[8,9216]{1,0:T(8,128)(2,1)S(1)}, u32[]{:S(2)}, u32[]{:S(2)}) collective-permute-start(bf16[8,9216]{1,0:T(8,128)(2,1)} %get-tuple-element.29), channel_id=1, source_target_pairs={{0,8},{4,12},{8,0},{12,4},{1,9},{5,13},{9,1},{13,5},{2,10},{6,14},... | collective-permute-start | bytes 442376 | tf_op jit(solution)/shard_map/ppermute | solution.py:361
  5.7 9.5 %collective-permute-start.2 = (bf16[8,9216]{1,0:T(8,128)(2,1)}, bf16[8,9216]{1,0:T(8,128)(2,1)S(1)}, u32[]{:S(2)}, u32[]{:S(2)}) collective-permute-start(bf16[8,9216]{1,0:T(8,128)(2,1)} %get-tuple-element.30), channel_id=1, source_target_pairs={{0,12},{4,8},{8,4},{12,0},{1,13},{5,9},{9,5},{13,1},{2,14},{6,10},... | collective-permute-start | bytes 442376 | tf_op jit(solution)/shard_map/ppermute | solution.py:361
  8.1 29.5 %collective-permute-start.9 = (bf16[224,2048]{1,0:T(8,128)(2,1)}, bf16[224,2048]{1,0:T(8,128)(2,1)}, u32[]{:S(2)}, u32[]{:S(2)}) collective-permute-start(bf16[224,2048]{1,0:T(8,128)(2,1)} %constant_dynamic-slice_fusion), channel_id=1, source_target_pairs={{0,8},{4,12},{8,0},{12,4},{1,9},{5,13},{9,1},{13,5},{2,10},{6,14},... | collective-permute-start | bytes 2752520 | tf_op jit(solution)/shard_map/ppermute | solution.py:351
  15.5 9.7 %collective-permute-start.3 = (bf16[16,4608]{1,0:T(8,128)(2,1)S(1)}, bf16[16,4608]{1,0:T(8,128)(2,1)S(1)}, u32[]{:S(2)}, u32[]{:S(2)}) collective-permute-start(bf16[16,4608]{1,0:T(8,128)(2,1)S(1)} %convolution_convert_fusion.1.refs_4_), channel_id=1, source_target_pairs={{0,1},{1,0},{2,3},{3,2},{4,5},{5,4},{6,7},{7,6},{8,9},{9,8},{10,11... | collective-permute-start | bytes 442376 | tf_op jit(solution)/shard_map/ppermute | solution.py:357
  17.2 16.1 %collective-permute-start.5 = (bf16[16,4608]{1,0:T(8,128)(2,1)S(1)}, bf16[16,4608]{1,0:T(8,128)(2,1)}, u32[]{:S(2)}, u32[]{:S(2)}) collective-permute-start(bf16[16,4608]{1,0:T(8,128)(2,1)S(1)} %convolution_convert_fusion.1.refs_4_), channel_id=1, source_target_pairs={{0,2},{1,3},{2,0},{3,1},{4,6},{5,7},{6,4},{7,5},{8,10},{9,11},{10,... | collective-permute-start | bytes 442376 | tf_op jit(solution)/shard_map/ppermute | solution.py:357
  20.0 10.5 %collective-permute-start.4 = (bf16[16,4608]{1,0:T(8,128)(2,1)S(1)}, bf16[16,4608]{1,0:T(8,128)(2,1)S(1)}, u32[]{:S(2)}, u32[]{:S(2)}) collective-permute-start(bf16[16,4608]{1,0:T(8,128)(2,1)S(1)} %convolution_convert_fusion.refs_5_), channel_id=1, source_target_pairs={{0,1},{1,0},{2,3},{3,2},{4,5},{5,4},{6,7},{7,6},{8,9},{9,8},{10,11... | collective-permute-start | bytes 442376 | tf_op jit(solution)/shard_map/ppermute | solution.py:357
  20.5 12.7 %collective-permute-start.6 = (bf16[16,4608]{1,0:T(8,128)(2,1)S(1)}, bf16[16,4608]{1,0:T(8,128)(2,1)}, u32[]{:S(2)}, u32[]{:S(2)}) collective-permute-start(bf16[16,4608]{1,0:T(8,128)(2,1)S(1)} %convolution_convert_fusion.refs_5_), channel_id=1, source_target_pairs={{0,2},{1,3},{2,0},{3,1},{4,6},{5,7},{6,4},{7,5},{8,10},{9,11},{10,... | collective-permute-start | bytes 442376 | tf_op jit(solution)/shard_map/ppermute | solution.py:357
  33.2 5.9 %collective-permute-start.7 = (bf16[16,4608]{1,0:T(8,128)(2,1)}, bf16[16,4608]{1,0:T(8,128)(2,1)}, u32[]{:S(2)}, u32[]{:S(2)}) collective-permute-start(bf16[16,4608]{1,0:T(8,128)(2,1)} %collective-permute-done.5.refs_8_), channel_id=1, source_target_pairs={{0,1},{1,0},{2,3},{3,2},{4,5},{5,4},{6,7},{7,6},{8,9},{9,8},{10,11... | collective-permute-start | bytes 442376 | tf_op jit(solution)/shard_map/ppermute | solution.py:357
  33.7 6.6 %collective-permute-start.8 = (bf16[16,4608]{1,0:T(8,128)(2,1)}, bf16[16,4608]{1,0:T(8,128)(2,1)}, u32[]{:S(2)}, u32[]{:S(2)}) collective-permute-start(bf16[16,4608]{1,0:T(8,128)(2,1)} %collective-permute-done.6.refs_9_), channel_id=1, source_target_pairs={{0,1},{1,0},{2,3},{3,2},{4,5},{5,4},{6,7},{7,6},{8,9},{9,8},{10,11... | collective-permute-start | bytes 442376 | tf_op jit(solution)/shard_map/ppermute | solution.py:357
  37.1 19.5 %collective-permute-start.11 = (bf16[208,2048]{1,0:T(8,128)(2,1)}, bf16[208,2048]{1,0:T(8,128)(2,1)}, u32[]{:S(2)}, u32[]{:S(2)}) collective-permute-start(bf16[208,2048]{1,0:T(8,128)(2,1)} %get-tuple-element.35), channel_id=1, source_target_pairs={{0,8},{4,12},{8,0},{12,4},{1,9},{5,13},{9,1},{13,5},{2,10},{6,14},... | collective-permute-start | bytes 2555912 | tf_op jit(solution)/shard_map/ppermute | solution.py:351
  37.6 19.6 %collective-permute-start.10 = (bf16[224,2048]{1,0:T(8,128)(2,1)}, bf16[224,2048]{1,0:T(8,128)(2,1)}, u32[]{:S(2)}, u32[]{:S(2)}) collective-permute-start(bf16[224,2048]{1,0:T(8,128)(2,1)} %collective-permute-done.9.refs_4_), channel_id=1, source_target_pairs={{0,16},{16,0},{1,17},{17,1},{2,18},{18,2},{3,19},{19,3},{4,20},{20... | collective-permute-start | bytes 2752520 | tf_op jit(solution)/shard_map/ppermute | solution.py:354
  57.2 22.0 %collective-permute-start.16 = (bf16[208,2048]{1,0:T(8,128)(2,1)}, bf16[208,2048]{1,0:T(8,128)(2,1)S(1)}, u32[]{:S(2)}, u32[]{:S(2)}) collective-permute-start(bf16[208,2048]{1,0:T(8,128)(2,1)} %get-tuple-element.37.refs_3_), channel_id=1, source_target_pairs={{0,8},{4,12},{8,0},{12,4},{1,9},{5,13},{9,1},{13,5},{2,10},{6,14},... | collective-permute-start | bytes 2555912 | tf_op jit(solution)/shard_map/ppermute | solution.py:351
  58.7 21.3 %collective-permute-start.17 = (bf16[208,2048]{1,0:T(8,128)(2,1)}, bf16[208,2048]{1,0:T(8,128)(2,1)S(1)}, u32[]{:S(2)}, u32[]{:S(2)}) collective-permute-start(bf16[208,2048]{1,0:T(8,128)(2,1)} %collective-permute-done.11.refs_4_), channel_id=1, source_target_pairs={{0,16},{16,0},{1,17},{17,1},{2,18},{18,2},{3,19},{19,3},{4,20},{20... | collective-permute-start | bytes 2555912 | tf_op jit(solution)/shard_map/ppermute | solution.py:354
  65.8 20.1 %collective-permute-start.13 = (bf16[2,448,512]{2,1,0:T(8,128)(2,1)S(1)}, bf16[2,448,512]{2,1,0:T(8,128)(2,1)S(1)}, u32[]{:S(2)}, u32[]{:S(2)}) collective-permute-start(bf16[2,448,512]{2,1,0:T(8,128)(2,1)S(1)} %project.4), channel_id=1, source_target_pairs={{1,0},{3,2},{4,5},{6,7},{9,8},{11,10},{12,13},{14,15},{17,16},{19,... | collective-permute-start | bytes 2752520 | tf_op jit(solution)/shard_map/ppermute | solution.py:428
  67.3 30.2 %collective-permute-start.19 = (bf16[208,2048]{1,0:T(8,128)(2,1)S(1)}, bf16[208,2048]{1,0:T(8,128)(2,1)S(1)}, u32[]{:S(2)}, u32[]{:S(2)}) collective-permute-start(bf16[208,2048]{1,0:T(8,128)(2,1)S(1)} %copy-done), channel_id=1, source_target_pairs={{0,8},{4,12},{8,0},{12,4},{1,9},{5,13},{9,1},{13,5},{2,10},{6,14},... | collective-permute-start | bytes 2555912 | tf_op jit(solution)/shard_map/ppermute | solution.py:351
  84.5 17.6 %collective-permute-start.18 = (bf16[2,416,512]{2,1,0:T(8,128)(2,1)S(1)}, bf16[2,416,512]{2,1,0:T(8,128)(2,1)S(1)}, u32[]{:S(2)}, u32[]{:S(2)}) collective-permute-start(bf16[2,416,512]{2,1,0:T(8,128)(2,1)S(1)} %project.5), channel_id=1, source_target_pairs={{1,0},{3,2},{4,5},{6,7},{9,8},{11,10},{12,13},{14,15},{17,16},{19,... | collective-permute-start | bytes 2555912 | tf_op jit(solution)/shard_map/ppermute | solution.py:428
  86.1 11.4 %collective-permute-start.14 = (bf16[224,512]{1,0:T(8,128)(2,1)S(1)}, bf16[224,512]{1,0:T(8,128)(2,1)S(1)}, u32[]{:S(2)}, u32[]{:S(2)}) collective-permute-start(bf16[224,512]{1,0:T(8,128)(2,1)S(1)} %get-tuple-element.53), channel_id=1, source_target_pairs={{0,2},{2,0},{5,7},{7,5},{8,10},{10,8},{13,15},{15,13},{16,18},{18,... | collective-permute-start | bytes 688136 | tf_op jit(solution)/shard_map/ppermute | solution.py:434
  93.8 14.9 %collective-permute-start.21 = (bf16[2,208,512]{2,1,0:T(8,128)(2,1)S(1)}, bf16[2,208,512]{2,1,0:T(8,128)(2,1)S(1)}, u32[]{:S(2)}, u32[]{:S(2)}) collective-permute-start(bf16[2,208,512]{2,1,0:T(8,128)(2,1)S(1)} %project.6), channel_id=1, source_target_pairs={{1,0},{3,2},{4,5},{6,7},{9,8},{11,10},{12,13},{14,15},{17,16},{19,... | collective-permute-start | bytes 1277960 | tf_op jit(solution)/shard_map/ppermute | solution.py:428
  95.1 19.7 %collective-permute-start.15 = (bf16[224,512]{1,0:T(8,128)(2,1)S(1)}, bf16[224,512]{1,0:T(8,128)(2,1)S(1)}, u32[]{:S(2)}, u32[]{:S(2)}) collective-permute-start(bf16[224,512]{1,0:T(8,128)(2,1)S(1)} %get-tuple-element.52), channel_id=1, source_target_pairs={{0,2},{2,0},{5,7},{7,5},{8,10},{10,8},{13,15},{15,13},{16,18},{18,... | collective-permute-start | bytes 688136 | tf_op jit(solution)/shard_map/ppermute | solution.py:434
  100.8 15.6 %collective-permute-start.23 = (bf16[2,208,512]{2,1,0:T(8,128)(2,1)S(1)}, bf16[2,208,512]{2,1,0:T(8,128)(2,1)S(1)}, u32[]{:S(2)}, u32[]{:S(2)}) collective-permute-start(bf16[2,208,512]{2,1,0:T(8,128)(2,1)S(1)} %project.7), channel_id=1, source_target_pairs={{1,0},{3,2},{4,5},{6,7},{9,8},{11,10},{12,13},{14,15},{17,16},{19,... | collective-permute-start | bytes 1277960 | tf_op jit(solution)/shard_map/ppermute | solution.py:428
  102.2 23.4 %collective-permute-start.20 = (bf16[416,512]{1,0:T(8,128)(2,1)S(1)}, bf16[416,512]{1,0:T(8,128)(2,1)S(1)}, u32[]{:S(2)}, u32[]{:S(2)}) collective-permute-start(bf16[416,512]{1,0:T(8,128)(2,1)S(1)} %fusion.2), channel_id=1, source_target_pairs={{0,2},{2,0},{5,7},{7,5},{8,10},{10,8},{13,15},{15,13},{16,18},{18,... | collective-permute-start | bytes 1277960 | tf_op jit(solution)/shard_map/ppermute | solution.py:434
  108.7 16.7 %collective-permute-start.22 = (bf16[208,512]{1,0:T(8,128)(2,1)S(1)}, bf16[208,512]{1,0:T(8,128)(2,1)S(1)}, u32[]{:S(2)}, u32[]{:S(2)}) collective-permute-start(bf16[208,512]{1,0:T(8,128)(2,1)S(1)} %fusion.7), channel_id=1, source_target_pairs={{0,2},{2,0},{5,7},{7,5},{8,10},{10,8},{13,15},{15,13},{16,18},{18,... | collective-permute-start | bytes 638984 | tf_op jit(solution)/shard_map/ppermute | solution.py:434
  116.4 11.4 %collective-permute-start.25 = (bf16[208,512]{1,0:T(8,128)(2,1)S(1)}, bf16[208,512]{1,0:T(8,128)(2,1)S(1)}, u32[]{:S(2)}, u32[]{:S(2)}) collective-permute-start(bf16[208,512]{1,0:T(8,128)(2,1)S(1)} %fusion.8), channel_id=1, source_target_pairs={{0,2},{2,0},{5,7},{7,5},{8,10},{10,8},{13,15},{15,13},{16,18},{18,... | collective-permute-start | bytes 638984 | tf_op jit(solution)/shard_map/ppermute | solution.py:434
  (13 other events, 73.0 us)
